TPU v7x, 32 devices: a whole 2x2x4 slice. The times are simulated.
32 devices in a mesh: stream: 16 (over z, y, core), dp: 2 (over x).
Axes of the slice: x: 2, y: 2, z: 4, core: 2. Of those that a mesh axis runs over, the one named last changes fastest.
Arguments:
- states: bfloat16 [27648, 768], P(('stream', 'dp')), may hold values from -6 to 6
- cotangent: bfloat16 [27648, 768], P(('stream', 'dp')), may hold values from -6 to 6
- word_lengths: int32 [384], replicated, may hold values from 5 to 20, as said below
- object_project: bfloat16 [768, 2304], P(None, ('stream', 'dp')), may hold values from -0.21875 to 0.21875
- object_output: bfloat16 [768, 768], P(None, ('stream', 'dp')), may hold values from -0.5 to 0.5
- object_up: bfloat16 [768, 3072], P(None, ('stream', 'dp')), may hold values from -0.21875 to 0.21875
- object_down: bfloat16 [3072, 768], P(('stream', 'dp')), may hold values from -0.109375 to 0.109375
- object_gains: bfloat16 [2, 768], P(None, ('stream', 'dp')), may hold values from 0.5 to 1.5
- cross_project: bfloat16 [768, 2304], P(None, ('stream', 'dp')), may hold values from -0.21875 to 0.21875
- cross_output: bfloat16 [768, 768], P(None, ('stream', 'dp')), may hold values from -0.5 to 0.5
- words_project: bfloat16 [768, 2304], P(None, ('stream', 'dp')), may hold values from -0.21875 to 0.21875
- words_output: bfloat16 [768, 768], P(None, ('stream', 'dp')), may hold values from -0.5 to 0.5
- region_project: bfloat16 [768, 2304], P(None, ('stream', 'dp')), may hold values from -0.21875 to 0.21875
- region_output: bfloat16 [768, 768], P(None, ('stream', 'dp')), may hold values from -0.5 to 0.5
- words_up: bfloat16 [768, 3072], P(None, ('stream', 'dp')), may hold values from -0.21875 to 0.21875
- words_down: bfloat16 [3072, 768], P(('stream', 'dp')), may hold values from -0.109375 to 0.109375
- region_up: bfloat16 [768, 3072], P(None, ('stream', 'dp')), may hold values from -0.21875 to 0.21875
- region_down: bfloat16 [3072, 768], P(('stream', 'dp')), may hold values from -0.109375 to 0.109375
- layer_gains: bfloat16 [5, 768], P(None, ('stream', 'dp')), may hold values from 0.5 to 1.5
Outputs:
- out_states: bfloat16 [27648, 768], P(('stream', 'dp'))
- grad_states: float32 [27648, 768], P(('stream', 'dp'))
- grad_object_project: float32 [768, 2304], P(None, ('stream', 'dp'))
- grad_object_output: float32 [768, 768], P(None, ('stream', 'dp'))
- grad_object_up: float32 [768, 3072], P(None, ('stream', 'dp'))
- grad_object_down: float32 [3072, 768], P(('stream', 'dp'))
- grad_object_gains: float32 [2, 768], P(None, ('stream', 'dp'))
- grad_cross_project: float32 [768, 2304], P(None, ('stream', 'dp'))
- grad_cross_output: float32 [768, 768], P(None, ('stream', 'dp'))
- grad_words_project: float32 [768, 2304], P(None, ('stream', 'dp'))
- grad_words_output: float32 [768, 768], P(None, ('stream', 'dp'))
- grad_region_project: float32 [768, 2304], P(None, ('stream', 'dp'))
- grad_region_output: float32 [768, 768], P(None, ('stream', 'dp'))
- grad_words_up: float32 [768, 3072], P(None, ('stream', 'dp'))
- grad_words_down: float32 [3072, 768], P(('stream', 'dp'))
- grad_region_up: float32 [768, 3072], P(None, ('stream', 'dp'))
- grad_region_down: float32 [3072, 768], P(('stream', 'dp'))
- grad_layer_gains: float32 [5, 768], P(None, ('stream', 'dp'))
Inputs may be any that keep to these rules, and one draw needn't show every extreme that they name: Words of item i; its language positions from word_lengths[i] to 35 are padding; some item has exactly 20 words and some exactly 5.
All inputs are finite; a program needn't handle non-finite values.
Results may differ from a plain program's by a relative error of at most 0.025.
Values may be sent and summed in bfloat16 or wider, within the bound.
No kernel may reach another device: no remote copies, remote signals or barrier semaphores. Data moves between devices by JAX's collectives and lax.ppermute only.
A program may use at most 320 MiB of HBM per device.

v0:
```python
import jax
import jax.numpy as jnp
from jax import lax
from jax.sharding import PartitionSpec as P

HEADS = 12
SLOT = 36


EPSILON = 1e-06
MASKED = -1000000000.0


def from_behind(shard, axis, by):
    size = lax.axis_size(axis)
    return lax.ppermute(shard, axis, [(i, (i + by) % size) for i in range(size)])


def layer_norm(total, gain):
    center = total - jnp.mean(total, axis=-1, keepdims=True)
    spread = jnp.mean(center * center, axis=-1, keepdims=True)
    return center * lax.rsqrt(spread + EPSILON) * gain


def gelu(value):
    return 0.5 * value * (1.0 + jax.scipy.special.erf(value * 0.7071067811865476))


def split_heads(rows):
    count = rows.shape[0] // SLOT
    return rows.reshape(count, SLOT, HEADS, rows.shape[1] // HEADS)


def scores_of(queries, keys, keep):
    scale = (queries.shape[1] // HEADS) ** (-0.5)
    scores = (
        jnp.einsum(
            "nahd,nbhd->nhab",
            split_heads(queries),
            split_heads(keys),
            preferred_element_type=jnp.float32,
        )
        * scale
    )
    return jnp.where(keep[:, None, None, :], scores, MASKED)


def attention_forward(queries, keys, values, keep):
    scores = scores_of(queries, keys, keep)
    top = jnp.max(scores, axis=-1, keepdims=True)
    raised = jnp.exp(scores - top)
    total = jnp.sum(raised, axis=-1, keepdims=True)
    weights = (raised / total).astype(jnp.bfloat16)
    context = jnp.einsum(
        "nhab,nbhd->nahd", weights, split_heads(values), preferred_element_type=jnp.float32
    )
    return (context.reshape(queries.shape).astype(jnp.bfloat16), top + jnp.log(total))


def attention_backward(queries, keys, values, keep, log_total, grad_context):
    scale = (queries.shape[1] // HEADS) ** (-0.5)
    probs = jnp.exp(scores_of(queries, keys, keep) - log_total)
    grad_heads = split_heads(grad_context)
    grad_probs = jnp.einsum(
        "nahd,nbhd->nhab", grad_heads, split_heads(values), preferred_element_type=jnp.float32
    )
    grad_scores = (
        probs * (grad_probs - jnp.sum(probs * grad_probs, axis=-1, keepdims=True))
    ).astype(jnp.bfloat16)
    grad_query = (
        jnp.einsum(
            "nhab,nbhd->nahd", grad_scores, split_heads(keys), preferred_element_type=jnp.float32
        )
        * scale
    )
    grad_keys = (
        jnp.einsum(
            "nhab,nahd->nbhd", grad_scores, split_heads(queries), preferred_element_type=jnp.float32
        )
        * scale
    )
    grad_values = jnp.einsum(
        "nhab,nahd->nbhd",
        probs.astype(jnp.bfloat16),
        grad_heads,
        preferred_element_type=jnp.float32,
    )
    shape = queries.shape
    return (grad_query.reshape(shape), grad_keys.reshape(shape), grad_values.reshape(shape))


def norm_backward(total, gain, grad_out):
    unused, pullback = jax.vjp(layer_norm, total, gain)
    return pullback(grad_out)


def output_backward(total, gain, context, output, grad_out):
    grad_total, grad_gain = norm_backward(total, gain, grad_out)
    grad_branch = grad_total.astype(jnp.bfloat16)
    grad_output = jnp.einsum("rd,re->de", context, grad_branch, preferred_element_type=jnp.float32)
    grad_context = jnp.einsum(
        "re,de->rd", grad_branch, output, preferred_element_type=jnp.float32
    ).astype(jnp.bfloat16)
    return (grad_total, grad_gain, grad_output, grad_context)


def attention_block(rows, project, output, gain, keep):
    width = rows.shape[1]
    joined = jnp.dot(rows, project, preferred_element_type=jnp.float32).astype(jnp.bfloat16)
    context, log_total = attention_forward(
        joined[:, :width], joined[:, width : 2 * width], joined[:, 2 * width :], keep
    )
    total = rows.astype(jnp.float32) + jnp.dot(context, output, preferred_element_type=jnp.float32)
    return (layer_norm(total, gain).astype(jnp.bfloat16), (joined, log_total, context, total))


def attention_block_backward(rows, project, output, gain, keep, saved, grad_out):
    joined, log_total, context, total = saved
    width = rows.shape[1]
    grad_total, grad_gain, grad_output, grad_context = output_backward(
        total, gain, context, output, grad_out
    )
    grad_query, grad_keys, grad_values = attention_backward(
        joined[:, :width],
        joined[:, width : 2 * width],
        joined[:, 2 * width :],
        keep,
        log_total,
        grad_context,
    )
    grad_joined = jnp.concatenate([grad_query, grad_keys, grad_values], axis=1).astype(jnp.bfloat16)
    grad_project = jnp.einsum("rd,re->de", rows, grad_joined, preferred_element_type=jnp.float32)
    grad_rows = grad_total + jnp.einsum(
        "re,de->rd", grad_joined, project, preferred_element_type=jnp.float32
    )
    return (grad_rows, grad_project, grad_output, grad_gain)


def feed_block(rows, upward, downward, gain):
    raised = jnp.dot(rows, upward, preferred_element_type=jnp.float32)
    hidden = gelu(raised).astype(jnp.bfloat16)
    total = rows.astype(jnp.float32) + jnp.dot(hidden, downward, preferred_element_type=jnp.float32)
    return (layer_norm(total, gain).astype(jnp.bfloat16), (raised, hidden, total))


def feed_block_backward(rows, upward, downward, gain, saved, grad_out):
    raised, hidden, total = saved
    grad_total, grad_gain = norm_backward(total, gain, grad_out)
    grad_branch = grad_total.astype(jnp.bfloat16)
    grad_down = jnp.einsum("rf,rd->fd", hidden, grad_branch, preferred_element_type=jnp.float32)
    grad_hidden = jnp.einsum("rd,fd->rf", grad_branch, downward, preferred_element_type=jnp.float32)
    unused, pullback = jax.vjp(gelu, raised)
    grad_raised = pullback(grad_hidden)[0].astype(jnp.bfloat16)
    grad_up = jnp.einsum("rd,rf->df", rows, grad_raised, preferred_element_type=jnp.float32)
    grad_rows = grad_total + jnp.einsum(
        "rf,df->rd", grad_raised, upward, preferred_element_type=jnp.float32
    )
    return (grad_rows, grad_up, grad_down, grad_gain)


def object_forward(rows, weights, keep_all):
    project, output, upward, downward, gains = weights
    gain_rows = gains.astype(jnp.float32)
    first, unused = attention_block(rows, project, output, gain_rows[0], keep_all)
    second, unused = feed_block(first, upward, downward, gain_rows[1])
    return second


def object_backward(rows, weights, keep_all, grad_out):
    project, output, upward, downward, gains = weights
    gain_rows = gains.astype(jnp.float32)
    first, first_saved = attention_block(rows, project, output, gain_rows[0], keep_all)
    second, second_saved = feed_block(first, upward, downward, gain_rows[1])
    grad_first, grad_up, grad_down, gain_second = feed_block_backward(
        first, upward, downward, gain_rows[1], second_saved, grad_out
    )
    grad_rows, grad_project, grad_output, gain_first = attention_block_backward(
        rows, project, output, gain_rows[0], keep_all, first_saved, grad_first
    )
    return (
        grad_rows,
        (grad_project, grad_output, grad_up, grad_down, jnp.stack([gain_first, gain_second])),
    )


def to_pieces(grad, dim, owners):
    if dim == 0:
        return grad.reshape(owners, -1)
    rows = grad.shape[0]
    return (
        grad.reshape(rows, owners, grad.shape[1] // owners).transpose(1, 0, 2).reshape(owners, -1)
    )


def from_flat(flat, listing, owners):
    result = []
    offset = 0
    for shape, dim in listing:
        length = shape[0] * shape[1] // owners
        piece = flat[offset : offset + length]
        offset = offset + length
        if dim == 0:
            result.append(piece.reshape(shape[0] // owners, shape[1]))
        else:
            result.append(piece.reshape(shape[0], shape[1] // owners))
    return result


def on_device(
    states,
    cotangent,
    word_lengths,
    object_project,
    object_output,
    object_up,
    object_down,
    object_gains,
    cross_project,
    cross_output,
    words_project,
    words_output,
    region_project,
    region_output,
    words_up,
    words_down,
    region_up,
    region_down,
    layer_gains,
):
    half = lax.axis_size("stream") // 2
    position = lax.axis_index("stream")
    is_words = position < half
    count = states.shape[0] // SLOT
    block = position % half * lax.axis_size("dp") + lax.axis_index("dp")
    lengths = lax.dynamic_slice_in_dim(word_lengths, block * count, count)
    keep_words = jnp.arange(SLOT)[None, :] < lengths[:, None]
    keep_all = jnp.ones((count, SLOT), jnp.bool_)
    self_keep = jnp.logical_or(keep_words, jnp.logical_not(is_words))
    cross_keep = jnp.logical_or(keep_words, is_words)
    object_weights = (
        lax.all_gather(object_project, ("stream", "dp"), axis=1, tiled=True),
        lax.all_gather(object_output, ("stream", "dp"), axis=1, tiled=True),
        lax.all_gather(object_up, ("stream", "dp"), axis=1, tiled=True),
        lax.all_gather(object_down, ("stream", "dp"), axis=0, tiled=True),
        lax.all_gather(object_gains, ("stream", "dp"), axis=1, tiled=True),
    )
    (
        cross_in,
        cross_out,
        words_in,
        words_out,
        region_in,
        region_out,
        words_upward,
        words_downward,
        region_upward,
        region_downward,
        gain_table,
    ) = (
        lax.all_gather(cross_project, ("stream", "dp"), axis=1, tiled=True),
        lax.all_gather(cross_output, ("stream", "dp"), axis=1, tiled=True),
        lax.all_gather(words_project, ("stream", "dp"), axis=1, tiled=True),
        lax.all_gather(words_output, ("stream", "dp"), axis=1, tiled=True),
        lax.all_gather(region_project, ("stream", "dp"), axis=1, tiled=True),
        lax.all_gather(region_output, ("stream", "dp"), axis=1, tiled=True),
        lax.all_gather(words_up, ("stream", "dp"), axis=1, tiled=True),
        lax.all_gather(words_down, ("stream", "dp"), axis=0, tiled=True),
        lax.all_gather(region_up, ("stream", "dp"), axis=1, tiled=True),
        lax.all_gather(region_down, ("stream", "dp"), axis=0, tiled=True),
        lax.all_gather(layer_gains, ("stream", "dp"), axis=1, tiled=True),
    )
    gains = gain_table.astype(jnp.float32)
    self_in = jnp.where(is_words, words_in, region_in)
    self_out = jnp.where(is_words, words_out, region_out)
    feed_up = jnp.where(is_words, words_upward, region_upward)
    feed_down = jnp.where(is_words, words_downward, region_downward)
    self_gain = jnp.where(is_words, gains[1], gains[2])
    feed_gain = jnp.where(is_words, gains[3], gains[4])
    entry = lax.cond(
        is_words,
        lambda rows: rows,
        lambda rows: object_forward(rows, object_weights, keep_all),
        states,
    )
    width = entry.shape[1]
    joined = jnp.dot(entry, cross_in, preferred_element_type=jnp.float32).astype(jnp.bfloat16)
    partner = from_behind(joined[:, width:], "stream", half)
    cross_context, cross_log = attention_forward(
        joined[:, :width], partner[:, :width], partner[:, width:], cross_keep
    )
    cross_total = entry.astype(jnp.float32) + jnp.dot(
        cross_context, cross_out, preferred_element_type=jnp.float32
    )
    third = layer_norm(cross_total, gains[0]).astype(jnp.bfloat16)
    fourth, fourth_saved = attention_block(third, self_in, self_out, self_gain, self_keep)
    fifth, fifth_saved = feed_block(fourth, feed_up, feed_down, feed_gain)
    grad_fifth = cotangent.astype(jnp.float32)
    grad_fourth, grad_feed_up, grad_feed_down, grad_feed_gain = feed_block_backward(
        fourth, feed_up, feed_down, feed_gain, fifth_saved, grad_fifth
    )
    grad_third, grad_self_in, grad_self_out, grad_self_gain = attention_block_backward(
        third, self_in, self_out, self_gain, self_keep, fourth_saved, grad_fourth
    )
    grad_cross_total, grad_cross_gain, grad_cross_out, grad_cross_context = output_backward(
        cross_total, gains[0], cross_context, cross_out, grad_third
    )
    grad_query, grad_keys, grad_values = attention_backward(
        joined[:, :width],
        partner[:, :width],
        partner[:, width:],
        cross_keep,
        cross_log,
        grad_cross_context,
    )
    returned = from_behind(
        jnp.concatenate([grad_keys, grad_values], axis=1).astype(jnp.bfloat16), "stream", half
    )
    grad_joined = jnp.concatenate([grad_query.astype(jnp.bfloat16), returned], axis=1)
    grad_cross_in = jnp.einsum("rd,re->de", entry, grad_joined, preferred_element_type=jnp.float32)
    grad_entry = grad_cross_total + jnp.einsum(
        "re,de->rd", grad_joined, cross_in, preferred_element_type=jnp.float32
    )
    words_side = is_words.astype(jnp.float32)
    region_side = 1.0 - words_side
    sum_gains = jnp.stack(
        [
            grad_cross_gain,
            words_side * grad_self_gain,
            region_side * grad_self_gain,
            words_side * grad_feed_gain,
            region_side * grad_feed_gain,
        ]
    )

    def skip_back(grad_rows):
        return (
            grad_rows,
            tuple((jnp.zeros(weight.shape, jnp.float32) for weight in object_weights)),
        )

    def object_back(grad_rows):
        return object_backward(states, object_weights, keep_all, grad_rows)

    grad_states, first_grads = lax.cond(is_words, skip_back, object_back, grad_entry)
    object_in, object_out, object_upward, object_downward, object_gain = first_grads
    owners = lax.axis_size("stream") * lax.axis_size("dp")
    cross_list = ((grad_cross_in, 1), (grad_cross_out, 1), (sum_gains, 1))
    self_list = ((grad_self_in, 1), (grad_self_out, 1), (grad_feed_up, 1), (grad_feed_down, 0))
    object_list = (
        (object_in, 1),
        (object_out, 1),
        (object_upward, 1),
        (object_downward, 0),
        (object_gain, 1),
    )
    every = cross_list + self_list + object_list
    outgoing = jnp.concatenate([to_pieces(grad, dim, owners) for grad, dim in every], axis=1)
    incoming = lax.all_to_all(
        outgoing.astype(jnp.bfloat16), ("stream", "dp"), split_axis=0, concat_axis=0, tiled=True
    ).astype(outgoing.dtype)
    cross_width = sum((grad.size for grad, dim in cross_list)) // owners
    self_width = sum((grad.size for grad, dim in self_list)) // owners
    parted = owners // 2
    cross_flat = jnp.sum(incoming[:, :cross_width], axis=0)
    words_flat = jnp.sum(incoming[:parted, cross_width : cross_width + self_width], axis=0)
    region_flat = jnp.sum(incoming[parted:, cross_width : cross_width + self_width], axis=0)
    object_flat = jnp.sum(incoming[parted:, cross_width + self_width :], axis=0)
    cross_parts = from_flat(
        cross_flat, tuple(((grad.shape, dim) for grad, dim in cross_list)), owners
    )
    words_parts = from_flat(
        words_flat, tuple(((grad.shape, dim) for grad, dim in self_list)), owners
    )
    region_parts = from_flat(
        region_flat, tuple(((grad.shape, dim) for grad, dim in self_list)), owners
    )
    first_summed = from_flat(
        object_flat, tuple(((grad.shape, dim) for grad, dim in object_list)), owners
    )
    second_summed = (
        cross_parts[0],
        cross_parts[1],
        words_parts[0],
        words_parts[1],
        region_parts[0],
        region_parts[1],
        words_parts[2],
        words_parts[3],
        region_parts[2],
        region_parts[3],
        cross_parts[2],
    )
    return (fifth, grad_states) + tuple(first_summed) + tuple(second_summed)


def solution(mesh):
    in_specs = (
        P(("stream", "dp"), None),
        P(("stream", "dp"), None),
        P(),
        P(None, ("stream", "dp")),
        P(None, ("stream", "dp")),
        P(None, ("stream", "dp")),
        P(("stream", "dp"), None),
        P(None, ("stream", "dp")),
        P(None, ("stream", "dp")),
        P(None, ("stream", "dp")),
        P(None, ("stream", "dp")),
        P(None, ("stream", "dp")),
        P(None, ("stream", "dp")),
        P(None, ("stream", "dp")),
        P(None, ("stream", "dp")),
        P(("stream", "dp"), None),
        P(None, ("stream", "dp")),
        P(("stream", "dp"), None),
        P(None, ("stream", "dp")),
    )
    out_specs = (
        P(("stream", "dp"), None),
        P(("stream", "dp"), None),
        P(None, ("stream", "dp")),
        P(None, ("stream", "dp")),
        P(None, ("stream", "dp")),
        P(("stream", "dp"), None),
        P(None, ("stream", "dp")),
        P(None, ("stream", "dp")),
        P(None, ("stream", "dp")),
        P(None, ("stream", "dp")),
        P(None, ("stream", "dp")),
        P(None, ("stream", "dp")),
        P(None, ("stream", "dp")),
        P(None, ("stream", "dp")),
        P(("stream", "dp"), None),
        P(None, ("stream", "dp")),
        P(("stream", "dp"), None),
        P(None, ("stream", "dp")),
    )
    return jax.shard_map(
        on_device, mesh=mesh, in_specs=in_specs, out_specs=out_specs, check_vma=False
    )
```

profile of v0, /device:TPU:0, one launch (start us, length us, event | category | flops | bytes accessed | tf_op | source)
XLA Modules:
  0.0 2743.2 jit_solution(14819369914224030553)
XLA Ops:
  16.1 69.5 %all-gather = bf16[32,24,2]{1,2,0:T(2,128)(2,1)S(1)} all-gather(bf16[1,24,2]{1,2,0:T(2,128)(2,1)} %bitcast.145), channel_id=1, replica_groups=mesh['stream'=16,'dp'=2] {'stream','dp'}, dimensions={0}, use_global_device_ids=true | all-gather | bytes 3168 | tf_op jit(solution)/shard_map/all_gather | solution.py:245
  86.2 43.6 %all-gather.17.cloned.1.call-done = bf16[768,2304]{0,1:T(8,128)(2,1)} async-done(((bf16[768,72]{0,1:T(8,128)(2,1)}), bf16[768,2304]{0,1:T(8,128)(2,1)}) %all-gather.17.cloned.1.call-update) | async-done | bytes 3538960 | tf_op jit(solution)/shard_map/all_gather | solution.py:241
  129.9 65.4 %all-gather.21.cloned.1.call-done = bf16[768,3072]{0,1:T(8,128)(2,1)} async-done(((bf16[768,96]{0,1:T(8,128)(2,1)}), bf16[768,3072]{0,1:T(8,128)(2,1)}) %all-gather.21.cloned.1.call-update) | async-done | bytes 4718608 | tf_op jit(solution)/shard_map/all_gather | solution.py:243
  195.3 65.3 %all-gather.23.cloned.1.call-done = bf16[3072,768]{1,0:T(8,128)(2,1)} async-done(((bf16[96,768]{1,0:T(8,128)(2,1)}), bf16[3072,768]{1,0:T(8,128)(2,1)}) %all-gather.23.cloned.1.call-update) | async-done | bytes 4718608 | tf_op jit(solution)/shard_map/all_gather | solution.py:244
  266.4 55.9 %all-gather.25.cloned.1.call-done = bf16[768,2304]{0,1:T(8,128)(2,1)} async-done(((bf16[768,72]{0,1:T(8,128)(2,1)}), bf16[768,2304]{0,1:T(8,128)(2,1)}) %all-gather.25.cloned.1.call-update) | async-done | bytes 3538960 | tf_op jit(solution)/shard_map/all_gather | solution.py:260
  336.7 138.9 %all-gather.1 = bf16[32,24,5]{1,2,0:T(8,128)(2,1)S(1)} all-gather(bf16[1,24,5]{1,2,0:T(8,128)(2,1)S(1)} %bitcast.144), channel_id=1, replica_groups=mesh['stream'=16,'dp'=2] {'stream','dp'}, dimensions={0}, use_global_device_ids=true | all-gather | bytes 7920 | tf_op jit(solution)/shard_map/all_gather | solution.py:270
  520.8 14.3 all-gather.29.cloned.1.call-done
  535.1 61.9 %all-gather.31.cloned.1.call-done = bf16[768,2304]{0,1:T(8,128)(2,1)} async-done(((bf16[768,72]{0,1:T(8,128)(2,1)}), bf16[768,2304]{0,1:T(8,128)(2,1)}) %all-gather.31.cloned.1.call-update) | async-done | bytes 3538960 | tf_op jit(solution)/shard_map/all_gather | solution.py:264
  637.3 15.6 all-gather.33.cloned.1.call-done
  652.9 55.9 %all-gather.35.cloned.1.call-done = bf16[768,768]{0,1:T(8,128)(2,1)} async-done(((bf16[768,24]{0,1:T(8,128)(2,1)}), bf16[768,768]{0,1:T(8,128)(2,1)}) %all-gather.35.cloned.1.call-update) | async-done | bytes 1179664 | tf_op jit(solution)/shard_map/all_gather | solution.py:265
  714.0 60.3 %all-gather.37.cloned.1.call-done = bf16[768,3072]{0,1:T(8,128)(2,1)} async-done(((bf16[768,96]{0,1:T(8,128)(2,1)}), bf16[768,3072]{0,1:T(8,128)(2,1)}) %all-gather.37.cloned.1.call-update) | async-done | bytes 4718608 | tf_op jit(solution)/shard_map/all_gather | solution.py:266
  774.3 65.3 %all-gather.39.cloned.1.call-done = bf16[768,3072]{0,1:T(8,128)(2,1)} async-done(((bf16[768,96]{0,1:T(8,128)(2,1)}), bf16[768,3072]{0,1:T(8,128)(2,1)}) %all-gather.39.cloned.1.call-update) | async-done | bytes 4718608 | tf_op jit(solution)/shard_map/all_gather | solution.py:268
  849.6 55.3 %all-gather.41.cloned.1.call-done = bf16[3072,768]{1,0:T(8,128)(2,1)} async-done(((bf16[96,768]{1,0:T(8,128)(2,1)}), bf16[3072,768]{1,0:T(8,128)(2,1)}) %all-gather.41.cloned.1.call-update) | async-done | bytes 4718608 | tf_op jit(solution)/shard_map/all_gather | solution.py:267
  905.0 65.3 %all-gather.43.cloned.1.call-done = bf16[3072,768]{1,0:T(8,128)(2,1)} async-done(((bf16[96,768]{1,0:T(8,128)(2,1)}), bf16[3072,768]{1,0:T(8,128)(2,1)}) %all-gather.43.cloned.1.call-update) | async-done | bytes 4718608 | tf_op jit(solution)/shard_map/all_gather | solution.py:269
  1198.2 14.0 concatenate.60
  1220.9 13.0 concatenate.58
  1255.7 34.0 %collective-permute-done.1 = bf16[864,1536]{1,0:T(8,128)(2,1)} collective-permute-done((bf16[864,1536]{1,0:T(8,128)(2,1)}, bf16[864,1536]{1,0:T(8,128)(2,1)}, u32[]{:S(2)}, u32[]{:S(2)}) %collective-permute-start.1) | collective-permute-done | bytes 2654240 | tf_op jit(solution)/shard_map/ppermute | solution.py:16
  1315.0 17.6 conditional.3
  1342.6 13.8 concatenate.64
  1406.7 13.3 concatenate.65
  1424.4 19.8 dynamic-update-slice.6
  1452.9 27.5 %dynamic-update-slice.8 = bf16[32,1,516264]{2,0,1:T(8,128)(2,1)} dynamic-update-slice(bf16[32,1,516264]{2,0,1:T(8,128)(2,1)} %dynamic-update-slice.7, bf16[32,1,73728]{2,0,1:T(8,128)(2,1)} %concatenate.62, s32[]{} %constant.145, s32[]{} %constant.145, s32[]{} %constant.150) | dynamic-update-slice | bytes 9437188
  1480.4 27.7 %dynamic-update-slice.9 = bf16[32,1,516264]{2,0,1:T(8,128)(2,1)} dynamic-update-slice(bf16[32,1,516264]{2,0,1:T(8,128)(2,1)} %dynamic-update-slice.8, bf16[32,1,73728]{2,0,1:T(8,128)(2,1)} %concatenate.63, s32[]{} %constant.145, s32[]{} %constant.145, s32[]{} %constant.151) | dynamic-update-slice | bytes 9437188
  1508.1 18.6 dynamic-update-slice.10
  1535.7 27.5 %dynamic-update-slice.12 = bf16[32,1,516264]{2,0,1:T(8,128)(2,1)} dynamic-update-slice(bf16[32,1,516264]{2,0,1:T(8,128)(2,1)} %dynamic-update-slice.11, bf16[32,1,73728]{2,0,1:T(8,128)(2,1)} %concatenate.66, s32[]{} %constant.145, s32[]{} %constant.145, s32[]{} %constant.154) | dynamic-update-slice | bytes 9437188
  1563.2 27.2 dynamic-update-slice.13
  1592.4 29.2 %reduce.14 = bf16[32,516264]{1,0:T(8,128)(2,1)} reduce(bf16[32,1,516264]{2,0,1:T(8,128)(2,1)} %dynamic-update-slice.14, bf16[]{:T(256)} %broadcast.528), dimensions={1}, to_apply=%copy.332.reduce_sub_computation | reduce | bytes 66081792 | tf_op jit(solution)/shard_map/concatenate | solution.py:357
  1621.6 47.0 %reshape.837 = bf16[32,2,258132]{2,1,0:T(2,128)(2,1)} reshape(bf16[32,516264]{1,0:T(8,128)(2,1)} %reduce.14) | data formatting | bytes 66081792
  1668.6 862.3 %all_to_all.6 = bf16[32,2,258132]{2,1,0:T(2,128)(2,1)} all-to-all(bf16[32,2,258132]{2,1,0:T(2,128)(2,1)} %reshape.837), channel_id=1, replica_groups=mesh['stream'=16,'dp'=2] {'stream','dp'}, dimensions={0} | all-to-all | bytes 66081792 | tf_op jit(solution)/shard_map/all_to_all | solution.py:358
  2530.9 107.4 %reshape.838 = bf16[32,1,516264]{2,1,0:T(2,128)(2,1)} reshape(bf16[32,2,258132]{2,1,0:T(2,128)(2,1)} %all_to_all.6) | data formatting | bytes 66081792
  2638.4 43.9 %copy.455 = f32[32,1,516264]{2,0,1:T(8,128)} copy(bf16[32,1,516264]{2,1,0:T(2,128)(2,1)} %reshape.838) | data formatting | bytes 99122688
  2698.2 22.0 slice_reduce_fusion.5
  (390 shorter events, 540.7 us)
Async XLA Ops:
  7.2 253.3 %copy-start.27 = (bf16[864,768]{1,0:T(8,128)(2,1)S(1)}, bf16[864,768]{1,0:T(8,128)(2,1)}, u32[]{:S(2)}) copy-start(bf16[864,768]{1,0:T(8,128)(2,1)} %param.23) | copy-start | bytes 3981316
  7.2 79.0 %all-gather.19.cloned.1.call-start = ((), (), s32[]{:S(2)}) async-start(), calls=%async_computation.2 | async-start | bytes 1216512 | tf_op jit(solution)/shard_map/all_gather | solution.py:242
  7.9 121.9 %all-gather.17.cloned.1.call-start = ((), (), s32[]{:S(2)}) async-start(), calls=%async_computation.1 | async-start | bytes 3649536 | tf_op jit(solution)/shard_map/all_gather | solution.py:241
  8.7 186.6 %all-gather.21.cloned.1.call-start = ((), (), s32[]{:S(2)}) async-start(), calls=%async_computation.3 | async-start | bytes 4866048 | tf_op jit(solution)/shard_map/all_gather | solution.py:243
  9.4 251.1 %all-gather.23.cloned.1.call-start = ((), (), s32[]{:S(2)}) async-start(), calls=%async_computation.4 | async-start | bytes 4866048 | tf_op jit(solution)/shard_map/all_gather | solution.py:244
  10.0 312.3 %all-gather.25.cloned.1.call-start = ((), (), s32[]{:S(2)}) async-start(), calls=%async_computation.5 | async-start | bytes 3649536 | tf_op jit(solution)/shard_map/all_gather | solution.py:260
  10.6 505.4 %all-gather.27.cloned.1.call-start = ((), (), s32[]{:S(2)}) async-start(), calls=%async_computation.6 | async-start | bytes 1216512 | tf_op jit(solution)/shard_map/all_gather | solution.py:261
  11.2 523.9 %all-gather.29.cloned.1.call-start = ((), (), s32[]{:S(2)}) async-start(), calls=%async_computation.7 | async-start | bytes 3649536 | tf_op jit(solution)/shard_map/all_gather | solution.py:262
  11.9 585.1 %all-gather.31.cloned.1.call-start = ((), (), s32[]{:S(2)}) async-start(), calls=%async_computation.8 | async-start | bytes 3649536 | tf_op jit(solution)/shard_map/all_gather | solution.py:264
  12.7 640.2 %all-gather.33.cloned.1.call-start = ((), (), s32[]{:S(2)}) async-start(), calls=%async_computation.9 | async-start | bytes 1216512 | tf_op jit(solution)/shard_map/all_gather | solution.py:263
  13.4 695.4 %all-gather.35.cloned.1.call-start = ((), (), s32[]{:S(2)}) async-start(), calls=%async_computation.10 | async-start | bytes 1216512 | tf_op jit(solution)/shard_map/all_gather | solution.py:265
  14.0 760.3 %all-gather.37.cloned.1.call-start = ((), (), s32[]{:S(2)}) async-start(), calls=%async_computation.11 | async-start | bytes 4866048 | tf_op jit(solution)/shard_map/all_gather | solution.py:266
  14.7 824.8 %all-gather.39.cloned.1.call-start = ((), (), s32[]{:S(2)}) async-start(), calls=%async_computation.12 | async-start | bytes 4866048 | tf_op jit(solution)/shard_map/all_gather | solution.py:268
  15.3 889.7 %all-gather.41.cloned.1.call-start = ((), (), s32[]{:S(2)}) async-start(), calls=%async_computation.13 | async-start | bytes 4866048 | tf_op jit(solution)/shard_map/all_gather | solution.py:267
  16.0 954.2 %all-gather.43.cloned.1.call-start = ((), (), s32[]{:S(2)}) async-start(), calls=%async_computation.14 | async-start | bytes 4866048 | tf_op jit(solution)/shard_map/all_gather | solution.py:269
  331.6 145.8 %slice-start.6 = ((bf16[864,2304]{1,0:T(8,128)(2,1)}), bf16[864,768]{1,0:T(8,128)(2,1)S(1)}, s32[]{:S(2)}) async-start(bf16[864,2304]{1,0:T(8,128)(2,1)} %copy-done.37), calls=%async_computation.21 | async-start | bytes 2654208 | tf_op jit(solution)/shard_map/slice | solution.py:289
  331.6 149.3 %collective-permute-start = (bf16[864,1536]{1,0:T(8,128)(2,1)}, bf16[864,1536]{1,0:T(8,128)(2,1)}, u32[]{:S(2)}, u32[]{:S(2)}) collective-permute-start(bf16[864,1536]{1,0:T(8,128)(2,1)} %slice.299), channel_id=1, source_target_pairs={{0,16},{2,18},{4,20},{6,22},{8,24},{10,26},{12,28},{14,30},{16,0},... | collective-permute-start | bytes 7962632 | tf_op jit(solution)/shard_map/ppermute | solution.py:16
  520.3 82.7 %copy-start.9 = (f32[864,768]{1,0:T(8,128)}, f32[864,768]{1,0:T(8,128)S(1)}, u32[]{:S(2)}) copy-start(f32[864,768]{1,0:T(8,128)S(1)} %get-tuple-element.235) | copy-start | bytes 7962628
  520.7 82.3 %copy-start.64 = (f32[864]{0:T(1024)}, f32[864]{0:T(1024)S(1)}, u32[]{:S(2)}) copy-start(f32[864]{0:T(1024)S(1)} %multiply_reduce_fusion.19) | copy-start | bytes 10372
  520.8 82.3 %copy-start.69 = (f32[864]{0:T(1024)}, f32[864]{0:T(1024)S(1)}, u32[]{:S(2)}) copy-start(f32[864]{0:T(1024)S(1)} %fusion.110) | copy-start | bytes 10372
  609.2 18.0 copy-start.15
  637.3 76.0 %copy-start.56 = (f32[24,12,36]{2,1,0:T(8,128)S(1)}, f32[24,12,36]{2,1,0:T(8,128)}, u32[]{:S(2)}) copy-start(f32[24,12,36]{2,1,0:T(8,128)} %get-tuple-element.232) | copy-start | bytes 124420
  637.3 76.0 %copy-start.58 = (f32[24,12,36]{2,1,0:T(8,128)S(1)}, f32[24,12,36]{2,1,0:T(8,128)}, u32[]{:S(2)}) copy-start(f32[24,12,36]{2,1,0:T(8,128)} %copy-done.57) | copy-start | bytes 124420
  984.6 28.7 %slice-start.16 = ((s8[4718592]{0:T(1024)(128)(4,1)}), s8[4194304]{0:T(1024)(128)(4,1)S(1)}, s32[]{:S(2)}) async-start(s8[4718592]{0:T(1024)(128)(4,1)} %bitcast.150), calls=%async_computation.31 | async-start | bytes 8388608
  984.6 28.7 %slice-start.18 = ((s8[4718592]{0:T(1024)(128)(4,1)}), s8[4194304]{0:T(1024)(128)(4,1)S(1)}, s32[]{:S(2)}) async-start(s8[4718592]{0:T(1024)(128)(4,1)} %bitcast.152), calls=%async_computation.33 | async-start | bytes 8388608
  991.8 21.5 slice-start.17
  991.8 21.5 slice-start.19
  1082.9 15.6 slice-start.2
  1171.4 118.4 %collective-permute-start.1 = (bf16[864,1536]{1,0:T(8,128)(2,1)}, bf16[864,1536]{1,0:T(8,128)(2,1)}, u32[]{:S(2)}, u32[]{:S(2)}) collective-permute-start(bf16[864,1536]{1,0:T(8,128)(2,1)} %pad_maximum_fusion.1), channel_id=1, source_target_pairs={{0,16},{2,18},{4,20},{6,22},{8,24},{10,26},{12,28},{14,30},{16,0},... | collective-permute-start | bytes 7962632 | tf_op jit(solution)/shard_map/ppermute | solution.py:16
  1424.4 19.8 copy-start.38
  1480.4 27.7 %copy-start.13 = (bf16[32,1,55296]{2,0,1:T(8,128)(2,1)S(1)}, bf16[32,1,55296]{2,0,1:T(8,128)(2,1)}, u32[]{:S(2)}) copy-start(bf16[32,1,55296]{2,0,1:T(8,128)(2,1)} %concatenate.64) | copy-start | bytes 10616836
  2698.2 22.3 copy-start.40
  (66 other events, 389.4 us)
Sparse Core Ops, SparseCore 0:
  11.0 56.7 all-gather.18
  70.7 59.1 all-gather.16
  132.8 62.4 all-gather.20
  198.0 62.4 all-gather.22
  263.3 58.9 all-gather.24
  325.1 147.9 all-gather.26
  476.0 59.0 all-gather.28
  538.0 58.9 all-gather.30
  599.9 52.9 all-gather.32
  655.7 53.0 all-gather.34
  711.7 62.5 all-gather.36
  777.1 62.4 all-gather.38
  842.5 62.4 all-gather.40
  907.7 62.4 all-gather.42
where the time goes:
time: 2760 us; the launch traced here: 2740 us
  blocking collectives  1070 us (39%)
  local copies, waits for them, and re-layouts  705 us (26%)
  waiting for transfers between devices  666 us (24%)
  matrix products  164 us (6%)
  other arithmetic  101 us (4%)
    all_to_all x1, blocking collectives, on_device(): lax.all_to_all(outgoing.astype(jnp.bfloat16), ('stream', 'dp'), split_axi...  862 us
    unnamed x185, local copies, waits for them, and re-layouts  391 us
    all_gather x1, blocking collectives, on_device(): lax.all_gather(layer_gains, ('stream', 'dp'), axis=1, tiled=True)  139 us
    concatenate x14, local copies, waits for them, and re-layouts, on_device(): jnp.concatenate([to_pieces(grad, dim, owners) for grad, dim in every], ax...  114 us
    all_gather x1, blocking collectives, on_device(): lax.all_gather(object_gains, ('stream', 'dp'), axis=1, tiled=True)  69.5 us
    all_gather x1, waiting for transfers between devices, on_device(): lax.all_gather(object_up, ('stream', 'dp'), axis=1, tiled=True)  65.4 us
    all_gather x1, waiting for transfers between devices, on_device(): lax.all_gather(region_up, ('stream', 'dp'), axis=1, tiled=True)  65.3 us
    all_gather x1, waiting for transfers between devices, on_device(): lax.all_gather(object_down, ('stream', 'dp'), axis=0, tiled=True)  65.3 us
  transfers between devices with their start and end apart: 16, of which 13 were waited for; matrix products, arithmetic and copies ran while one was open for 7% of the time, Pallas kernels for 0%

commit v1 on v0

v1 whole, which is shorter than its diff:
```python
import functools

import jax
import jax.numpy as jnp
from jax import lax
from jax.experimental import pallas as pl
from jax.experimental.pallas import tpu as pltpu
from jax.sharding import PartitionSpec as P

HEADS = 12
SLOT = 36
PACK = 4
EPSILON = 1e-06
MASKED = -1000000000.0
APART = -1e30
BF = jnp.bfloat16
F32 = jnp.float32
VMEM_LIMIT = 48 * 1024 * 1024

NN = (((1,), (0,)), ((), ()))
NT = (((1,), (1,)), ((), ()))
TN = (((0,), (0,)), ((), ()))


def mm(left, right, dims):
    return lax.dot_general(left, right, dims, preferred_element_type=F32)


def norm_forward(total):
    center = total - jnp.mean(total, axis=-1, keepdims=True)
    spread = jnp.mean(center * center, axis=-1, keepdims=True)
    rate = lax.rsqrt(spread + EPSILON)
    return center * rate, rate


def norm_backward(grad, normed, rate, gain):
    slope = grad * gain
    first = jnp.mean(slope, axis=-1, keepdims=True)
    second = jnp.mean(slope * normed, axis=-1, keepdims=True)
    terms = grad * normed
    rows, width = terms.shape
    return rate * (slope - first - normed * second), jnp.sum(
        terms.reshape(rows // 8, 8, width), axis=0
    )


def gelu_pair(value):
    size = jnp.abs(value) * 0.7071067811865476
    t = 1.0 / (1.0 + 0.3275911 * size)
    bell = jnp.exp(-size * size)
    poly = t * (
        0.254829592
        + t * (-0.284496736 + t * (1.421413741 + t * (-1.453152027 + t * 1.061405429)))
    )
    tail = 0.5 * poly * bell
    phi = jnp.where(value >= 0.0, 1.0 - tail, tail)
    return value * phi, phi + value * bell * 0.3989422804014327


def head_masks(width, head):
    lane = lax.broadcasted_iota(jnp.int32, (1, width), 1)
    return [jnp.where(lane // head == i, 1.0, 0.0).astype(F32) for i in range(width // head)]


def spread_heads(block, masks):
    return jnp.concatenate([block * mask.astype(block.dtype) for mask in masks], axis=0)


def fold_heads(stacked, masks):
    rows = stacked.shape[0] // len(masks)
    total = stacked[:rows] * masks[0]
    for i in range(1, len(masks)):
        total = total + stacked[i * rows : (i + 1) * rows] * masks[i]
    return total


def attend_kernel(cross, x_ref, y_ref, p_ref, o_ref, g_ref, kb_ref, apart_ref,
                  out_ref, joined_ref, probs_ref, context_ref, normed_ref, rate_ref):
    x = x_ref[...]
    width = x.shape[1]
    head = width // HEADS
    quad = 4 * head
    scale = head ** (-0.5)
    if cross:
        joined_ref[:, :width] = mm(x, p_ref[:width], NT).astype(BF)
        joined_ref[:, width:] = mm(y_ref[...], p_ref[width:], NT).astype(BF)
    else:
        joined_ref[...] = mm(x, p_ref[...], NT).astype(BF)
    masks = head_masks(quad, head)
    bias = apart_ref[...] + kb_ref[...]
    for i in range(width // quad):
        q = joined_ref[:, i * quad : (i + 1) * quad]
        k = joined_ref[:, width + i * quad : width + (i + 1) * quad]
        v = joined_ref[:, 2 * width + i * quad : 2 * width + (i + 1) * quad]
        scores = mm(k, spread_heads(q, masks), NT) * scale + bias
        raised = jnp.exp(scores - jnp.max(scores, axis=0, keepdims=True))
        probs = (raised * (1.0 / jnp.sum(raised, axis=0, keepdims=True))).astype(BF)
        probs_ref[0, i] = probs
        context_ref[:, i * quad : (i + 1) * quad] = fold_heads(mm(probs, v, TN), masks).astype(BF)
    total = x.astype(F32) + mm(context_ref[...], o_ref[...], NT)
    normed, rate = norm_forward(total)
    out_ref[...] = (normed * g_ref[...]).astype(BF)
    normed_ref[...] = normed.astype(BF)
    rate_ref[...] = rate


def whole(shape):
    return pl.BlockSpec(shape, lambda *_: (0,) * len(shape))


def attention_block(x, y, project, output, gain, key_bias, apart, cross):
    rows, width = x.shape
    block = PACK * SLOT
    groups = rows // block
    quads = HEADS // 4
    row = lambda w: pl.BlockSpec((block, w), lambda i: (i, 0))
    out, joined, probs, context, normed, rate = pl.pallas_call(
        functools.partial(attend_kernel, cross),
        grid=(groups,),
        in_specs=[
            row(width), row(width), whole(project.shape), whole(output.shape), whole((1, width)),
            row(1), whole(apart.shape),
        ],
        out_specs=[
            row(width), row(3 * width),
            pl.BlockSpec((1, quads, block, 4 * block), lambda i: (i, 0, 0, 0)),
            row(width), row(width), row(1),
        ],
        out_shape=[
            jax.ShapeDtypeStruct((rows, width), BF),
            jax.ShapeDtypeStruct((rows, 3 * width), BF),
            jax.ShapeDtypeStruct((groups, quads, block, 4 * block), BF),
            jax.ShapeDtypeStruct((rows, width), BF),
            jax.ShapeDtypeStruct((rows, width), BF),
            jax.ShapeDtypeStruct((rows, 1), F32),
        ],
        compiler_params=pltpu.CompilerParams(vmem_limit_bytes=VMEM_LIMIT),
        cost_estimate=pl.CostEstimate(
            flops=2 * rows * width * 6 * width, bytes_accessed=24 * rows * width, transcendentals=0
        ),
        name="attend",
    )(x, y, project, output, gain, key_bias, apart)
    return out, (joined, probs, context, normed, rate)


def attend_back_kernel(cross, grad_ref, normed_ref, rate_ref, g_ref, joined_ref, probs_ref, p_ref, o_ref,
                       branch_ref, dj_ref, dx_ref, *rest):
    gain_ref = rest[-1]
    width = grad_ref.shape[1]
    head = width // HEADS
    quad = 4 * head
    scale = head ** (-0.5)
    total, terms = norm_backward(
        grad_ref[...].astype(F32), normed_ref[...].astype(F32), rate_ref[...], g_ref[...]
    )

    @pl.when(pl.program_id(0) == 0)
    def _():
        gain_ref[...] = jnp.zeros_like(gain_ref)

    gain_ref[...] += terms
    branch = total.astype(BF)
    branch_ref[...] = branch
    grad_context = mm(branch, o_ref[...], NN).astype(BF)
    masks = head_masks(quad, head)
    for i in range(width // quad):
        low, high = i * quad, (i + 1) * quad
        q = joined_ref[:, low:high]
        k = joined_ref[:, width + low : width + high]
        v = joined_ref[:, 2 * width + low : 2 * width + high]
        probs = probs_ref[0, i]
        wide = probs.astype(F32)
        grad_heads = spread_heads(grad_context[:, low:high], masks)
        grad_probs = mm(v, grad_heads, NT)
        mean = jnp.sum(wide * grad_probs, axis=0, keepdims=True)
        grad_scores = (wide * (grad_probs - mean)).astype(BF)
        dj_ref[:, low:high] = (fold_heads(mm(grad_scores, k, TN), masks) * scale).astype(BF)
        dj_ref[:, width + low : width + high] = (
            mm(grad_scores, spread_heads(q, masks), NN) * scale
        ).astype(BF)
        dj_ref[:, 2 * width + low : 2 * width + high] = mm(probs, grad_heads, NN).astype(BF)
    if cross:
        dx_ref[...] = total + mm(dj_ref[:, :width], p_ref[:width], NN)
        rest[0][...] = mm(dj_ref[:, width:], p_ref[width:], NN).astype(rest[0].dtype)
    else:
        dx_ref[...] = total + mm(dj_ref[...], p_ref[...], NN)


def attention_block_backward(grad, project, output, gain, saved, cross):
    joined, probs, context, normed, rate = saved
    rows, width = normed.shape
    block = PACK * SLOT
    groups = rows // block
    quads = HEADS // 4
    row = lambda w: pl.BlockSpec((block, w), lambda i: (i, 0))
    extra_spec = [row(width)] if cross else []
    extra_shape = [jax.ShapeDtypeStruct((rows, width), F32)] if cross else []
    return pl.pallas_call(
        functools.partial(attend_back_kernel, cross),
        grid=(groups,),
        in_specs=[
            row(width), row(width), row(1), whole((1, width)), row(3 * width),
            pl.BlockSpec((1, quads, block, 4 * block), lambda i: (i, 0, 0, 0)),
            whole(project.shape), whole(output.shape),
        ],
        out_specs=[row(width), row(3 * width), row(width)] + extra_spec + [whole((8, width))],
        out_shape=[
            jax.ShapeDtypeStruct((rows, width), BF),
            jax.ShapeDtypeStruct((rows, 3 * width), BF),
            jax.ShapeDtypeStruct((rows, width), F32),
        ]
        + extra_shape
        + [jax.ShapeDtypeStruct((8, width), F32)],
        compiler_params=pltpu.CompilerParams(vmem_limit_bytes=VMEM_LIMIT),
        cost_estimate=pl.CostEstimate(
            flops=2 * rows * width * 7 * width, bytes_accessed=32 * rows * width, transcendentals=0
        ),
        name="attend_back",
    )(grad, normed, rate, gain, joined, probs, project, output)


def attend_weights_kernel(parts, dj_ref, x_ref, y_ref, branch_ref, context_ref, p_ref, o_ref):
    step = pl.program_id(0)

    @pl.when(step < parts)
    def _():
        p_ref[...] = mm(dj_ref[...], x_ref[...], TN).astype(BF)

    @pl.when((step >= parts) & (step < 3 * parts))
    def _():
        p_ref[...] = mm(dj_ref[...], y_ref[...], TN).astype(BF)

    @pl.when(step >= 3 * parts)
    def _():
        o_ref[...] = mm(branch_ref[...], context_ref[...], TN).astype(BF)


def attention_weights(dj, x, y, branch, context):
    rows, width = x.shape
    tile = 384
    parts = width // tile
    return pl.pallas_call(
        functools.partial(attend_weights_kernel, parts),
        grid=(4 * parts,),
        in_specs=[
            pl.BlockSpec((rows, tile), lambda i: (0, jnp.minimum(i, 3 * parts - 1))),
            whole(x.shape), whole(y.shape),
            pl.BlockSpec((rows, tile), lambda i: (0, jnp.maximum(i - 3 * parts, 0))),
            whole(context.shape),
        ],
        out_specs=[
            pl.BlockSpec((tile, width), lambda i: (jnp.minimum(i, 3 * parts - 1), 0)),
            pl.BlockSpec((tile, width), lambda i: (jnp.maximum(i - 3 * parts, 0), 0)),
        ],
        out_shape=[
            jax.ShapeDtypeStruct((3 * width, width), BF),
            jax.ShapeDtypeStruct((width, width), BF),
        ],
        compiler_params=pltpu.CompilerParams(vmem_limit_bytes=VMEM_LIMIT),
        cost_estimate=pl.CostEstimate(
            flops=2 * rows * width * 4 * width, bytes_accessed=16 * rows * width, transcendentals=0
        ),
        name="attend_weights",
    )(dj, x, y, branch, context)


def feed_kernel(x_ref, *refs):
    weights, (g_ref, out_ref, hidden_ref, slope_ref, normed_ref, rate_ref) = refs[:4], refs[4:]
    x = x_ref[...]
    wide = weights[0].shape[1]
    total = x.astype(F32)
    for i, weight in enumerate(weights):
        hidden, slope = gelu_pair(mm(x, weight[0], NT))
        hidden = hidden.astype(BF)
        hidden_ref[:, i * wide : (i + 1) * wide] = hidden
        slope_ref[:, i * wide : (i + 1) * wide] = slope.astype(BF)
        total = total + mm(hidden, weight[1], NN)
    normed, rate = norm_forward(total)
    out_ref[...] = (normed * g_ref[...]).astype(BF)
    normed_ref[...] = normed.astype(BF)
    rate_ref[...] = rate


def feed_block(x, weights, gain):
    rows, width = x.shape
    wide = weights[0].shape[1]
    hidden = wide * len(weights)
    block = rows // 3
    row = lambda w: pl.BlockSpec((block, w), lambda i: (i, 0))
    out, *saved = pl.pallas_call(
        feed_kernel,
        grid=(rows // block,),
        in_specs=[row(width)] + [whole(w.shape) for w in weights] + [whole((1, width))],
        out_specs=[row(width), row(hidden), row(hidden), row(width), row(1)],
        out_shape=[
            jax.ShapeDtypeStruct((rows, width), BF),
            jax.ShapeDtypeStruct((rows, hidden), BF),
            jax.ShapeDtypeStruct((rows, hidden), BF),
            jax.ShapeDtypeStruct((rows, width), BF),
            jax.ShapeDtypeStruct((rows, 1), F32),
        ],
        compiler_params=pltpu.CompilerParams(vmem_limit_bytes=VMEM_LIMIT),
        cost_estimate=pl.CostEstimate(
            flops=4 * rows * width * hidden, bytes_accessed=4 * (rows + width) * hidden, transcendentals=0
        ),
        name="feed",
    )(x, *weights, gain)
    return out, tuple(saved)


def norm_back_kernel(grad_ref, normed_ref, rate_ref, g_ref, total_ref, branch_ref, gain_ref):
    total, terms = norm_backward(
        grad_ref[...].astype(F32), normed_ref[...].astype(F32), rate_ref[...], g_ref[...]
    )

    @pl.when(pl.program_id(0) == 0)
    def _():
        gain_ref[...] = jnp.zeros_like(gain_ref)

    gain_ref[...] += terms
    total_ref[...] = total
    branch_ref[...] = total.astype(BF)


def norm_block_backward(grad, normed, rate, gain):
    rows, width = normed.shape
    block = rows // 3
    row = lambda w: pl.BlockSpec((block, w), lambda i: (i, 0))
    return pl.pallas_call(
        norm_back_kernel,
        grid=(rows // block,),
        in_specs=[row(width), row(width), row(1), whole((1, width))],
        out_specs=[row(width), row(width), whole((8, width))],
        out_shape=[
            jax.ShapeDtypeStruct((rows, width), F32),
            jax.ShapeDtypeStruct((rows, width), BF),
            jax.ShapeDtypeStruct((8, width), F32),
        ],
        cost_estimate=pl.CostEstimate(
            flops=10 * rows * width, bytes_accessed=12 * rows * width, transcendentals=0
        ),
        name="norm_back",
    )(grad, normed, rate, gain)


def feed_back_kernel(start_ref, branch_ref, x_ref, *refs):
    inputs, outputs = refs[:8], refs[8:]
    dx_ref = outputs[-1]

    @pl.when(pl.program_id(0) == 0)
    def _():
        dx_ref[...] = start_ref[...]

    branch = branch_ref[...]
    x = x_ref[...]
    for i in range(2):
        up_ref, down_ref, hidden_ref, slope_ref = inputs[4 * i : 4 * i + 4]
        grad_ref = outputs[i]
        grad_hidden = mm(branch, down_ref[0], NT)
        grad_raised = (grad_hidden * slope_ref[...].astype(F32)).astype(BF)
        grad_ref[0] = mm(grad_raised, x, TN).astype(BF)
        grad_ref[1] = mm(hidden_ref[...], branch, TN).astype(BF)
        dx_ref[...] += mm(grad_raised, up_ref[0], NN)


def feed_back(start, branch, x, weights, hidden, slope, first):
    rows, width = x.shape
    wide = weights[0].shape[1]
    tile = 256
    steps = wide // tile
    in_specs = [whole(start.shape), whole(branch.shape), whole(x.shape)]
    operands = [start, branch, x]
    for i, weight in enumerate(weights):
        base = (first + i) * steps
        in_specs += [
            pl.BlockSpec((1, tile, width), lambda s: (0, s, 0)),
            pl.BlockSpec((1, tile, width), lambda s: (1, s, 0)),
            pl.BlockSpec((rows, tile), lambda s, base=base: (0, base + s)),
            pl.BlockSpec((rows, tile), lambda s, base=base: (0, base + s)),
        ]
        operands += [weight, weight, hidden, slope]
    return pl.pallas_call(
        feed_back_kernel,
        grid=(steps,),
        in_specs=in_specs,
        out_specs=[pl.BlockSpec((2, tile, width), lambda s: (0, s, 0))] * 2 + [whole((rows, width))],
        out_shape=[jax.ShapeDtypeStruct((2, wide, width), BF)] * 2
        + [jax.ShapeDtypeStruct((rows, width), F32)],
        compiler_params=pltpu.CompilerParams(vmem_limit_bytes=VMEM_LIMIT),
        cost_estimate=pl.CostEstimate(
            flops=16 * rows * width * wide, bytes_accessed=30 * wide * width, transcendentals=0
        ),
        name="feed_back",
    )(*operands)


def place_kernel(table_ref, mine_ref, theirs_ref, p_ref, o_ref):
    count = mine_ref.shape[0]

    def put(i, carry):
        for source, offset in ((mine_ref, 0), (theirs_ref, count)):
            to = table_ref[offset + i]
            p_ref[to] = source[i, 0:3]
            o_ref[to] = source[i, 3]
        return carry

    lax.fori_loop(0, count, put, 0)


def in_vmem(shape):
    return pl.BlockSpec(shape, lambda: (0,) * len(shape))


def place_weights(table, mine, theirs):
    count, unit, width = mine.shape[0], mine.shape[1] // 4, mine.shape[2]
    cut = lambda a: a.reshape(count, 4, unit, width)
    project, output = pl.pallas_call(
        place_kernel,
        in_specs=[pl.BlockSpec(memory_space=pltpu.SMEM)] + [in_vmem((count, 4, unit, width))] * 2,
        out_specs=[in_vmem((2 * count, 3, unit, width)), in_vmem((2 * count, unit, width))],
        out_shape=[
            jax.ShapeDtypeStruct((2 * count, 3, unit, width), BF),
            jax.ShapeDtypeStruct((2 * count, unit, width), BF),
        ],
        compiler_params=pltpu.CompilerParams(vmem_limit_bytes=VMEM_LIMIT),
        cost_estimate=pl.CostEstimate(flops=0, bytes_accessed=32 * count * unit * width, transcendentals=0),
        name="place",
    )(table, cut(mine), cut(theirs))
    return project.reshape(-1, width), output.reshape(-1, width)


def pick_kernel(table_ref, p_ref, o_ref, mine_ref, theirs_ref):
    count = mine_ref.shape[0]

    def take(i, carry):
        for target, offset in ((mine_ref, 0), (theirs_ref, count)):
            at = table_ref[offset + i]
            target[i, 0:3] = p_ref[at]
            target[i, 3] = o_ref[at]
        return carry

    lax.fori_loop(0, count, take, 0)


def pick_weights(table, project, output):
    width = project.shape[1]
    count = table.shape[0] // 2
    unit = width // (2 * count)
    mine, theirs = pl.pallas_call(
        pick_kernel,
        in_specs=[
            pl.BlockSpec(memory_space=pltpu.SMEM),
            in_vmem((2 * count, 3, unit, width)),
            in_vmem((2 * count, unit, width)),
        ],
        out_specs=[in_vmem((count, 4, unit, width))] * 2,
        out_shape=[jax.ShapeDtypeStruct((count, 4, unit, width), BF)] * 2,
        compiler_params=pltpu.CompilerParams(vmem_limit_bytes=VMEM_LIMIT),
        cost_estimate=pl.CostEstimate(flops=0, bytes_accessed=32 * count * unit * width, transcendentals=0),
        name="pick",
    )(table, project.reshape(2 * count, 3, unit, width), output.reshape(2 * count, unit, width))
    return mine.reshape(count, 4 * unit, width), theirs.reshape(count, 4 * unit, width)


class Cube:
    def __init__(self):
        self.replicas = lax.axis_size("dp")
        self.streams = lax.axis_size("stream")
        low = self.replicas.bit_length() - 1
        bits = low + self.streams.bit_length() - 1
        self.half = bits - 1
        self.core = low
        self.inner = [b for b in range(bits) if b not in (self.half, self.core)]
        self.number = lax.axis_index("stream") * self.replicas + lax.axis_index("dp")

    def swap(self, value, bit):
        step = 1 << bit
        if step < self.replicas:
            return lax.ppermute(value, "dp", [(i, i ^ step) for i in range(self.replicas)])
        step //= self.replicas
        return lax.ppermute(value, "stream", [(i, i ^ step) for i in range(self.streams)])

    def order(self, turn):
        turn %= len(self.inner)
        return self.inner[turn:] + self.inner[:turn]

    def table(self, turn):
        stages = [self.half] + self.order(turn)
        relative = []
        for i in range(1 << len(stages)):
            relative.append(sum(1 << bit for place, bit in enumerate(stages) if i >> place & 1))
        relative += [r | 1 << self.core for r in relative]
        return self.number ^ jnp.array(relative, jnp.int32)

    def gather(self, own, other, turn, axis):
        pieces = jnp.concatenate([own, self.swap(other, self.half)], axis=axis)
        for bit in self.order(turn):
            pieces = jnp.concatenate([pieces, self.swap(pieces, bit)], axis=axis)
        return pieces, self.swap(pieces, self.core)

    def scatter(self, keep, send, turn, axis):
        total = add(keep, self.swap(send, self.core))
        for bit in reversed(self.order(turn)):
            count = total.shape[axis] // 2
            kept = lax.slice_in_dim(total, 0, count, axis=axis)
            sent = lax.slice_in_dim(total, count, 2 * count, axis=axis)
            total = add(kept, self.swap(sent, bit))
        return lax.slice_in_dim(total, 0, 1, axis=axis), lax.slice_in_dim(total, 1, 2, axis=axis)


def add(left, right):
    return (left.astype(F32) + right.astype(F32)).astype(left.dtype)


def on_device(
    states,
    cotangent,
    word_lengths,
    object_project,
    object_output,
    object_up,
    object_down,
    object_gains,
    cross_project,
    cross_output,
    words_project,
    words_output,
    region_project,
    region_output,
    words_up,
    words_down,
    region_up,
    region_down,
    layer_gains,
):
    cube = Cube()
    width = states.shape[1]
    half = cube.streams // 2
    position = lax.axis_index("stream")
    is_words = position < half
    count = states.shape[0] // SLOT
    block = position % half * cube.replicas + lax.axis_index("dp")
    lengths = lax.dynamic_slice_in_dim(word_lengths, block * count, count)
    key_bias = jnp.where(jnp.arange(SLOT)[None, :] < lengths[:, None], 0.0, MASKED).reshape(-1, 1)
    no_bias = jnp.zeros_like(key_bias)
    self_bias = jnp.where(is_words, key_bias, no_bias)
    cross_bias = jnp.where(is_words, no_bias, key_bias)
    packed = PACK * SLOT
    keys = lax.broadcasted_iota(jnp.int32, (packed, 4 * packed), 0) // SLOT
    queries = lax.broadcasted_iota(jnp.int32, (packed, 4 * packed), 1) % packed // SLOT
    apart = jnp.where(keys == queries, 0.0, APART).astype(F32)

    def attention_shard(project, output):
        return jnp.concatenate([project.T, output.T], axis=0)[None]

    def feed_shards(up, down):
        both = jnp.stack([up.T, down])
        middle = both.shape[1] // 2
        return both[:, None, :middle], both[:, None, middle:]

    def gather_layer(own, other, turn):
        attention = cube.gather(own[0], other[0], turn, 0)
        feed = tuple(cube.gather(own[i], other[i], turn + i, 1) for i in (1, 2))
        return attention, tuple(
            piece.reshape(2, -1, width) for pair in feed for piece in pair
        )

    object_shards = (attention_shard(object_project, object_output), *feed_shards(object_up, object_down))
    words_shards = (attention_shard(words_project, words_output), *feed_shards(words_up, words_down))
    region_shards = (attention_shard(region_project, region_output), *feed_shards(region_up, region_down))
    cross_shard = attention_shard(cross_project, cross_output)
    own_shards = tuple(jnp.where(is_words, w, r) for w, r in zip(words_shards, region_shards))
    other_shards = tuple(jnp.where(is_words, r, w) for w, r in zip(words_shards, region_shards))

    gain_shard = jnp.concatenate([object_gains, layer_gains], axis=0)
    kinds, span = gain_shard.shape
    gain_piece = jnp.pad(gain_shard, ((0, 8 - kinds), (0, 128 - span)))[None]
    gain_mine, gain_theirs = cube.gather(gain_piece, gain_piece, 0, 0)
    gain_table = cube.table(0)
    gain_pieces = jnp.concatenate([gain_mine, gain_theirs], axis=0)[jnp.argsort(gain_table)]
    gains = gain_pieces[:, :kinds, :span].transpose(1, 0, 2).reshape(kinds, width).astype(F32)

    (object_pair, object_feed) = gather_layer(object_shards, object_shards, 0)
    others = cube.swap(states, cube.half)
    cross_pair = cube.gather(cross_shard, cross_shard, 2, 0)
    (self_pair, self_feed) = gather_layer(own_shards, other_shards, 0)

    first_table, cross_table = cube.table(0), cube.table(2)
    object_in, object_out = place_weights(first_table, *object_pair)
    cross_in, cross_out = place_weights(cross_table, *cross_pair)
    self_in, self_out = place_weights(first_table, *self_pair)
    self_gain = jnp.where(is_words, gains[3], gains[4])[None]
    feed_gain = jnp.where(is_words, gains[5], gains[6])[None]

    language = jnp.where(is_words, states, others)
    vision = jnp.where(is_words, others, states)

    one, one_saved = attention_block(
        vision, vision, object_in, object_out, gains[0:1], no_bias, apart, False
    )
    two, two_saved = feed_block(one, object_feed, gains[1:2])
    x = jnp.where(is_words, language, two)
    y = jnp.where(is_words, two, language)
    three, three_saved = attention_block(x, y, cross_in, cross_out, gains[2:3], cross_bias, apart, True)
    four, four_saved = attention_block(
        three, three, self_in, self_out, self_gain, self_bias, apart, False
    )
    five, five_saved = feed_block(four, self_feed, feed_gain)

    def feed_backward(grad, rows, weights, gain, saved):
        hidden, slope, normed, rate = saved
        start, branch, gain_terms = norm_block_backward(grad, normed, rate, gain)
        b_keep, b_send, middle = feed_back(start, branch, rows, weights[:2], hidden, slope, 0)
        c_keep, c_send, result = feed_back(middle, branch, rows, weights[2:], hidden, slope, 2)
        return result, gain_terms, ((b_keep, b_send), (c_keep, c_send))

    def scatter_feed(pairs, turn):
        pieces = cube.replicas * cube.streams // 2
        cut = lambda a: a.reshape(2, pieces, -1, width)
        return [cube.scatter(cut(keep), cut(send), turn + i, 1) for i, (keep, send) in ((1, pairs[0]), (2, pairs[1]))]

    grad_four, feed_terms, self_feed_pairs = feed_backward(cotangent, four, self_feed, feed_gain, five_saved)
    self_feed_sums = scatter_feed(self_feed_pairs, 0)

    branch, dj, grad_three, self_terms = attention_block_backward(
        grad_four, self_in, self_out, self_gain, four_saved, False
    )
    self_sums = cube.scatter(
        *pick_weights(first_table, *attention_weights(dj, three, three, branch, four_saved[2])), 0, 0
    )

    branch, dj, grad_x, grad_y, cross_terms = attention_block_backward(
        grad_three, cross_in, cross_out, gains[2:3], three_saved, True
    )
    cross_sums = cube.scatter(
        *pick_weights(cross_table, *attention_weights(dj, x, y, branch, three_saved[2])), 2, 0
    )

    grad_two = jnp.where(is_words, grad_y, grad_x)
    grad_one, two_terms, object_feed_pairs = feed_backward(grad_two, one, object_feed, gains[1:2], two_saved)
    object_feed_sums = scatter_feed(object_feed_pairs, 0)
    branch, dj, grad_vision, one_terms = attention_block_backward(
        grad_one, object_in, object_out, gains[0:1], one_saved, False
    )
    object_sums = cube.scatter(
        *pick_weights(first_table, *attention_weights(dj, vision, vision, branch, one_saved[2])), 0, 0
    )
    sent = jnp.where(is_words, grad_vision, grad_y).astype(BF)
    received = cube.swap(sent, cube.half).astype(F32)
    grad_states = jnp.where(is_words, grad_x, grad_vision) + received

    words_side = is_words.astype(F32)
    region_side = 1.0 - words_side
    sums = [one_terms, two_terms, cross_terms, self_terms, self_terms, feed_terms, feed_terms]
    sides = [1.0, 1.0, 1.0, words_side, region_side, words_side, region_side]
    gain_sums = jnp.stack([jnp.sum(s, axis=0) * side for s, side in zip(sums, sides)])
    gain_cut = gain_sums.reshape(kinds, -1, span).transpose(1, 0, 2)
    gain_cut = jnp.pad(gain_cut, ((0, 0), (0, 8 - kinds), (0, 128 - span)))[gain_table]
    middle = gain_cut.shape[0] // 2
    gain_own, gain_other = cube.scatter(gain_cut[:middle], gain_cut[middle:], 0, 0)
    gain_grad = (gain_own + cube.swap(gain_other, cube.half))[0, :kinds, :span]

    def both(sums):
        own, other = sums
        return own.astype(F32) + cube.swap(other, cube.half).astype(F32)

    def apart_by_stream(sums):
        own, other = sums
        received = cube.swap(other, cube.half)
        return (
            jnp.where(is_words, own, received).astype(F32),
            jnp.where(is_words, received, own).astype(F32),
        )

    def attention_grads(piece):
        flat = piece[0]
        cut = 3 * flat.shape[0] // 4
        return flat[:cut].T, flat[cut:].T

    def feed_grads(first, second):
        joined = jnp.concatenate([first[:, 0], second[:, 0]], axis=1)
        return joined[0].T, joined[1]

    object_project_grad, object_output_grad = attention_grads(both(object_sums))
    object_up_grad, object_down_grad = feed_grads(*[both(s) for s in object_feed_sums])
    cross_project_grad, cross_output_grad = attention_grads(both(cross_sums))
    words_piece, region_piece = apart_by_stream(self_sums)
    words_project_grad, words_output_grad = attention_grads(words_piece)
    region_project_grad, region_output_grad = attention_grads(region_piece)
    split = [apart_by_stream(s) for s in self_feed_sums]
    words_up_grad, words_down_grad = feed_grads(split[0][0], split[1][0])
    region_up_grad, region_down_grad = feed_grads(split[0][1], split[1][1])
    return (
        five,
        grad_states,
        object_project_grad,
        object_output_grad,
        object_up_grad,
        object_down_grad,
        gain_grad[:2],
        cross_project_grad,
        cross_output_grad,
        words_project_grad,
        words_output_grad,
        region_project_grad,
        region_output_grad,
        words_up_grad,
        words_down_grad,
        region_up_grad,
        region_down_grad,
        gain_grad[2:],
    )


def solution(mesh):
    rows = P(("stream", "dp"), None)
    columns = P(None, ("stream", "dp"))
    in_specs = (
        rows, rows, P(),
        columns, columns, columns, rows, columns,
        columns, columns,
        columns, columns, columns, columns,
        columns, rows, columns, rows,
        columns,
    )
    out_specs = (
        rows, rows,
        columns, columns, columns, rows, columns,
        columns, columns,
        columns, columns, columns, columns,
        columns, rows, columns, rows,
        columns,
    )
    return jax.shard_map(
        on_device, mesh=mesh, in_specs=in_specs, out_specs=out_specs, check_vma=False
    )
```

time: 2760 us -> 797 us (0.29)
  blocking collectives: 1070 us -> 0 us
  local copies, waits for them, and re-layouts: 705 us -> 99 us
  waiting for transfers between devices: 666 us -> 245 us
  Pallas kernels: 0 us -> 294 us
  matrix products: 164 us -> 0 us
  starting transfers between devices: 8.77 us -> 86.7 us
  other arithmetic: 101 us -> 61 us
    all_to_all x1 -> x0, blocking collectives: 862 us -> none  [on_device(): lax.all_to_all(outgoing.astype(jnp.bfloat16), ('stream', 'dp'), split_axi...]
    all_gather x14 -> x0, waiting for transfers between devices: 624 us -> none  [the longest x1 65.4 us: on_device(): lax.all_gather(object_up, ('stream', 'dp'), axis=1, tiled=True)]
    unnamed x185 -> x200, local copies, waits for them, and re-layouts: 391 us -> 43.6 us
    pallas_call x0 -> x23, Pallas kernels: none -> 294 us  [the longest x4 70.9 us: feed_back(): pl.pallas_call(feed_back_kernel, grid=(steps,), in_specs=in_specs, out_sp...]
    ppermute x2 -> x82, waiting for transfers between devices: 34 us -> 245 us  [the longest x66 195 us: swap(): lax.ppermute(value, 'stream', [(i, i ^ step) for i in range(self.streams)])]
    all_gather x2 -> x0, blocking collectives: 208 us -> none  [the longest x1 139 us: on_device(): lax.all_gather(layer_gains, ('stream', 'dp'), axis=1, tiled=True)]
    dot_general x30 -> x0, matrix products: 164 us -> none  [the longest x2 18.3 us: attention_backward(): jnp.einsum('nahd,nbhd->nhab', grad_heads, split_heads(values), preferred_...]
    concatenate x16, local copies, waits for them, and re-layouts: 116 us -> 16.6 us  [the longest x15 16.6 us: gather(): pieces = jnp.concatenate([pieces, self.swap(pieces, bit)], axis=axis)]
  transfers between devices with their start and end apart: 16 -> 82, of which waited for: 13 -> 28; matrix products, arithmetic and copies ran while one was open for 7% -> 16% of each run, Pallas kernels for 0% -> 17%
where the time goes in v1:
time: 797 us; the launch traced here: 788 us
  Pallas kernels  294 us (37%)
  waiting for transfers between devices  245 us (31%)
  local copies, waits for them, and re-layouts  99 us (12%)
  starting transfers between devices  86.7 us (11%)
  other arithmetic  61 us (8%)
    ppermute x66, waiting for transfers between devices, swap(): lax.ppermute(value, 'stream', [(i, i ^ step) for i in range(self.streams)])  195 us
    pallas_call x4, Pallas kernels, feed_back(): pl.pallas_call(feed_back_kernel, grid=(steps,), in_specs=in_specs, out_sp...  70.9 us
    ppermute x66, starting transfers between devices, swap(): lax.ppermute(value, 'stream', [(i, i ^ step) for i in range(self.streams)])  68.7 us
    pallas_call x3, Pallas kernels, attention_block(): pl.pallas_call(functools.partial(attend_kernel, cross), grid=(groups,), i...  62.4 us
    pallas_call x3, Pallas kernels, attention_block_backward(): pl.pallas_call(functools.partial(attend_back_kernel, cross), grid=(groups...  58 us
    ppermute x16, waiting for transfers between devices, swap(): lax.ppermute(value, 'dp', [(i, i ^ step) for i in range(self.replicas)])  49.3 us
    unnamed x200, local copies, waits for them, and re-layouts  43.6 us
    pallas_call x2, Pallas kernels, feed_block(): pl.pallas_call(feed_kernel, grid=(rows // block,), in_specs=[row(width)]...  42.2 us
  transfers between devices with their start and end apart: 82, of which 28 were waited for; matrix products, arithmetic and copies ran while one was open for 16% of the time, Pallas kernels for 17%

profile of v1, /device:TPU:0, one launch (start us, length us, event | category | flops | bytes accessed | tf_op | source)
XLA Modules:
  0.0 788.3 jit_solution(10769849789161640971)
XLA Ops:
  80.8 6.2 collective-permute-done.3
  95.1 7.6 collective-permute-done.18
  105.3 24.9 %collective-permute-done.13 = bf16[2,4,48,768]{3,2,0,1:T(8,128)(2,1)S(1)} collective-permute-done((bf16[2,4,48,768]{3,2,0,1:T(8,128)(2,1)S(1)}, bf16[2,4,48,768]{3,2,0,1:T(8,128)(2,1)S(1)}, u32[]{:S(2)}, u32[]{:S(2)}) %collective-permute-start.13) | collective-permute-done | bytes 589856 | tf_op jit(solution)/shard_map/ppermute | solution.py:481
  137.1 5.8 collective-permute-done.33
  146.9 10.9 %collective-permute-done.38 = bf16[2,4,48,768]{3,2,0,1:T(8,128)(2,1)S(1)} collective-permute-done((bf16[2,4,48,768]{3,2,0,1:T(8,128)(2,1)S(1)}, bf16[2,4,48,768]{3,2,0,1:T(8,128)(2,1)S(1)}, u32[]{:S(2)}, u32[]{:S(2)}) %collective-permute-start.38) | collective-permute-done | bytes 589856 | tf_op jit(solution)/shard_map/ppermute | solution.py:479
  162.4 10.6 %collective-permute-start = (bf16[864,768]{1,0:T(8,128)(2,1)S(1)}, bf16[864,768]{1,0:T(8,128)(2,1)S(1)}, u32[]{:S(2)}, u32[]{:S(2)}) collective-permute-start(bf16[864,768]{1,0:T(8,128)(2,1)S(1)} %copy-done.59), channel_id=1, source_target_pairs={{0,16},{2,18},{4,20},{6,22},{8,24},{10,26},{12,28},{14,30},{16,0},... | collective-permute-start | bytes 3981320 | tf_op jit(solution)/shard_map/ppermute | solution.py:481
  180.1 7.1 collective-permute-done.24
  192.2 20.3 %collective-permute-done = bf16[864,768]{1,0:T(8,128)(2,1)S(1)} collective-permute-done((bf16[864,768]{1,0:T(8,128)(2,1)S(1)}, bf16[864,768]{1,0:T(8,128)(2,1)S(1)}, u32[]{:S(2)}, u32[]{:S(2)}) %collective-permute-start) | collective-permute-done | bytes 1327136 | tf_op jit(solution)/shard_map/ppermute | solution.py:481
  230.6 20.6 %attend.3 = (bf16[864,768]{1,0:T(8,128)(2,1)S(1)}, bf16[864,2304]{1,0:T(8,128)(2,1)}, bf16[6,3,144,576]{3,2,1,0:T(8,128)(2,1)}, bf16[864,768]{1,0:T(8,128)(2,1)S...) custom-call(bf16[864,768]{1,0:T(8,128)(2,1)} %broadcast_select_fusion.3.x_ref.y_ref, ...), custom_call_target="tpu_custom_call" | custom-call | flops 6115295232 | bytes 15925248 | tf_op jit(solution)/shard_map/attend/pallas_call | solution.py:117
  271.2 21.3 %feed.2 = (bf16[864,768]{1,0:T(8,128)(2,1)S(1)}, bf16[864,3072]{1,0:T(8,128)(2,1)}, bf16[864,3072]{1,0:T(8,128)(2,1)}, bf16[864,768]{1,0:T(8,128)(2,1)S(1)}, f32[864,1]{1,0:T(8,128)S(1)}) custom-call(bf16[864,768]{1,0:T(8,128)(2,1)S(1)} %get-tuple-element.99.x_ref, bf16[2,768,768]{2,1,0:T(8,128)(2,1)} %bitcast.214, bf16[2,768,768]{2,1,0:T(8,128)(2,1)} %bitcast.223, ...), custom_call_target="tpu_custom_call" | custom-call | flops 8153726976 | bytes 20054016 | tf_op jit(solution)/shard_map/feed/pallas_call | solution.py:290
  294.6 20.6 %attend.4 = (bf16[864,768]{1,0:T(8,128)(2,1)S(1)}, bf16[864,2304]{1,0:T(8,128)(2,1)}, bf16[6,3,144,576]{3,2,1,0:T(8,128)(2,1)}, bf16[864,768]{1,0:T(8,128)(2,1)S...) custom-call(bf16[864,768]{1,0:T(8,128)(2,1)} %get-tuple-element.192.x_ref, ...), custom_call_target="tpu_custom_call" | custom-call | flops 6115295232 | bytes 15925248 | tf_op jit(solution)/shard_map/attend/pallas_call | solution.py:117
  316.3 21.2 %attend.5 = (bf16[864,768]{1,0:T(8,128)(2,1)S(1)}, bf16[864,2304]{1,0:T(8,128)(2,1)}, bf16[6,3,144,576]{3,2,1,0:T(8,128)(2,1)}, bf16[864,768]{1,0:T(8,128)(2,1)S...) custom-call(bf16[864,768]{1,0:T(8,128)(2,1)} %copy-done.38, bf16[864,768]{1,0:T(8,128)(2,1)} %copy-done.38, ...), custom_call_target="tpu_custom_call" | custom-call | flops 6115295232 | bytes 15925248 | tf_op jit(solution)/shard_map/attend/pallas_call | solution.py:117
  342.0 20.8 %feed.3 = (bf16[864,768]{1,0:T(8,128)(2,1)}, bf16[864,3072]{1,0:T(8,128)(2,1)}, bf16[864,3072]{1,0:T(8,128)(2,1)}, bf16[864,768]{1,0:T(8,128)(2,1)S(1)}, f32[864,1]{1,0:T(8,128)S(1)}) custom-call(bf16[864,768]{1,0:T(8,128)(2,1)S(1)} %get-tuple-element.106.x_ref, bf16[2,768,768]{2,1,0:T(8,128)(2,1)S(1)} %bitcast.191, bf16[2,768,768]{2,1,0:T(8,128)(2,1)} %bitcast.226, ...), custom_call_target="tpu_custom_call" | custom-call | flops 8153726976 | bytes 20054016 | tf_op jit(solution)/shard_map/feed/pallas_call | solution.py:290
  371.6 17.6 %feed_back.4 = (bf16[2,768,768]{2,1,0:T(8,128)(2,1)S(1)}, bf16[2,768,768]{2,1,0:T(8,128)(2,1)}, f32[864,768]{1,0:T(8,128)}) custom-call(f32[864,768]{1,0:T(8,128)} %get-tuple-element.110.start_ref, bf16[864,768]{1,0:T(8,128)(2,1)S(1)} %copy-done.6, bf16[864,768]{1,0:T(8,128)(2,1)S(1)} %copy-done.4, bf16[2,768,768]{2,1,0:T(8,128)(2,1)} %bitcast.192, ...), custom_call_target="tpu_custom_call" | custom-call | flops 8153726976 | bytes 17694720 | tf_op jit(solution)/shard_map/feed_back/pallas_call | solution.py:382
  390.6 17.8 %feed_back.5 = (bf16[2,768,768]{2,1,0:T(8,128)(2,1)S(1)}, bf16[2,768,768]{2,1,0:T(8,128)(2,1)}, f32[864,768]{1,0:T(8,128)}) custom-call(f32[864,768]{1,0:T(8,128)} %get-tuple-element.114.start_ref, bf16[864,768]{1,0:T(8,128)(2,1)S(1)} %copy-done.6, bf16[864,768]{1,0:T(8,128)(2,1)S(1)} %copy-done.4, bf16[2,768,768]{2,1,0:T(8,128)(2,1)} %bitcast.221, ...), custom_call_target="tpu_custom_call" | custom-call | flops 8153726976 | bytes 17694720 | tf_op jit(solution)/shard_map/feed_back/pallas_call | solution.py:382
  409.8 19.5 %attend_back.3 = (bf16[864,768]{1,0:T(8,128)(2,1)S(1)}, bf16[864,2304]{1,0:T(8,128)(2,1)}, f32[864,768]{1,0:T(8,128)}, f32[8,768]{1,0:T(8,128)S(1)}) custom-call(f32[864,768]{1,0:T(8,128)} %get-tuple-element.115.grad_ref, bf16[864,768]{1,0:T(8,128)(2,1)S(1)} %copy-done.50, f32[864,1]{1,0:T(8,128)S(1)} %copy-done.56, f32[1,768]{1,0:T(1,128)S(1)} %select_n.256.g_ref, ...), custom_call_target="tpu_custom_call" | custom-call | flops 7134511104 | bytes 21233664 | tf_op jit(solution)/shard_map/attend_back/pallas_call | solution.py:198
  430.4 19.1 %attend_back.4 = (bf16[864,768]{1,0:T(8,128)(2,1)S(1)}, bf16[864,2304]{1,0:T(8,128)(2,1)}, f32[864,768]{1,0:T(8,128)}, f32[864,768]{1,0:T(8,128)}, f32[8,768]{1,0:T(8,128)S(1)}) custom-call(f32[864,768]{1,0:T(8,128)} %get-tuple-element.120.grad_ref, bf16[864,768]{1,0:T(8,128)(2,1)S(1)} %copy-done.49, f32[864,1]{1,0:T(8,128)S(1)} %copy-done.54, ...), custom_call_target="tpu_custom_call" | custom-call | flops 7134511104 | bytes 21233664 | tf_op jit(solution)/shard_map/attend_back/pallas_call | solution.py:198
  453.6 5.8 norm_back.3
  460.7 18.0 %feed_back.6 = (bf16[2,768,768]{2,1,0:T(8,128)(2,1)S(1)}, bf16[2,768,768]{2,1,0:T(8,128)(2,1)}, f32[864,768]{1,0:T(8,128)}) custom-call(f32[864,768]{1,0:T(8,128)} %get-tuple-element.129.start_ref, bf16[864,768]{1,0:T(8,128)(2,1)S(1)} %copy-done.5, bf16[864,768]{1,0:T(8,128)(2,1)S(1)} %copy-done.2, bf16[2,768,768]{2,1,0:T(8,128)(2,1)} %bitcast.215, ...), custom_call_target="tpu_custom_call" | custom-call | flops 8153726976 | bytes 17694720 | tf_op jit(solution)/shard_map/feed_back/pallas_call | solution.py:382
  480.2 17.6 %feed_back.7 = (bf16[2,768,768]{2,1,0:T(8,128)(2,1)S(1)}, bf16[2,768,768]{2,1,0:T(8,128)(2,1)}, f32[864,768]{1,0:T(8,128)}) custom-call(f32[864,768]{1,0:T(8,128)} %get-tuple-element.133.start_ref, bf16[864,768]{1,0:T(8,128)(2,1)S(1)} %copy-done.5, bf16[864,768]{1,0:T(8,128)(2,1)S(1)} %copy-done.2, bf16[2,768,768]{2,1,0:T(8,128)(2,1)} %bitcast.212, ...), custom_call_target="tpu_custom_call" | custom-call | flops 8153726976 | bytes 17694720 | tf_op jit(solution)/shard_map/feed_back/pallas_call | solution.py:382
  499.2 19.4 %attend_back.5 = (bf16[864,768]{1,0:T(8,128)(2,1)S(1)}, bf16[864,2304]{1,0:T(8,128)(2,1)}, f32[864,768]{1,0:T(8,128)}, f32[8,768]{1,0:T(8,128)S(1)}) custom-call(f32[864,768]{1,0:T(8,128)} %get-tuple-element.134.grad_ref, bf16[864,768]{1,0:T(8,128)(2,1)S(1)} %copy-done.48, f32[864,1]{1,0:T(8,128)S(1)} %copy-done.52, f32[1,768]{1,0:T(1,128)S(1)} %slice.339.g_ref, ...), custom_call_target="tpu_custom_call" | custom-call | flops 7134511104 | bytes 21233664 | tf_op jit(solution)/shard_map/attend_back/pallas_call | solution.py:198
  534.7 9.8 %attend_weights.5 = (bf16[2304,768]{1,0:T(8,128)(2,1)}, bf16[768,768]{1,0:T(8,128)(2,1)S(1)}) custom-call(bf16[864,2304]{1,0:T(8,128)(2,1)} %get-tuple-element.163.dj_ref, bf16[864,768]{1,0:T(8,128)(2,1)S(1)} %copy-done.39, bf16[864,768]{1,0:T(8,128)(2,1)S(1)} %copy-done.39, bf16[864,768]{1,0:T(8,128)(2,1)S(1)} %copy-done.47, bf16[864,768]{1,0:T(8,128)(2,1)S(1)} %copy-done.41), custom_call_target="tpu_custom_call" | custom-call | flops 4076863488 | bytes 10616832 | tf_op jit(solution)/shard_map/attend_weights/pallas_call | solution.py:242
  549.1 10.3 %attend_weights.4 = (bf16[2304,768]{1,0:T(8,128)(2,1)}, bf16[768,768]{1,0:T(8,128)(2,1)S(1)}) custom-call(bf16[864,2304]{1,0:T(8,128)(2,1)} %get-tuple-element.156.dj_ref, bf16[864,768]{1,0:T(8,128)(2,1)S(1)} %copy-done.22, bf16[864,768]{1,0:T(8,128)(2,1)S(1)} %copy-done.21, bf16[864,768]{1,0:T(8,128)(2,1)S(1)} %copy-done.43, bf16[864,768]{1,0:T(8,128)(2,1)} %copy-done.37), custom_call_target="tpu_custom_call" | custom-call | flops 4076863488 | bytes 10616832 | tf_op jit(solution)/shard_map/attend_weights/pallas_call | solution.py:242
  562.0 29.4 %collective-permute-done.61 = f32[1,8,128]{2,1,0:T(8,128)S(1)} collective-permute-done((f32[1,8,128]{2,1,0:T(8,128)S(1)}, f32[1,8,128]{2,1,0:T(8,128)S(1)}, u32[]{:S(2)}, u32[]{:S(2)}) %collective-permute-start.61) | collective-permute-done | bytes 4128 | tf_op jit(solution)/shard_map/ppermute | solution.py:481
  591.4 9.8 %attend_weights.3 = (bf16[2304,768]{1,0:T(8,128)(2,1)}, bf16[768,768]{1,0:T(8,128)(2,1)S(1)}) custom-call(bf16[864,2304]{1,0:T(8,128)(2,1)} %get-tuple-element.140.dj_ref, bf16[864,768]{1,0:T(8,128)(2,1)S(1)} %copy-done.20, bf16[864,768]{1,0:T(8,128)(2,1)S(1)} %copy-done.20, bf16[864,768]{1,0:T(8,128)(2,1)S(1)} %copy-done.45, bf16[864,768]{1,0:T(8,128)(2,1)S(1)} %copy-done.36), custom_call_target="tpu_custom_call" | custom-call | flops 4076863488 | bytes 10616832 | tf_op jit(solution)/shard_map/attend_weights/pallas_call | solution.py:242
  635.5 15.3 %collective-permute-done.73 = bf16[2,8,48,768]{3,2,0,1:T(8,128)(2,1)S(1)} collective-permute-done((bf16[2,8,48,768]{3,2,0,1:T(8,128)(2,1)S(1)}, bf16[2,8,48,768]{3,2,0,1:T(8,128)(2,1)S(1)}, u32[]{:S(2)}, u32[]{:S(2)}) %collective-permute-start.73) | collective-permute-done | bytes 1179680 | tf_op jit(solution)/shard_map/ppermute | solution.py:479
  659.4 21.1 %collective-permute-done.63 = bf16[8,96,768]{2,1,0:T(8,128)(2,1)S(1)} collective-permute-done((bf16[8,96,768]{2,1,0:T(8,128)(2,1)S(1)}, bf16[8,96,768]{2,1,0:T(8,128)(2,1)S(1)}, u32[]{:S(2)}, u32[]{:S(2)}) %collective-permute-start.63) | collective-permute-done | bytes 1179680 | tf_op jit(solution)/shard_map/ppermute | solution.py:481
  682.6 23.2 %collective-permute-done.53 = bf16[2,8,48,768]{3,2,0,1:T(8,128)(2,1)S(1)} collective-permute-done((bf16[2,8,48,768]{3,2,0,1:T(8,128)(2,1)S(1)}, bf16[2,8,48,768]{3,2,0,1:T(8,128)(2,1)S(1)}, u32[]{:S(2)}, u32[]{:S(2)}) %collective-permute-start.53) | collective-permute-done | bytes 1179680 | tf_op jit(solution)/shard_map/ppermute | solution.py:481
  710.3 8.1 %collective-permute-done.69 = bf16[4,96,768]{2,1,0:T(8,128)(2,1)S(1)} collective-permute-done((bf16[4,96,768]{2,1,0:T(8,128)(2,1)S(1)}, bf16[4,96,768]{2,1,0:T(8,128)(2,1)S(1)}, u32[]{:S(2)}, u32[]{:S(2)}) %collective-permute-start.69) | collective-permute-done | bytes 589856 | tf_op jit(solution)/shard_map/ppermute | solution.py:481
  722.6 11.7 %collective-permute-done.54 = bf16[2,4,48,768]{3,2,0,1:T(8,128)(2,1)S(1)} collective-permute-done((bf16[2,4,48,768]{3,2,0,1:T(8,128)(2,1)S(1)}, bf16[2,4,48,768]{3,2,0,1:T(8,128)(2,1)S(1)}, u32[]{:S(2)}, u32[]{:S(2)}) %collective-permute-start.54) | collective-permute-done | bytes 589856 | tf_op jit(solution)/shard_map/ppermute | solution.py:479
  740.5 9.7 %collective-permute-done.65 = bf16[2,96,768]{2,1,0:T(8,128)(2,1)S(1)} collective-permute-done((bf16[2,96,768]{2,1,0:T(8,128)(2,1)S(1)}, bf16[2,96,768]{2,1,0:T(8,128)(2,1)S(1)}, u32[]{:S(2)}, u32[]{:S(2)}) %collective-permute-start.65) | collective-permute-done | bytes 294944 | tf_op jit(solution)/shard_map/ppermute | solution.py:481
  756.8 14.2 %collective-permute-done.81 = bf16[2,1,48,768]{3,2,0,1:T(8,128)(2,1)S(1)} collective-permute-done((bf16[2,1,48,768]{3,2,0,1:T(8,128)(2,1)S(1)}, bf16[2,1,48,768]{3,2,0,1:T(8,128)(2,1)S(1)}, u32[]{:S(2)}, u32[]{:S(2)}) %collective-permute-start.81) | collective-permute-done | bytes 147488 | tf_op jit(solution)/shard_map/ppermute | solution.py:481
  (546 shorter events, 290.2 us)
Async XLA Ops:
  7.7 35.1 %collective-permute-start.1 = (bf16[1,96,768]{2,1,0:T(8,128)(2,1)}, bf16[1,96,768]{2,1,0:T(8,128)(2,1)}, u32[]{:S(2)}, u32[]{:S(2)}) collective-permute-start(bf16[1,96,768]{2,1,0:T(8,128)(2,1)} %get-tuple-element.214), channel_id=1, source_target_pairs={{0,16},{2,18},{4,20},{6,22},{8,24},{10,26},{12,28},{14,30},{16,0},... | collective-permute-start | bytes 442376 | tf_op jit(solution)/shard_map/ppermute | solution.py:481
  9.6 37.1 %collective-permute-start.16 = (bf16[2,1,48,768]{3,2,0,1:T(8,128)(2,1)}, bf16[2,1,48,768]{3,2,0,1:T(8,128)(2,1)}, u32[]{:S(2)}, u32[]{:S(2)}) collective-permute-start(bf16[2,1,48,768]{3,2,0,1:T(8,128)(2,1)} %get-tuple-element.186), channel_id=1, source_target_pairs={{0,16},{2,18},{4,20},{6,22},{8,24},{10,26},{12,28},{14,30},{16,0},... | collective-permute-start | bytes 442376 | tf_op jit(solution)/shard_map/ppermute | solution.py:481
  12.5 39.9 %collective-permute-start.11 = (bf16[2,1,48,768]{3,2,0,1:T(8,128)(2,1)}, bf16[2,1,48,768]{3,2,0,1:T(8,128)(2,1)}, u32[]{:S(2)}, u32[]{:S(2)}) collective-permute-start(bf16[2,1,48,768]{3,2,0,1:T(8,128)(2,1)} %get-tuple-element.211), channel_id=1, source_target_pairs={{0,16},{2,18},{4,20},{6,22},{8,24},{10,26},{12,28},{14,30},{16,0},... | collective-permute-start | bytes 442376 | tf_op jit(solution)/shard_map/ppermute | solution.py:481
  14.2 34.8 %collective-permute-start.21 = (bf16[1,96,768]{2,1,0:T(8,128)(2,1)}, bf16[1,96,768]{2,1,0:T(8,128)(2,1)}, u32[]{:S(2)}, u32[]{:S(2)}) collective-permute-start(bf16[1,96,768]{2,1,0:T(8,128)(2,1)} %get-tuple-element.212), channel_id=1, source_target_pairs={{0,16},{2,18},{4,20},{6,22},{8,24},{10,26},{12,28},{14,30},{16,0},... | collective-permute-start | bytes 442376 | tf_op jit(solution)/shard_map/ppermute | solution.py:481
  88.6 45.9 %collective-permute-start.4 = (bf16[8,96,768]{2,1,0:T(8,128)(2,1)S(1)}, bf16[8,96,768]{2,1,0:T(8,128)(2,1)S(1)}, u32[]{:S(2)}, u32[]{:S(2)}) collective-permute-start(bf16[8,96,768]{2,1,0:T(8,128)(2,1)S(1)} %pad_maximum_fusion), channel_id=1, source_target_pairs={{0,8},{2,10},{4,12},{6,14},{8,0},{10,2},{12,4},{14,6},{16,24},{18,... | collective-permute-start | bytes 3538952 | tf_op jit(solution)/shard_map/ppermute | solution.py:481
  91.6 38.7 %collective-permute-start.13 = (bf16[2,4,48,768]{3,2,0,1:T(8,128)(2,1)S(1)}, bf16[2,4,48,768]{3,2,0,1:T(8,128)(2,1)S(1)}, u32[]{:S(2)}, u32[]{:S(2)}) collective-permute-start(bf16[2,4,48,768]{3,2,0,1:T(8,128)(2,1)S(1)} %pad_maximum_fusion.8), channel_id=1, source_target_pairs={{0,8},{2,10},{4,12},{6,14},{8,0},{10,2},{12,4},{14,6},{16,24},{18,... | collective-permute-start | bytes 1769480 | tf_op jit(solution)/shard_map/ppermute | solution.py:481
  92.8 39.0 %collective-permute-start.28 = (bf16[4,96,768]{2,1,0:T(8,128)(2,1)S(1)}, bf16[4,96,768]{2,1,0:T(8,128)(2,1)S(1)}, u32[]{:S(2)}, u32[]{:S(2)}) collective-permute-start(bf16[4,96,768]{2,1,0:T(8,128)(2,1)S(1)} %pad_maximum_fusion.11), channel_id=1, source_target_pairs={{0,4},{2,6},{4,0},{6,2},{8,12},{10,14},{12,8},{14,10},{16,20},{18,... | collective-permute-start | bytes 1769480 | tf_op jit(solution)/shard_map/ppermute | solution.py:481
  93.5 42.9 %collective-permute-start.23 = (bf16[4,96,768]{2,1,0:T(8,128)(2,1)S(1)}, bf16[4,96,768]{2,1,0:T(8,128)(2,1)S(1)}, u32[]{:S(2)}, u32[]{:S(2)}) collective-permute-start(bf16[4,96,768]{2,1,0:T(8,128)(2,1)S(1)} %pad_maximum_fusion.10), channel_id=1, source_target_pairs={{0,1},{1,0},{2,3},{3,2},{4,5},{5,4},{6,7},{7,6},{8,9},{9,8},{10,11... | collective-permute-start | bytes 1769480 | tf_op jit(solution)/shard_map/ppermute | solution.py:479
  102.8 40.1 %collective-permute-start.33 = (bf16[2,4,48,768]{3,2,0,1:T(8,128)(2,1)S(1)}, bf16[2,4,48,768]{3,2,0,1:T(8,128)(2,1)S(1)}, u32[]{:S(2)}, u32[]{:S(2)}) collective-permute-start(bf16[2,4,48,768]{3,2,0,1:T(8,128)(2,1)S(1)} %pad_maximum_fusion.12), channel_id=1, source_target_pairs={{0,8},{2,10},{4,12},{6,14},{8,0},{10,2},{12,4},{14,6},{16,24},{18,... | collective-permute-start | bytes 1769480 | tf_op jit(solution)/shard_map/ppermute | solution.py:481
  131.9 41.1 %collective-permute-start.14 = (bf16[2,8,48,768]{3,2,0,1:T(8,128)(2,1)S(1)}, bf16[2,8,48,768]{3,2,0,1:T(8,128)(2,1)S(1)}, u32[]{:S(2)}, u32[]{:S(2)}) collective-permute-start(bf16[2,8,48,768]{3,2,0,1:T(8,128)(2,1)S(1)} %pad_maximum_fusion.1), channel_id=1, source_target_pairs={{0,1},{1,0},{2,3},{3,2},{4,5},{5,4},{6,7},{7,6},{8,9},{9,8},{10,11... | collective-permute-start | bytes 3538952 | tf_op jit(solution)/shard_map/ppermute | solution.py:479
  134.5 41.0 %collective-permute-start.29 = (bf16[8,96,768]{2,1,0:T(8,128)(2,1)S(1)}, bf16[8,96,768]{2,1,0:T(8,128)(2,1)S(1)}, u32[]{:S(2)}, u32[]{:S(2)}) collective-permute-start(bf16[8,96,768]{2,1,0:T(8,128)(2,1)S(1)} %pad_maximum_fusion.4), channel_id=1, source_target_pairs={{0,8},{2,10},{4,12},{6,14},{8,0},{10,2},{12,4},{14,6},{16,24},{18,... | collective-permute-start | bytes 3538952 | tf_op jit(solution)/shard_map/ppermute | solution.py:481
  142.9 70.1 %collective-permute-start.5 = (bf16[16,96,768]{2,1,0:T(8,128)(2,1)S(1)}, bf16[16,96,768]{2,1,0:T(8,128)(2,1)S(1)}, u32[]{:S(2)}, u32[]{:S(2)}) collective-permute-start(bf16[16,96,768]{2,1,0:T(8,128)(2,1)S(1)} %constant_dynamic-update-slice_fusion.5), channel_id=1, source_target_pairs={{0,2},{2,0},{4,6},{6,4},{8,10},{10,8},{12,14},{14,12},{16,18},{18,... | collective-permute-start | bytes 7077896 | tf_op jit(solution)/shard_map/ppermute | solution.py:481
  162.4 50.1 %collective-permute-start = (bf16[864,768]{1,0:T(8,128)(2,1)S(1)}, bf16[864,768]{1,0:T(8,128)(2,1)S(1)}, u32[]{:S(2)}, u32[]{:S(2)}) collective-permute-start(bf16[864,768]{1,0:T(8,128)(2,1)S(1)} %copy-done.59), channel_id=1, source_target_pairs={{0,16},{2,18},{4,20},{6,22},{8,24},{10,26},{12,28},{14,30},{16,0},... | collective-permute-start | bytes 3981320 | tf_op jit(solution)/shard_map/ppermute | solution.py:481
  175.5 37.1 %collective-permute-start.39 = (bf16[2,8,48,768]{3,2,0,1:T(8,128)(2,1)S(1)}, bf16[2,8,48,768]{3,2,0,1:T(8,128)(2,1)S(1)}, u32[]{:S(2)}, u32[]{:S(2)}) collective-permute-start(bf16[2,8,48,768]{3,2,0,1:T(8,128)(2,1)S(1)} %pad_maximum_fusion.6), channel_id=1, source_target_pairs={{0,4},{2,6},{4,0},{6,2},{8,12},{10,14},{12,8},{14,10},{16,20},{18,... | collective-permute-start | bytes 3538952 | tf_op jit(solution)/shard_map/ppermute | solution.py:481
  187.2 42.9 %collective-permute-start.30 = (bf16[16,96,768]{2,1,0:T(8,128)(2,1)}, bf16[16,96,768]{2,1,0:T(8,128)(2,1)}, u32[]{:S(2)}, u32[]{:S(2)}) collective-permute-start(bf16[16,96,768]{2,1,0:T(8,128)(2,1)} %constant_dynamic-update-slice_fusion.46), channel_id=1, source_target_pairs={{0,2},{2,0},{4,6},{6,4},{8,10},{10,8},{12,14},{14,12},{16,18},{18,... | collective-permute-start | bytes 7077896 | tf_op jit(solution)/shard_map/ppermute | solution.py:481
  190.5 70.5 %collective-permute-start.20 = (bf16[2,16,48,768]{3,2,0,1:T(8,128)(2,1)}, bf16[2,16,48,768]{3,2,0,1:T(8,128)(2,1)}, u32[]{:S(2)}, u32[]{:S(2)}) collective-permute-start(bf16[2,16,48,768]{3,2,0,1:T(8,128)(2,1)} %constant_dynamic-update-slice_fusion.26), channel_id=1, source_target_pairs={{0,2},{2,0},{4,6},{6,4},{8,10},{10,8},{12,14},{14,12},{16,18},{18,... | collective-permute-start | bytes 7077896 | tf_op jit(solution)/shard_map/ppermute | solution.py:481
  212.5 52.2 %collective-permute-start.15 = (bf16[2,16,48,768]{3,2,0,1:T(8,128)(2,1)}, bf16[2,16,48,768]{3,2,0,1:T(8,128)(2,1)}, u32[]{:S(2)}, u32[]{:S(2)}) collective-permute-start(bf16[2,16,48,768]{3,2,0,1:T(8,128)(2,1)} %constant_dynamic-update-slice_fusion.21), channel_id=1, source_target_pairs={{0,2},{2,0},{4,6},{6,4},{8,10},{10,8},{12,14},{14,12},{16,18},{18,... | collective-permute-start | bytes 7077896 | tf_op jit(solution)/shard_map/ppermute | solution.py:481
  212.5 44.3 %collective-permute-start.25 = (bf16[16,96,768]{2,1,0:T(8,128)(2,1)}, bf16[16,96,768]{2,1,0:T(8,128)(2,1)}, u32[]{:S(2)}, u32[]{:S(2)}) collective-permute-start(bf16[16,96,768]{2,1,0:T(8,128)(2,1)} %constant_dynamic-update-slice_fusion.36), channel_id=1, source_target_pairs={{0,2},{2,0},{4,6},{6,4},{8,10},{10,8},{12,14},{14,12},{16,18},{18,... | collective-permute-start | bytes 7077896 | tf_op jit(solution)/shard_map/ppermute | solution.py:481
  213.0 54.9 %collective-permute-start.35 = (bf16[2,16,48,768]{3,2,0,1:T(8,128)(2,1)}, bf16[2,16,48,768]{3,2,0,1:T(8,128)(2,1)}, u32[]{:S(2)}, u32[]{:S(2)}) collective-permute-start(bf16[2,16,48,768]{3,2,0,1:T(8,128)(2,1)} %constant_dynamic-update-slice_fusion.51), channel_id=1, source_target_pairs={{0,2},{2,0},{4,6},{6,4},{8,10},{10,8},{12,14},{14,12},{16,18},{18,... | collective-permute-start | bytes 7077896 | tf_op jit(solution)/shard_map/ppermute | solution.py:481
  230.2 107.4 %collective-permute-start.40 = (bf16[2,16,48,768]{3,2,0,1:T(8,128)(2,1)}, bf16[2,16,48,768]{3,2,0,1:T(8,128)(2,1)}, u32[]{:S(2)}, u32[]{:S(2)}) collective-permute-start(bf16[2,16,48,768]{3,2,0,1:T(8,128)(2,1)} %copy-done.64), channel_id=1, source_target_pairs={{0,2},{2,0},{4,6},{6,4},{8,10},{10,8},{12,14},{14,12},{16,18},{18,... | collective-permute-start | bytes 7077896 | tf_op jit(solution)/shard_map/ppermute | solution.py:481
  526.2 84.6 %collective-permute-start.72 = (bf16[2,16,48,768]{3,2,0,1:T(8,128)(2,1)}, bf16[2,16,48,768]{3,2,0,1:T(8,128)(2,1)}, u32[]{:S(2)}, u32[]{:S(2)}) collective-permute-start(bf16[2,16,48,768]{3,2,0,1:T(8,128)(2,1)} %copy.77), channel_id=1, source_target_pairs={{0,2},{2,0},{4,6},{6,4},{8,10},{10,8},{12,14},{14,12},{16,18},{18,... | collective-permute-start | bytes 7077896 | tf_op jit(solution)/shard_map/ppermute | solution.py:481
  528.2 86.8 %collective-permute-start.77 = (bf16[2,16,48,768]{3,2,0,1:T(8,128)(2,1)}, bf16[2,16,48,768]{3,2,0,1:T(8,128)(2,1)}, u32[]{:S(2)}, u32[]{:S(2)}) collective-permute-start(bf16[2,16,48,768]{3,2,0,1:T(8,128)(2,1)} %copy.79), channel_id=1, source_target_pairs={{0,2},{2,0},{4,6},{6,4},{8,10},{10,8},{12,14},{14,12},{16,18},{18,... | collective-permute-start | bytes 7077896 | tf_op jit(solution)/shard_map/ppermute | solution.py:481
  530.4 78.6 %collective-permute-start.41 = (bf16[864,768]{1,0:T(8,128)(2,1)}, bf16[864,768]{1,0:T(8,128)(2,1)}, u32[]{:S(2)}, u32[]{:S(2)}) collective-permute-start(bf16[864,768]{1,0:T(8,128)(2,1)} %select_convert_fusion), channel_id=1, source_target_pairs={{0,16},{2,18},{4,20},{6,22},{8,24},{10,26},{12,28},{14,30},{16,0},... | collective-permute-start | bytes 3981320 | tf_op jit(solution)/shard_map/ppermute | solution.py:481
  547.1 74.8 %collective-permute-start.67 = (bf16[16,96,768]{2,1,0:T(8,128)(2,1)S(1)}, bf16[16,96,768]{2,1,0:T(8,128)(2,1)}, u32[]{:S(2)}, u32[]{:S(2)}) collective-permute-start(bf16[16,96,768]{2,1,0:T(8,128)(2,1)S(1)} %bitcast.202), channel_id=1, source_target_pairs={{0,2},{2,0},{4,6},{6,4},{8,10},{10,8},{12,14},{14,12},{16,18},{18,... | collective-permute-start | bytes 7077896 | tf_op jit(solution)/shard_map/ppermute | solution.py:481
  547.2 44.2 %collective-permute-start.61 = (f32[1,8,128]{2,1,0:T(8,128)S(1)}, f32[1,8,128]{2,1,0:T(8,128)S(1)}, u32[]{:S(2)}, u32[]{:S(2)}) collective-permute-start(f32[1,8,128]{2,1,0:T(8,128)S(1)} %slice.499), channel_id=1, source_target_pairs={{0,16},{2,18},{4,20},{6,22},{8,24},{10,26},{12,28},{14,30},{16,0},... | collective-permute-start | bytes 12296 | tf_op jit(solution)/shard_map/ppermute | solution.py:481
  591.4 34.8 %collective-permute-start.62 = (bf16[16,96,768]{2,1,0:T(8,128)(2,1)S(1)}, bf16[16,96,768]{2,1,0:T(8,128)(2,1)}, u32[]{:S(2)}, u32[]{:S(2)}) collective-permute-start(bf16[16,96,768]{2,1,0:T(8,128)(2,1)S(1)} %bitcast.204), channel_id=1, source_target_pairs={{0,2},{2,0},{4,6},{6,4},{8,10},{10,8},{12,14},{14,12},{16,18},{18,... | collective-permute-start | bytes 7077896 | tf_op jit(solution)/shard_map/ppermute | solution.py:481
  630.9 49.6 %collective-permute-start.63 = (bf16[8,96,768]{2,1,0:T(8,128)(2,1)S(1)}, bf16[8,96,768]{2,1,0:T(8,128)(2,1)S(1)}, u32[]{:S(2)}, u32[]{:S(2)}) collective-permute-start(bf16[8,96,768]{2,1,0:T(8,128)(2,1)S(1)} %slice.501), channel_id=1, source_target_pairs={{0,4},{2,6},{4,0},{6,2},{8,12},{10,14},{12,8},{14,10},{16,20},{18,... | collective-permute-start | bytes 3538952 | tf_op jit(solution)/shard_map/ppermute | solution.py:481
  634.3 46.7 %collective-permute-start.48 = (bf16[2,8,48,768]{3,2,0,1:T(8,128)(2,1)}, bf16[2,8,48,768]{3,2,0,1:T(8,128)(2,1)S(1)}, u32[]{:S(2)}, u32[]{:S(2)}) collective-permute-start(bf16[2,8,48,768]{3,2,0,1:T(8,128)(2,1)} %slice.475), channel_id=1, source_target_pairs={{0,1},{1,0},{2,3},{3,2},{4,5},{5,4},{6,7},{7,6},{8,9},{9,8},{10,11... | collective-permute-start | bytes 3538952 | tf_op jit(solution)/shard_map/ppermute | solution.py:479
  650.8 54.9 %collective-permute-start.53 = (bf16[2,8,48,768]{3,2,0,1:T(8,128)(2,1)S(1)}, bf16[2,8,48,768]{3,2,0,1:T(8,128)(2,1)S(1)}, u32[]{:S(2)}, u32[]{:S(2)}) collective-permute-start(bf16[2,8,48,768]{3,2,0,1:T(8,128)(2,1)S(1)} %slice.483), channel_id=1, source_target_pairs={{0,4},{2,6},{4,0},{6,2},{8,12},{10,14},{12,8},{14,10},{16,20},{18,... | collective-permute-start | bytes 3538952 | tf_op jit(solution)/shard_map/ppermute | solution.py:481
  655.2 51.1 %collective-permute-start.43 = (bf16[8,96,768]{2,1,0:T(8,128)(2,1)S(1)}, bf16[8,96,768]{2,1,0:T(8,128)(2,1)S(1)}, u32[]{:S(2)}, u32[]{:S(2)}) collective-permute-start(bf16[8,96,768]{2,1,0:T(8,128)(2,1)S(1)} %slice.465), channel_id=1, source_target_pairs={{0,8},{2,10},{4,12},{6,14},{8,0},{10,2},{12,4},{14,6},{16,24},{18,... | collective-permute-start | bytes 3538952 | tf_op jit(solution)/shard_map/ppermute | solution.py:481
  659.0 47.8 %collective-permute-start.74 = (bf16[2,4,48,768]{3,2,0,1:T(8,128)(2,1)S(1)}, bf16[2,4,48,768]{3,2,0,1:T(8,128)(2,1)S(1)}, u32[]{:S(2)}, u32[]{:S(2)}) collective-permute-start(bf16[2,4,48,768]{3,2,0,1:T(8,128)(2,1)S(1)} %slice.525), channel_id=1, source_target_pairs={{0,8},{2,10},{4,12},{6,14},{8,0},{10,2},{12,4},{14,6},{16,24},{18,... | collective-permute-start | bytes 1769480 | tf_op jit(solution)/shard_map/ppermute | solution.py:481
  681.0 37.4 %collective-permute-start.69 = (bf16[4,96,768]{2,1,0:T(8,128)(2,1)S(1)}, bf16[4,96,768]{2,1,0:T(8,128)(2,1)S(1)}, u32[]{:S(2)}, u32[]{:S(2)}) collective-permute-start(bf16[4,96,768]{2,1,0:T(8,128)(2,1)S(1)} %slice.513), channel_id=1, source_target_pairs={{0,4},{2,6},{4,0},{6,2},{8,12},{10,14},{12,8},{14,10},{16,20},{18,... | collective-permute-start | bytes 1769480 | tf_op jit(solution)/shard_map/ppermute | solution.py:481
  (132 other events, 2550.1 us)

commit v2 on v1

v2 whole, which is shorter than its diff:
```python
import functools

import jax
import jax.numpy as jnp
from jax import lax
from jax.experimental import pallas as pl
from jax.experimental.pallas import tpu as pltpu
from jax.sharding import PartitionSpec as P

HEADS = 12
SLOT = 36
PACK = 4
EPSILON = 1e-06
MASKED = -1000000000.0
APART = -1e30
BF = jnp.bfloat16
F32 = jnp.float32
VMEM_LIMIT = 48 * 1024 * 1024

NN = (((1,), (0,)), ((), ()))
NT = (((1,), (1,)), ((), ()))
TN = (((0,), (0,)), ((), ()))


def mm(left, right, dims):
    return lax.dot_general(left, right, dims, preferred_element_type=F32)


def norm_forward(total):
    center = total - jnp.mean(total, axis=-1, keepdims=True)
    spread = jnp.mean(center * center, axis=-1, keepdims=True)
    rate = lax.rsqrt(spread + EPSILON)
    return center * rate, rate


def norm_backward(grad, normed, rate, gain):
    slope = grad * gain
    first = jnp.mean(slope, axis=-1, keepdims=True)
    second = jnp.mean(slope * normed, axis=-1, keepdims=True)
    terms = grad * normed
    rows, width = terms.shape
    return rate * (slope - first - normed * second), jnp.sum(
        terms.reshape(rows // 8, 8, width), axis=0
    )


def gelu_pair(value):
    size = jnp.abs(value) * 0.7071067811865476
    t = 1.0 / (1.0 + 0.3275911 * size)
    bell = jnp.exp(-size * size)
    poly = t * (
        0.254829592
        + t * (-0.284496736 + t * (1.421413741 + t * (-1.453152027 + t * 1.061405429)))
    )
    tail = 0.5 * poly * bell
    phi = jnp.where(value >= 0.0, 1.0 - tail, tail)
    return value * phi, phi + value * bell * 0.3989422804014327


def head_masks(width, head):
    lane = lax.broadcasted_iota(jnp.int32, (1, width), 1)
    return [jnp.where(lane // head == i, 1.0, 0.0).astype(F32) for i in range(width // head)]


def spread_heads(block, masks):
    return jnp.concatenate([block * mask.astype(block.dtype) for mask in masks], axis=0)


def fold_heads(stacked, masks):
    rows = stacked.shape[0] // len(masks)
    total = stacked[:rows] * masks[0]
    for i in range(1, len(masks)):
        total = total + stacked[i * rows : (i + 1) * rows] * masks[i]
    return total


def attend_kernel(cross, x_ref, y_ref, p_ref, o_ref, g_ref, kb_ref, apart_ref,
                  out_ref, joined_ref, probs_ref, context_ref, normed_ref, rate_ref):
    x = x_ref[...]
    width = x.shape[1]
    head = width // HEADS
    quad = 4 * head
    scale = head ** (-0.5)
    if cross:
        joined_ref[:, :width] = mm(x, p_ref[:width], NT).astype(BF)
        joined_ref[:, width:] = mm(y_ref[...], p_ref[width:], NT).astype(BF)
    else:
        joined_ref[...] = mm(x, p_ref[...], NT).astype(BF)
    masks = head_masks(quad, head)
    group = PACK * SLOT
    for g in range(x.shape[0] // group):
        rows = slice(g * group, (g + 1) * group)
        bias = apart_ref[...] + kb_ref[rows]
        for i in range(width // quad):
            q = joined_ref[rows, i * quad : (i + 1) * quad]
            k = joined_ref[rows, width + i * quad : width + (i + 1) * quad]
            v = joined_ref[rows, 2 * width + i * quad : 2 * width + (i + 1) * quad]
            scores = mm(k, spread_heads(q, masks), NT) * scale + bias
            raised = jnp.exp(scores - jnp.max(scores, axis=0, keepdims=True))
            probs = (raised * (1.0 / jnp.sum(raised, axis=0, keepdims=True))).astype(BF)
            probs_ref[g, i] = probs
            context_ref[rows, i * quad : (i + 1) * quad] = fold_heads(mm(probs, v, TN), masks).astype(BF)
    total = x.astype(F32) + mm(context_ref[...], o_ref[...], NT)
    normed, rate = norm_forward(total)
    out_ref[...] = (normed * g_ref[...]).astype(BF)
    normed_ref[...] = normed.astype(BF)
    rate_ref[...] = rate


def whole(shape):
    return pl.BlockSpec(shape, lambda *_: (0,) * len(shape))


def in_vmem(shape):
    return pl.BlockSpec(shape, lambda: (0,) * len(shape))


def attention_block(x, y, project, output, gain, key_bias, apart, cross):
    rows, width = x.shape
    group = PACK * SLOT
    groups = rows // group
    steps = groups // 2 if groups % 2 == 0 else groups
    block = rows // steps
    quads = HEADS // 4
    probs_block = pl.BlockSpec((groups // steps, quads, group, 4 * group), lambda i: (i, 0, 0, 0))
    row = lambda w: pl.BlockSpec((block, w), lambda i: (i, 0))
    out, joined, probs, context, normed, rate = pl.pallas_call(
        functools.partial(attend_kernel, cross),
        grid=(steps,),
        in_specs=[
            row(width), row(width), whole(project.shape), whole(output.shape), whole((1, width)),
            row(1), whole(apart.shape),
        ],
        out_specs=[
            row(width), row(3 * width),
            probs_block,
            row(width), row(width), row(1),
        ],
        out_shape=[
            jax.ShapeDtypeStruct((rows, width), BF),
            jax.ShapeDtypeStruct((rows, 3 * width), BF),
            jax.ShapeDtypeStruct((groups, quads, group, 4 * group), BF),
            jax.ShapeDtypeStruct((rows, width), BF),
            jax.ShapeDtypeStruct((rows, width), BF),
            jax.ShapeDtypeStruct((rows, 1), F32),
        ],
        compiler_params=pltpu.CompilerParams(vmem_limit_bytes=VMEM_LIMIT),
        cost_estimate=pl.CostEstimate(
            flops=2 * rows * width * 6 * width, bytes_accessed=24 * rows * width, transcendentals=0
        ),
        name="attend",
    )(x, y, project, output, gain, key_bias, apart)
    return out, (joined, probs, context, normed, rate)


def attend_back_kernel(cross, grad_ref, normed_ref, rate_ref, g_ref, joined_ref, probs_ref, p_ref, o_ref,
                       *rest):
    if cross:
        side_ref, branch_ref, dj_ref, dx_ref, dy_ref, gain_ref = rest
    else:
        branch_ref, dj_ref, dx_ref, gain_ref = rest
    width = grad_ref.shape[1]
    head = width // HEADS
    quad = 4 * head
    scale = head ** (-0.5)
    total, terms = norm_backward(
        grad_ref[...].astype(F32), normed_ref[...].astype(F32), rate_ref[...], g_ref[...]
    )

    @pl.when(pl.program_id(0) == 0)
    def _():
        gain_ref[...] = jnp.zeros_like(gain_ref)

    gain_ref[...] += terms
    branch = total.astype(BF)
    branch_ref[...] = branch
    grad_context = mm(branch, o_ref[...], NN).astype(BF)
    masks = head_masks(quad, head)
    group = PACK * SLOT
    for g in range(grad_context.shape[0] // group):
        rows = slice(g * group, (g + 1) * group)
        for i in range(width // quad):
            low, high = i * quad, (i + 1) * quad
            q = joined_ref[rows, low:high]
            k = joined_ref[rows, width + low : width + high]
            v = joined_ref[rows, 2 * width + low : 2 * width + high]
            probs = probs_ref[g, i]
            wide = probs.astype(F32)
            grad_heads = spread_heads(grad_context[rows, low:high], masks)
            grad_probs = mm(v, grad_heads, NT)
            mean = jnp.sum(wide * grad_probs, axis=0, keepdims=True)
            grad_scores = (wide * (grad_probs - mean)).astype(BF)
            dj_ref[rows, low:high] = (fold_heads(mm(grad_scores, k, TN), masks) * scale).astype(BF)
            dj_ref[rows, width + low : width + high] = (
                mm(grad_scores, spread_heads(q, masks), NN) * scale
            ).astype(BF)
            dj_ref[rows, 2 * width + low : 2 * width + high] = mm(probs, grad_heads, NN).astype(BF)
    if cross:
        dx = total + mm(dj_ref[:, :width], p_ref[:width], NN)
        dy = mm(dj_ref[:, width:], p_ref[width:], NN)
        words = side_ref[0] == 1
        dx_ref[...] = jnp.where(words, dx, dy)
        dy_ref[...] = jnp.where(words, dy, dx)
    else:
        dx_ref[...] = total + mm(dj_ref[...], p_ref[...], NN)


def attention_block_backward(grad, project, output, gain, saved, side=None):
    cross = side is not None
    joined, probs, context, normed, rate = saved
    rows, width = normed.shape
    group = PACK * SLOT
    groups = rows // group
    steps = groups // 2 if groups % 2 == 0 else groups
    block = rows // steps
    quads = HEADS // 4
    probs_block = pl.BlockSpec((groups // steps, quads, group, 4 * group), lambda i: (i, 0, 0, 0))
    row = lambda w: pl.BlockSpec((block, w), lambda i: (i, 0))
    extra_spec = [row(width)] if cross else []
    extra_shape = [jax.ShapeDtypeStruct((rows, width), F32)] if cross else []
    return pl.pallas_call(
        functools.partial(attend_back_kernel, cross),
        grid=(steps,),
        in_specs=[
            row(width), row(width), row(1), whole((1, width)), row(3 * width),
            probs_block,
            whole(project.shape), whole(output.shape),
        ]
        + [pl.BlockSpec(memory_space=pltpu.SMEM)] * cross,
        out_specs=[row(width), row(3 * width), row(width)] + extra_spec + [whole((8, width))],
        out_shape=[
            jax.ShapeDtypeStruct((rows, width), BF),
            jax.ShapeDtypeStruct((rows, 3 * width), BF),
            jax.ShapeDtypeStruct((rows, width), F32),
        ]
        + extra_shape
        + [jax.ShapeDtypeStruct((8, width), F32)],
        compiler_params=pltpu.CompilerParams(vmem_limit_bytes=VMEM_LIMIT),
        cost_estimate=pl.CostEstimate(
            flops=2 * rows * width * 7 * width, bytes_accessed=32 * rows * width, transcendentals=0
        ),
        name="attend_back",
    )(grad, normed, rate, gain, joined, probs, project, output, *([side] if cross else []))


def attend_weights_kernel(parts, extra, *refs):
    tables, (dj_ref, x_ref, y_ref, branch_ref, context_ref) = refs[:parts], refs[parts : parts + 5]
    extra_ref = refs[parts + 5] if extra else None
    outputs, total = refs[parts + 5 + extra : -1], refs[-1]
    width = x_ref.shape[1]
    total[:width] = mm(dj_ref[:, :width], x_ref[...], TN)
    total[width : 3 * width] = mm(dj_ref[:, width:], y_ref[...], TN)
    total[3 * width :] = mm(branch_ref[...], context_ref[...], TN)
    for part in range(parts):
        mine_ref, theirs_ref = outputs[2 * part : 2 * part + 2]
        count = mine_ref.shape[0]
        unit = width // (2 * count)
        first, last = part * 4 * unit // parts, (part + 1) * 4 * unit // parts

        def take(i, carry):
            for target, offset in ((mine_ref, 0), (theirs_ref, count)):
                at = tables[part][offset + i]
                filled = 0
                for start, size, base in ((0, 3 * unit, 0), (3 * unit, unit, 3 * width)):
                    low, high = max(first, start), min(last, start + size)
                    if low < high:
                        row = pl.multiple_of(base + at * size + low - start, 8)
                        block = total[pl.ds(row, high - low)].reshape(-1, 8, width)
                        target[i, filled : filled + block.shape[0]] = block.astype(BF)
                        filled += block.shape[0]
                if extra and part == 0:
                    target[i, filled] = extra_ref[at].astype(BF)
            return carry

        lax.fori_loop(0, count, take, 0)


def attention_weights(tables, dj, x, y, branch, context, extra=None):
    rows, width = x.shape
    count = tables[0].shape[0] // 2
    unit = width // (2 * count)
    parts = len(tables)
    units = 4 * unit // 8 // parts
    if unit % 8:
        project = jnp.concatenate([mm(dj[:, :width], x, TN), mm(dj[:, width:], y, TN)], axis=0)
        project = project.astype(BF).reshape(2 * count, 3 * unit, width)
        output = mm(branch, context, TN).astype(BF).reshape(2 * count, unit, width)
        joined = jnp.concatenate([project, output], axis=1).reshape(2 * count, units * parts, 8, width)
        pairs = []
        for part, table in enumerate(tables):
            piece = joined[:, part * units : (part + 1) * units]
            if extra is not None and part == 0:
                piece = jnp.concatenate([piece, extra[:, None].astype(BF)], axis=1)
            piece = piece[table]
            pairs.append((piece[:count], piece[count:]))
        return pairs
    more = [] if extra is None else [extra]
    shapes = [(count, units + (len(more) if part == 0 else 0), 8, width) for part in range(parts) for _ in (0, 1)]
    outputs = pl.pallas_call(
        functools.partial(attend_weights_kernel, parts, len(more)),
        in_specs=[pl.BlockSpec(memory_space=pltpu.SMEM)] * parts
        + [in_vmem(a.shape) for a in (dj, x, y, branch, context, *more)],
        out_specs=[in_vmem(shape) for shape in shapes],
        out_shape=[jax.ShapeDtypeStruct(shape, BF) for shape in shapes],
        scratch_shapes=[pltpu.VMEM((4 * width, width), F32)],
        compiler_params=pltpu.CompilerParams(vmem_limit_bytes=VMEM_LIMIT),
        cost_estimate=pl.CostEstimate(
            flops=2 * rows * width * 4 * width, bytes_accessed=16 * rows * width, transcendentals=0
        ),
        name="attend_weights",
    )(*tables, dj, x, y, branch, context, *more)
    return [tuple(outputs[2 * part : 2 * part + 2]) for part in range(parts)]


def flat(block):
    return block.reshape(-1, block.shape[-1])


def feed_operands(weight, unit, steps):
    pieces, _, width = weight.shape
    if unit % 16 == 0:
        block = (pieces // steps, unit, width)
        return [weight, weight], [
            pl.BlockSpec(block, lambda s: (s % steps, 0, 0)),
            pl.BlockSpec(block, lambda s: (s % steps, 1, 0)),
        ]
    arrays = [weight[:, i * unit : (i + 1) * unit].reshape(steps, -1, width) for i in (0, 1)]
    return arrays, [pl.BlockSpec((1,) + arrays[0].shape[1:], lambda s: (s % steps, 0, 0))] * 2


def feed_kernel(x_ref, *refs):
    weights, (g_ref, out_ref, hidden_ref, slope_ref, normed_ref, rate_ref) = refs[:8], refs[8:]
    x = x_ref[...]
    wide = weights[0].shape[0] * weights[0].shape[1]
    total = x.astype(F32)
    for i in range(4):
        hidden, slope = gelu_pair(mm(x, flat(weights[2 * i][...]), NT))
        hidden = hidden.astype(BF)
        hidden_ref[:, i * wide : (i + 1) * wide] = hidden
        slope_ref[:, i * wide : (i + 1) * wide] = slope.astype(BF)
        total = total + mm(hidden, flat(weights[2 * i + 1][...]), NN)
    normed, rate = norm_forward(total)
    out_ref[...] = (normed * g_ref[...]).astype(BF)
    normed_ref[...] = normed.astype(BF)
    rate_ref[...] = rate


def feed_block(x, weights, unit, gain):
    rows, width = x.shape
    hidden = weights[0].shape[0] * unit * len(weights)
    parts = [feed_operands(weight, unit, 1) for weight in weights]
    block = rows // 3
    row = lambda w: pl.BlockSpec((block, w), lambda i: (i, 0))
    out, *saved = pl.pallas_call(
        feed_kernel,
        grid=(rows // block,),
        in_specs=[row(width)] + [spec for _, specs in parts for spec in specs] + [whole((1, width))],
        out_specs=[row(width), row(hidden), row(hidden), row(width), row(1)],
        out_shape=[
            jax.ShapeDtypeStruct((rows, width), BF),
            jax.ShapeDtypeStruct((rows, hidden), BF),
            jax.ShapeDtypeStruct((rows, hidden), BF),
            jax.ShapeDtypeStruct((rows, width), BF),
            jax.ShapeDtypeStruct((rows, 1), F32),
        ],
        compiler_params=pltpu.CompilerParams(vmem_limit_bytes=VMEM_LIMIT),
        cost_estimate=pl.CostEstimate(
            flops=4 * rows * width * hidden, bytes_accessed=4 * (rows + width) * hidden, transcendentals=0
        ),
        name="feed",
    )(x, *[array for arrays, _ in parts for array in arrays], gain)
    return out, tuple(saved)


def feed_back_kernel(first, *refs):
    if first:
        grad_ref, normed_ref, rate_ref, g_ref, x_ref, *refs = refs
        inputs, (branch_ref, gain_ref, *outputs) = refs[:8], refs[8:]
    else:
        start_ref, branch_ref, x_ref, *refs = refs
        inputs, outputs = refs[:8], refs[8:]
    dx_ref = outputs[-1]

    @pl.when(pl.program_id(0) == 0)
    def _():
        if first:
            total, gain_ref[...] = norm_backward(
                grad_ref[...].astype(F32), normed_ref[...].astype(F32), rate_ref[...], g_ref[...]
            )
            dx_ref[...] = total
            branch_ref[...] = total.astype(BF)
        else:
            dx_ref[...] = start_ref[...]

    branch = branch_ref[...]
    x = x_ref[...]
    for i in range(2):
        up_ref, down_ref, hidden_ref, slope_ref = inputs[4 * i : 4 * i + 4]
        grad_ref = outputs[i]
        pieces, _, unit, width = grad_ref.shape
        grad_hidden = mm(branch, flat(down_ref[...]), NT)
        grad_raised = (grad_hidden * slope_ref[...].astype(F32)).astype(BF)
        grad_ref[:, 0] = mm(grad_raised, x, TN).astype(BF).reshape(pieces, unit, width)
        grad_ref[:, 1] = mm(hidden_ref[...], branch, TN).astype(BF).reshape(pieces, unit, width)
        dx_ref[...] += mm(grad_raised, flat(up_ref[...]), NN)


def feed_back(start, x, weights, unit, hidden, slope, quarter):
    rows, width = x.shape
    first = len(start) == 4
    pieces = weights[0].shape[0]
    steps = 2 if pieces * unit // 2 % 128 == 0 else 1
    tile = pieces * unit // steps
    specs = [whole(a.shape) for a in (*start, x)]
    operands = [*start, x]
    cut = pl.BlockSpec((pieces // steps, 2, unit, width), lambda s: (s, 0, 0, 0))
    for i, weight in enumerate(weights):
        columns = pl.BlockSpec((rows, tile), lambda s, base=(quarter + i) * steps: (0, base + s))
        arrays, blocks = feed_operands(weight, unit, steps)
        specs += [*blocks, columns, columns]
        operands += [*arrays, hidden, slope]
    out_specs = [cut, cut, whole((rows, width))]
    out_shape = [jax.ShapeDtypeStruct((pieces, 2, unit, width), BF)] * 2
    out_shape += [jax.ShapeDtypeStruct((rows, width), F32)]
    if first:
        out_specs = [whole((rows, width)), whole((8, width))] + out_specs
        out_shape = [jax.ShapeDtypeStruct((rows, width), BF), jax.ShapeDtypeStruct((8, width), F32)] + out_shape
    return pl.pallas_call(
        functools.partial(feed_back_kernel, first),
        grid=(steps,),
        in_specs=specs,
        out_specs=out_specs,
        out_shape=out_shape,
        compiler_params=pltpu.CompilerParams(vmem_limit_bytes=VMEM_LIMIT),
        cost_estimate=pl.CostEstimate(
            flops=16 * rows * width * pieces * unit, bytes_accessed=30 * pieces * unit * width, transcendentals=0
        ),
        name="feed_back",
    )(*operands)


def place_kernel(parts, rows, extra, *refs):
    tables, sources, (p_ref, o_ref, *more) = refs[:parts], refs[parts : 3 * parts], refs[3 * parts :]
    count = sources[0].shape[0]
    unit = o_ref.shape[1]

    def put(device, carry):
        found = []
        for part in range(parts):
            mine_ref, theirs_ref = sources[2 * part : 2 * part + 2]
            at = tables[part][device]
            mine = mine_ref[jnp.minimum(at, count - 1)].astype(F32)
            theirs = theirs_ref[jnp.maximum(at - count, 0)].astype(F32)
            found.append(jnp.where(at < count, mine, theirs))
        piece = found[0] if parts == 1 else jnp.concatenate(found, axis=0)
        p_ref[device] = piece[: 3 * unit].astype(BF)
        o_ref[device] = piece[3 * unit : 4 * unit].astype(BF)
        if extra:
            more[0][device] = piece[4 * unit :]
        return carry

    lax.fori_loop(0, 2 * count, put, 0)


def place_weights(tables, pairs, skip, extra=0):
    parts = len(pairs)
    count, _, width = pairs[0][0].shape
    unit = width // (2 * count)
    rows = 4 * unit // parts + extra
    places = [jnp.argsort(table) for table in tables]
    if unit % 8:
        pieces = [
            jnp.concatenate(pair, axis=0)[place, skip : skip + rows]
            for pair, place, skip in zip(pairs, places, skip)
        ]
        joined = jnp.concatenate(pieces, axis=1)
        made = [joined[:, : 3 * unit], joined[:, 3 * unit : 4 * unit], joined[:, 4 * unit :].astype(F32)]
    else:
        shapes = [(2 * count, 3 * unit, width), (2 * count, unit, width)] + [(2 * count, extra, width)] * (extra > 0)
        specs = []
        for offset in skip:
            block = pl.BlockSpec((count, rows, width), lambda i, at=offset // rows: (0, at, 0))
            specs += [block, block]
        made = pl.pallas_call(
            functools.partial(place_kernel, parts, rows, extra),
            grid=(1,),
            in_specs=[pl.BlockSpec(memory_space=pltpu.SMEM)] * parts + specs,
            out_specs=[whole(shape) for shape in shapes],
            out_shape=[jax.ShapeDtypeStruct(shape, F32 if i == 2 else BF) for i, shape in enumerate(shapes)],
            compiler_params=pltpu.CompilerParams(vmem_limit_bytes=VMEM_LIMIT),
            cost_estimate=pl.CostEstimate(flops=0, bytes_accessed=16 * width * width, transcendentals=0),
            name="place",
        )(*places, *[piece for pair in pairs for piece in pair])
    project, output = made[0].reshape(-1, width), made[1].reshape(-1, width)
    return (project, output, made[2]) if extra else (project, output)


class Cube:
    def __init__(self):
        self.replicas = lax.axis_size("dp")
        self.streams = lax.axis_size("stream")
        low = self.replicas.bit_length() - 1
        bits = low + self.streams.bit_length() - 1
        self.half = bits - 1
        self.core = low
        self.inner = [b for b in range(bits) if b not in (self.half, self.core)]
        self.number = lax.axis_index("stream") * self.replicas + lax.axis_index("dp")

    def swap(self, value, bit):
        step = 1 << bit
        if step < self.replicas:
            return lax.ppermute(value, "dp", [(i, i ^ step) for i in range(self.replicas)])
        step //= self.replicas
        return lax.ppermute(value, "stream", [(i, i ^ step) for i in range(self.streams)])

    def order(self, turn):
        turn %= len(self.inner)
        return self.inner[turn:] + self.inner[:turn]

    def pieces(self, stages):
        order = stages[::-1]
        relative = [
            sum(1 << bit for place, bit in enumerate(order) if i >> place & 1) for i in range(1 << len(order))
        ]
        return self.number ^ jnp.array(relative, jnp.int32)

    def table(self, order):
        return self.pieces([self.core] + order[::-1] + [self.half])


def after(value, *others):
    return lax.optimization_barrier((value,) + others)[0]


class Gather:
    def __init__(self, cube, own, other, order):
        self.cube, self.pieces = cube, own
        self.stages = [cube.half] + order + [cube.core]
        self.sent, self.got, self.done = other, None, 0

    def advance(self, *others):
        if self.done:
            pieces, got = self.pieces, self.got
            if others:
                pieces, got, *_ = lax.optimization_barrier((pieces, got, *others))
            self.sent = self.pieces = jnp.concatenate([pieces, got], axis=0)
        elif others:
            self.sent = after(self.sent, *others)
        self.got = self.cube.swap(self.sent, self.stages[self.done])
        self.done += 1

    def pair(self):
        return self.pieces, self.got


class Scatter:
    def __init__(self, cube, keep, send, order):
        self.cube = cube
        self.stages = [cube.core] + order[::-1] + [cube.half]
        self.kept, self.sent, self.got, self.done = keep, send, None, 0

    def advance(self, *others):
        if self.done:
            kept, got = self.kept, self.got
            if others:
                kept, got, *_ = lax.optimization_barrier((kept, got, *others))
            if self.done == len(self.stages):
                self.kept, self.got, self.sent = kept, got, got
                return
            count = kept.shape[0] // 2
            self.sent = add(kept[count:], got[count:])
            self.kept = add(kept[:count], got[:count])
        self.got = self.cube.swap(self.sent, self.stages[self.done])
        self.done += 1

    def finish(self, *others):
        while self.done < len(self.stages):
            self.advance()
        self.advance(*others)
        return self.kept.astype(F32), self.got.astype(F32)


def beside(value, *chains):
    for chain in chains:
        chain.advance(value)
    return after(value, *[chain.sent for chain in chains])


def add(left, right):
    return (left.astype(F32) + right.astype(F32)).astype(left.dtype)


def on_device(
    states,
    cotangent,
    word_lengths,
    object_project,
    object_output,
    object_up,
    object_down,
    object_gains,
    cross_project,
    cross_output,
    words_project,
    words_output,
    region_project,
    region_output,
    words_up,
    words_down,
    region_up,
    region_down,
    layer_gains,
):
    cube = Cube()
    width = states.shape[1]
    half = cube.streams // 2
    position = lax.axis_index("stream")
    is_words = position < half
    count = states.shape[0] // SLOT
    block = position % half * cube.replicas + lax.axis_index("dp")
    lengths = lax.dynamic_slice_in_dim(word_lengths, block * count, count)
    key_bias = jnp.where(jnp.arange(SLOT)[None, :] < lengths[:, None], 0.0, MASKED).reshape(-1, 1)
    no_bias = jnp.zeros_like(key_bias)
    self_bias = jnp.where(is_words, key_bias, no_bias)
    cross_bias = jnp.where(is_words, no_bias, key_bias)
    packed = PACK * SLOT
    keys = lax.broadcasted_iota(jnp.int32, (packed, 4 * packed), 0) // SLOT
    queries = lax.broadcasted_iota(jnp.int32, (packed, 4 * packed), 1) % packed // SLOT
    apart = jnp.where(keys == queries, 0.0, APART).astype(F32)

    unit = object_output.shape[1]
    feed_unit = object_down.shape[0] // 2

    def attention_shard(project, output):
        return [project.T, output.T]

    def feed_shards(up, down):
        up = up.T
        return [up[:feed_unit], down[:feed_unit]], [up[feed_unit:], down[feed_unit:]]

    def piece(rows):
        return jnp.concatenate(rows, axis=0)[None]

    gain_shard = jnp.concatenate([object_gains, layer_gains], axis=0)
    kinds, span = gain_shard.shape
    gain_rows = jnp.pad(gain_shard, ((0, 8 - kinds), (0, width - span)))
    object_shards = [
        attention_shard(object_project, object_output) + [gain_rows],
        *feed_shards(object_up, object_down),
    ]
    cross_rows = jnp.concatenate(attention_shard(cross_project, cross_output), axis=0)
    third = cross_rows.shape[0] // 3
    cross_shards = [cross_rows[i * third : (i + 1) * third] for i in range(3)]
    words_shards = [attention_shard(words_project, words_output), *feed_shards(words_up, words_down)]
    region_shards = [attention_shard(region_project, region_output), *feed_shards(region_up, region_down)]

    orders = [cube.order(turn) for turn in (1, 0, 2)]
    tables = [cube.table(order) for order in orders]
    first = [Gather(cube, piece(rows), piece(rows), order) for rows, order in zip(object_shards, orders)]
    second = []
    for words, region, cross, order in zip(words_shards, region_shards, cross_shards, orders):
        own = piece([jnp.where(is_words, w, r) for w, r in zip(words, region)] + [cross])
        other = piece([jnp.where(is_words, r, w) for w, r in zip(words, region)] + [cross])
        second.append(Gather(cube, own, other, order))

    def step(chains, *others):
        for chain in chains:
            chain.advance(*others)
        return [chain.got for chain in chains]

    for chain, mark in zip(second, step(first)):
        chain.advance(mark)
    marks = [chain.got for chain in second]
    others = cube.swap(after(states, *marks), cube.half)
    step(first)
    step(first)
    for _ in cube.inner[2:]:
        marks = step(first, *marks)
    later = step(first)
    step(second, *marks)
    for _ in cube.inner[2:]:
        step(second, *later)

    object_in, object_out, gain_pieces = place_weights(tables[:1], [first[0].pair()], [0], 8)
    object_feed = [part for chain in first[1:] for part in chain.pair()]
    gains = gain_pieces[:, :kinds, :span].transpose(1, 0, 2).reshape(kinds, width)
    self_gain = jnp.where(is_words, gains[3], gains[4])[None]
    feed_gain = jnp.where(is_words, gains[5], gains[6])[None]

    language = jnp.where(is_words, states, others)
    vision = jnp.where(is_words, others, states)

    ready = beside(vision, *second)
    one, one_saved = attention_block(
        ready, ready, object_in, object_out, gains[0:1], no_bias, apart, False
    )
    two, two_saved = feed_block(one, object_feed, feed_unit, gains[1:2])
    x = beside(jnp.where(is_words, language, two), *second)
    pairs = [chain.pair() for chain in second]
    cross_in, cross_out = place_weights(tables, pairs, [pairs[0][0].shape[1] - third] * 3)
    y = jnp.where(is_words, two, language)
    three, three_saved = attention_block(x, y, cross_in, cross_out, gains[2:3], cross_bias, apart, True)
    self_in, self_out = place_weights(tables[:1], pairs[:1], [0])
    self_feed = [part for pair in pairs[1:] for part in pair]
    four, four_saved = attention_block(
        three, three, self_in, self_out, self_gain, self_bias, apart, False
    )
    five, five_saved = feed_block(four, self_feed, feed_unit, feed_gain)

    side = is_words.astype(jnp.int32)[None]

    hidden, slope, normed, rate = five_saved
    branch, feed_terms, *pair, middle = feed_back(
        (cotangent, normed, rate, feed_gain), four, self_feed[:2], feed_unit, hidden, slope, 0
    )
    sb = Scatter(cube, *pair, orders[1])
    *pair, grad_four = feed_back((beside(middle, sb), branch), four, self_feed[2:], feed_unit, hidden, slope, 2)
    sc = Scatter(cube, *pair, orders[2])

    branch, dj, grad_three, self_terms = attention_block_backward(
        beside(grad_four, sb, sc), self_in, self_out, self_gain, four_saved
    )
    (pair,) = attention_weights(tables[:1], beside(dj, sc), three, three, branch, four_saved[2])
    sa = Scatter(cube, *pair, orders[0])

    branch, dj, grad_language, grad_two, cross_terms = attention_block_backward(
        beside(grad_three, sa, sb), cross_in, cross_out, gains[2:3], three_saved, side
    )
    (pair,) = attention_weights(tables[:1], beside(dj, sa, sc, sb), x, y, branch, three_saved[2])
    xa = Scatter(cube, *pair, orders[0])

    hidden, slope, normed, rate = two_saved
    branch, two_terms, *pair, middle = feed_back(
        (beside(grad_two, xa, sb, sc), normed, rate, gains[1:2]), one, object_feed[:2], feed_unit, hidden, slope, 0
    )
    ob = Scatter(cube, *pair, orders[1])
    *pair, grad_one = feed_back(
        (beside(middle, ob, sa, sb, sc, xa), branch), one, object_feed[2:], feed_unit, hidden, slope, 2
    )
    oc = Scatter(cube, *pair, orders[2])
    branch, dj, grad_vision, one_terms = attention_block_backward(
        beside(grad_one, oc, ob, sa, sc, xa), object_in, object_out, gains[0:1], one_saved
    )
    words_side = is_words.astype(F32)
    region_side = 1.0 - words_side
    sums = [one_terms, two_terms, cross_terms, self_terms, self_terms, feed_terms, feed_terms]
    sides = [1.0, 1.0, 1.0, words_side, region_side, words_side, region_side]
    gain_sums = jnp.stack([jnp.sum(s, axis=0) * side for s, side in zip(sums, sides)])
    gain_cut = gain_sums.reshape(kinds, -1, span).transpose(1, 0, 2)
    gain_cut = jnp.pad(gain_cut, ((0, 0), (0, 8 - kinds), (0, width - span)))
    *others, last = cube.inner
    orders = [[last] + others, [last] + others[::-1], [last] + others]
    tables = [cube.table(order) for order in orders]
    pairs = attention_weights(
        tables, beside(dj, ob, oc, sa, xa), ready, ready, branch, one_saved[2], gain_cut
    )
    oas = [Scatter(cube, *pair, order) for pair, order in zip(pairs, orders)]
    step(oas)
    step([oc])
    step(oas)
    step([ob])
    step(oas)
    step([oc])
    last = step(oas)
    sent = jnp.where(is_words, grad_vision, grad_language).astype(BF)
    received = after(cube.swap(sent, cube.half), *last).astype(F32)
    grad_states = jnp.where(is_words, grad_language, grad_vision) + received

    def both(chain):
        own, other = chain.finish(*last)
        return own + other

    def apart_by_stream(chain):
        own, other = chain.finish(*last)
        return jnp.where(is_words, own, other), jnp.where(is_words, other, own)

    def attention_grads(piece):
        rows = flat(piece)
        return rows[: 3 * unit].T, rows[3 * unit : 4 * unit].T

    def feed_grads(first, second):
        joined = jnp.concatenate([first, second], axis=2)
        return joined[0, 0].T, joined[0, 1]

    object_parts = [both(chain) for chain in oas]
    more = object_parts[0].shape[1] - 1
    gain_grad = object_parts[0][0, more, :kinds, :span]
    object_piece = jnp.concatenate([object_parts[0][:, :more], *object_parts[1:]], axis=1)
    object_project_grad, object_output_grad = attention_grads(object_piece)
    object_up_grad, object_down_grad = feed_grads(both(ob), both(oc))
    cross_project_grad, cross_output_grad = attention_grads(both(xa))
    words_piece, region_piece = apart_by_stream(sa)
    words_project_grad, words_output_grad = attention_grads(words_piece)
    region_project_grad, region_output_grad = attention_grads(region_piece)
    split = [apart_by_stream(s) for s in (sb, sc)]
    words_up_grad, words_down_grad = feed_grads(split[0][0], split[1][0])
    region_up_grad, region_down_grad = feed_grads(split[0][1], split[1][1])
    return (
        five,
        grad_states,
        object_project_grad,
        object_output_grad,
        object_up_grad,
        object_down_grad,
        gain_grad[:2],
        cross_project_grad,
        cross_output_grad,
        words_project_grad,
        words_output_grad,
        region_project_grad,
        region_output_grad,
        words_up_grad,
        words_down_grad,
        region_up_grad,
        region_down_grad,
        gain_grad[2:],
    )


def solution(mesh):
    rows = P(("stream", "dp"), None)
    columns = P(None, ("stream", "dp"))
    in_specs = (
        rows, rows, P(),
        columns, columns, columns, rows, columns,
        columns, columns,
        columns, columns, columns, columns,
        columns, rows, columns, rows,
        columns,
    )
    out_specs = (
        rows, rows,
        columns, columns, columns, rows, columns,
        columns, columns,
        columns, columns, columns, columns,
        columns, rows, columns, rows,
        columns,
    )
    return jax.shard_map(
        on_device, mesh=mesh, in_specs=in_specs, out_specs=out_specs, check_vma=False
    )
```

time: 797 us -> 671 us (0.84)
  local copies, waits for them, and re-layouts: 99 us -> 48.6 us
  waiting for transfers between devices: 245 us -> 212 us
  Pallas kernels: 294 us -> 264 us
  other arithmetic: 61 us -> 53 us
    ppermute x66 -> x62, waiting for transfers between devices: 195 us -> 162 us  [swap(): lax.ppermute(value, 'stream', [(i, i ^ step) for i in range(self.streams)])]
    pallas_call x21 -> x16, Pallas kernels: 252 us -> 221 us  [the longest x4 70.2 us: feed_back(): pl.pallas_call(functools.partial(feed_back_kernel, first), grid=(steps,),...]
    unnamed x200 -> x148, local copies, waits for them, and re-layouts: 43.6 us -> 18.2 us
    convert_element_type x28 -> x36, other arithmetic: 15.1 us -> 33 us  [add(): return (left.astype(F32) + right.astype(F32)).astype(left.dtype)]
    concatenate x26 -> x10, other arithmetic: 16.2 us -> 1.38 us  [the longest x1 0.79 us: on_device(): gain_shard = jnp.concatenate([object_gains, layer_gains], axis=0)]
    ppermute x4 -> x0, local copies, waits for them, and re-layouts: 14.6 us -> none  [swap(): lax.ppermute(value, 'stream', [(i, i ^ step) for i in range(self.streams)])]
    reshape x4 -> x0, local copies, waits for them, and re-layouts: 10.2 us -> none  [scatter_feed(): cut = lambda a: a.reshape(2, pieces, -1, width)]
    unnamed x6 -> x0, other arithmetic: 8.02 us -> none
  transfers between devices with their start and end apart: 82 -> 77, of which waited for: 28 -> 29; matrix products, arithmetic and copies ran while one was open for 16% -> 13% of each run, Pallas kernels for 17% -> 27%
where the time goes in v2:
time: 671 us; the launch traced here: 666 us
  Pallas kernels  264 us (39%)
  waiting for transfers between devices  212 us (32%)
  starting transfers between devices  86.1 us (13%)
  other arithmetic  53 us (8%)
  local copies, waits for them, and re-layouts  48.6 us (7%)
    ppermute x62, waiting for transfers between devices, swap(): lax.ppermute(value, 'stream', [(i, i ^ step) for i in range(self.streams)])  162 us
    pallas_call x4, Pallas kernels, feed_back(): pl.pallas_call(functools.partial(feed_back_kernel, first), grid=(steps,),...  70.2 us
    ppermute x62, starting transfers between devices, swap(): lax.ppermute(value, 'stream', [(i, i ^ step) for i in range(self.streams)])  66.5 us
    pallas_call x3, Pallas kernels, attention_block_backward(): pl.pallas_call(functools.partial(attend_back_kernel, cross), grid=(steps,...  57.6 us
    ppermute x15, waiting for transfers between devices, swap(): lax.ppermute(value, 'dp', [(i, i ^ step) for i in range(self.replicas)])  49.9 us
    pallas_call x3, Pallas kernels, attention_block(): pl.pallas_call(functools.partial(attend_kernel, cross), grid=(steps,), in...  46.6 us
    pallas_call x2, Pallas kernels, feed_block(): pl.pallas_call(feed_kernel, grid=(rows // block,), in_specs=[row(width)]...  43.4 us
    convert_element_type x36, other arithmetic, add(): return (left.astype(F32) + right.astype(F32)).astype(left.dtype)  33 us
  transfers between devices with their start and end apart: 77, of which 29 were waited for; matrix products, arithmetic and copies ran while one was open for 13% of the time, Pallas kernels for 27%

profile of v2, /device:TPU:0, one launch (start us, length us, event | category | flops | bytes accessed | tf_op | source)
XLA Modules:
  0.0 666.4 jit_solution(15686216225789283209)
XLA Ops:
  11.8 9.5 %collective-permute-done = bf16[1,104,768]{2,1,0:T(8,128)(2,1)S(1)} collective-permute-done((bf16[1,104,768]{2,1,0:T(8,128)(2,1)S(1)}, bf16[1,104,768]{2,1,0:T(8,128)(2,1)S(1)}, u32[]{:S(2)}, u32[]{:S(2)}) %collective-permute-start) | collective-permute-done | bytes 159776 | tf_op jit(solution)/shard_map/ppermute | solution.py:514
  44.3 8.6 %collective-permute-done.3 = bf16[1,128,768]{2,1,0:T(8,128)(2,1)S(1)} collective-permute-done((bf16[1,128,768]{2,1,0:T(8,128)(2,1)S(1)}, bf16[1,128,768]{2,1,0:T(8,128)(2,1)S(1)}, u32[]{:S(2)}, u32[]{:S(2)}) %collective-permute-start.3) | collective-permute-done | bytes 196640 | tf_op jit(solution)/shard_map/ppermute | solution.py:514
  57.1 11.0 %collective-permute-done.1 = bf16[1,128,768]{2,1,0:T(8,128)(2,1)S(1)} collective-permute-done((bf16[1,128,768]{2,1,0:T(8,128)(2,1)S(1)}, bf16[1,128,768]{2,1,0:T(8,128)(2,1)S(1)}, u32[]{:S(2)}, u32[]{:S(2)}) %collective-permute-start.1) | collective-permute-done | bytes 196640 | tf_op jit(solution)/shard_map/ppermute | solution.py:514
  75.3 23.0 %collective-permute-done.9 = bf16[8,104,768]{2,1,0:T(8,128)(2,1)S(1)} collective-permute-done((bf16[8,104,768]{2,1,0:T(8,128)(2,1)S(1)}, bf16[8,104,768]{2,1,0:T(8,128)(2,1)S(1)}, u32[]{:S(2)}, u32[]{:S(2)}) %collective-permute-start.9) | collective-permute-done | bytes 1277984 | tf_op jit(solution)/shard_map/ppermute | solution.py:512
  105.8 8.9 %collective-permute-done.16 = bf16[2,128,768]{2,1,0:T(8,128)(2,1)S(1)} collective-permute-done((bf16[2,128,768]{2,1,0:T(8,128)(2,1)S(1)}, bf16[2,128,768]{2,1,0:T(8,128)(2,1)S(1)}, u32[]{:S(2)}, u32[]{:S(2)}) %collective-permute-start.16) | collective-permute-done | bytes 393248 | tf_op jit(solution)/shard_map/ppermute | solution.py:514
  128.5 12.8 %collective-permute-done.23 = bf16[2,128,768]{2,1,0:T(8,128)(2,1)S(1)} collective-permute-done((bf16[2,128,768]{2,1,0:T(8,128)(2,1)S(1)}, bf16[2,128,768]{2,1,0:T(8,128)(2,1)S(1)}, u32[]{:S(2)}, u32[]{:S(2)}) %collective-permute-start.23) | collective-permute-done | bytes 393248 | tf_op jit(solution)/shard_map/ppermute | solution.py:514
  144.3 18.8 %collective-permute-done.6 = bf16[864,768]{1,0:T(8,128)(2,1)S(1)} collective-permute-done((bf16[864,768]{1,0:T(8,128)(2,1)}, bf16[864,768]{1,0:T(8,128)(2,1)S(1)}, u32[]{:S(2)}, u32[]{:S(2)}) %collective-permute-start.6) | collective-permute-done | bytes 1327136 | tf_op jit(solution)/shard_map/ppermute | solution.py:514
  182.5 15.5 %attend.3 = (bf16[864,768]{1,0:T(8,128)(2,1)S(1)}, bf16[864,2304]{1,0:T(8,128)(2,1)}, bf16[6,3,144,576]{3,2,1,0:T(8,128)(2,1)}, bf16[864,768]{1,0:T(8,128)(2,1)S...) custom-call(bf16[864,768]{1,0:T(8,128)(2,1)} %broadcast_select_fusion.2.x_ref.y_ref.refs_4_.refs_5_, ...), custom_call_target="tpu_custom_call" | custom-call | flops 6115295232 | bytes 15925248 | tf_op jit(solution)/shard_map/attend/pallas_call | solution.py:127
  199.8 21.7 %feed.2 = (bf16[864,768]{1,0:T(8,128)(2,1)S(1)}, bf16[864,3072]{1,0:T(8,128)(2,1)}, bf16[864,3072]{1,0:T(8,128)(2,1)}, bf16[864,768]{1,0:T(8,128)(2,1)S(1)}, f32[864,1]{1,0:T(8,128)S(1)}) custom-call(bf16[864,768]{1,0:T(8,128)(2,1)S(1)} %get-tuple-element.232.x_ref.refs_4_.refs_2_, ...), custom_call_target="tpu_custom_call" | custom-call | flops 8153726976 | bytes 20054016 | tf_op jit(solution)/shard_map/feed/pallas_call | solution.py:354
  243.8 5.4 place.4
  249.2 15.8 %attend.4 = (bf16[864,768]{1,0:T(8,128)(2,1)S(1)}, bf16[864,2304]{1,0:T(8,128)(2,1)}, bf16[6,3,144,576]{3,2,1,0:T(8,128)(2,1)}, bf16[864,768]{1,0:T(8,128)(2,1)S...) custom-call(bf16[864,768]{1,0:T(8,128)(2,1)} %get-tuple-element.240.x_ref.refs_2_, ...), custom_call_target="tpu_custom_call" | custom-call | flops 6115295232 | bytes 15925248 | tf_op jit(solution)/shard_map/attend/pallas_call | solution.py:127
  265.0 6.0 place.5
  271.1 15.4 %attend.5 = (bf16[864,768]{1,0:T(8,128)(2,1)S(1)}, bf16[864,2304]{1,0:T(8,128)(2,1)}, bf16[6,3,144,576]{3,2,1,0:T(8,128)(2,1)}, bf16[864,768]{1,0:T(8,128)(2,1)S...) custom-call(bf16[864,768]{1,0:T(8,128)(2,1)} %copy-done.22, bf16[864,768]{1,0:T(8,128)(2,1)} %copy-done.22, ...), custom_call_target="tpu_custom_call" | custom-call | flops 6115295232 | bytes 15925248 | tf_op jit(solution)/shard_map/attend/pallas_call | solution.py:127
  286.5 21.7 %feed.3 = (bf16[864,768]{1,0:T(8,128)(2,1)}, bf16[864,3072]{1,0:T(8,128)(2,1)}, bf16[864,3072]{1,0:T(8,128)(2,1)}, bf16[864,768]{1,0:T(8,128)(2,1)S(1)}, f32[864,1]{1,0:T(8,128)S(1)}) custom-call(bf16[864,768]{1,0:T(8,128)(2,1)S(1)} %get-tuple-element.248.x_ref.refs_4_.refs_2_, ...), custom_call_target="tpu_custom_call" | custom-call | flops 8153726976 | bytes 20054016 | tf_op jit(solution)/shard_map/feed/pallas_call | solution.py:354
  308.2 17.4 %feed_back.4 = (bf16[864,768]{1,0:T(8,128)(2,1)S(1)}, f32[8,768]{1,0:T(8,128)S(1)}, bf16[16,2,48,768]{3,2,1,0:T(8,128)(2,1)}, bf16[16,2,48,768]{3,2,1,0:T(8,128)(2,1)}, f32[864,768]{1,0:T(8,128)}) custom-call(bf16[864,768]{1,0:T(8,128)(2,1)S(1)} %copy-done.4, bf16[864,768]{1,0:T(8,128)(2,1)S(1)} %get-tuple-element.250.refs_1_, ...), custom_call_target="tpu_custom_call" | custom-call | flops 8153726976 | bytes 17694720 | tf_op jit(solution)/shard_map/feed_back/pallas_call | solution.py:428
  326.2 17.2 %feed_back.5 = (bf16[16,2,48,768]{3,2,1,0:T(8,128)(2,1)S(1)}, bf16[16,2,48,768]{3,2,1,0:T(8,128)(2,1)}, f32[864,768]{1,0:T(8,128)}) custom-call(f32[864,768]{1,0:T(8,128)} %get-tuple-element.256.refs_0_, bf16[864,768]{1,0:T(8,128)(2,1)S(1)} %get-tuple-element.257.refs_1_, bf16[864,768]{1,0:T(8,128)(2,1)S(1)} %get-tuple-element.248.x_ref.refs_4_.refs_2_, ...), custom_call_target="tpu_custom_call" | custom-call | flops 8153726976 | bytes 17694720 | tf_op jit(solution)/shard_map/feed_back/pallas_call | solution.py:428
  347.6 18.9 %attend_back.3 = (bf16[864,768]{1,0:T(8,128)(2,1)S(1)}, bf16[864,2304]{1,0:T(8,128)(2,1)}, f32[864,768]{1,0:T(8,128)}, f32[8,768]{1,0:T(8,128)S(1)}) custom-call(f32[864,768]{1,0:T(8,128)} %get-tuple-element.263.grad_ref, bf16[864,768]{1,0:T(8,128)(2,1)S(1)} %copy-done.26, f32[864,1]{1,0:T(8,128)S(1)} %get-tuple-element.265.rate_ref, ...), custom_call_target="tpu_custom_call" | custom-call | flops 7134511104 | bytes 21233664 | tf_op jit(solution)/shard_map/attend_back/pallas_call | solution.py:221
  368.8 10.0 %attend_weights.3 = (bf16[16,12,8,768]{3,2,1,0:T(8,128)(2,1)}, bf16[16,12,8,768]{3,2,1,0:T(8,128)(2,1)}) custom-call(s32[32]{0:T(128)S(1)} %broadcast_xor_fusion.3.refs_0_, bf16[864,2304]{1,0:T(8,128)(2,1)} %get-tuple-element.273.refs_1_, bf16[864,768]{1,0:T(8,128)(2,1)S(1)} %copy-done.23, bf16[864,768]{1,0:T(8,128)(2,1)S(1)} %copy-done.23, ...), custom_call_target="tpu_custom_call" | custom-call | flops 4076863488 | bytes 10616832 | tf_op jit(solution)/shard_map/attend_weights/pallas_call | solution.py:299
  383.1 19.8 %attend_back.4 = (bf16[864,768]{1,0:T(8,128)(2,1)S(1)}, bf16[864,2304]{1,0:T(8,128)(2,1)}, f32[864,768]{1,0:T(8,128)}, f32[864,768]{1,0:T(8,128)}, f32[8,768]{1,0:T(8,128)S(1)}) custom-call(f32[864,768]{1,0:T(8,128)} %get-tuple-element.279.grad_ref, bf16[864,768]{1,0:T(8,128)(2,1)S(1)} %copy-done.24, f32[864,1]{1,0:T(8,128)S(1)} %copy-done.28, ...), custom_call_target="tpu_custom_call" | custom-call | flops 7134511104 | bytes 21233664 | tf_op jit(solution)/shard_map/attend_back/pallas_call | solution.py:221
  411.3 8.7 %collective-permute-done.36 = bf16[4,2,48,768]{3,2,1,0:T(8,128)(2,1)S(1)} collective-permute-done((bf16[4,2,48,768]{3,2,1,0:T(8,128)(2,1)S(1)}, bf16[4,2,48,768]{3,2,1,0:T(8,128)(2,1)S(1)}, u32[]{:S(2)}, u32[]{:S(2)}) %collective-permute-start.36) | collective-permute-done | bytes 589856 | tf_op jit(solution)/shard_map/ppermute | solution.py:514
  428.5 10.1 %attend_weights.4 = (bf16[16,12,8,768]{3,2,1,0:T(8,128)(2,1)}, bf16[16,12,8,768]{3,2,1,0:T(8,128)(2,1)}) custom-call(s32[32]{0:T(128)S(1)} %broadcast_xor_fusion.3.refs_0_, bf16[864,2304]{1,0:T(8,128)(2,1)} %get-tuple-element.294.refs_1_, bf16[864,768]{1,0:T(8,128)(2,1)S(1)} %copy-done.8, bf16[864,768]{1,0:T(8,128)(2,1)S(1)} %copy-done.7, ...), custom_call_target="tpu_custom_call" | custom-call | flops 4076863488 | bytes 10616832 | tf_op jit(solution)/shard_map/attend_weights/pallas_call | solution.py:299
  441.0 18.6 %feed_back.6 = (bf16[864,768]{1,0:T(8,128)(2,1)S(1)}, f32[8,768]{1,0:T(8,128)S(1)}, bf16[16,2,48,768]{3,2,1,0:T(8,128)(2,1)}, bf16[16,2,48,768]{3,2,1,0:T(8,128)(2,1)}, f32[864,768]{1,0:T(8,128)}) custom-call(f32[864,768]{1,0:T(8,128)} %get-tuple-element.302.refs_0_, bf16[864,768]{1,0:T(8,128)(2,1)S(1)} %copy-done.6, f32[864,1]{1,0:T(8,128)S(1)} %copy-done.10, ...), custom_call_target="tpu_custom_call" | custom-call | flops 8153726976 | bytes 17694720 | tf_op jit(solution)/shard_map/feed_back/pallas_call | solution.py:428
  462.3 7.9 %collective-permute-done.40 = bf16[1,2,48,768]{3,2,1,0:T(8,128)(2,1)} collective-permute-done((bf16[1,2,48,768]{3,2,1,0:T(8,128)(2,1)}, bf16[1,2,48,768]{3,2,1,0:T(8,128)(2,1)}, u32[]{:S(2)}, u32[]{:S(2)}) %collective-permute-start.40) | collective-permute-done | bytes 147488 | tf_op jit(solution)/shard_map/ppermute | solution.py:514
  481.8 17.0 %feed_back.7 = (bf16[16,2,48,768]{3,2,1,0:T(8,128)(2,1)S(1)}, bf16[16,2,48,768]{3,2,1,0:T(8,128)(2,1)}, f32[864,768]{1,0:T(8,128)}) custom-call(f32[864,768]{1,0:T(8,128)} %get-tuple-element.317.refs_0_, bf16[864,768]{1,0:T(8,128)(2,1)S(1)} %get-tuple-element.318.refs_1_, bf16[864,768]{1,0:T(8,128)(2,1)S(1)} %copy-done.1, ...), custom_call_target="tpu_custom_call" | custom-call | flops 8153726976 | bytes 17694720 | tf_op jit(solution)/shard_map/feed_back/pallas_call | solution.py:428
  510.0 18.9 %attend_back.5 = (bf16[864,768]{1,0:T(8,128)(2,1)S(1)}, bf16[864,2304]{1,0:T(8,128)(2,1)}, f32[864,768]{1,0:T(8,128)}, f32[8,768]{1,0:T(8,128)S(1)}) custom-call(f32[864,768]{1,0:T(8,128)} %get-tuple-element.329.grad_ref, bf16[864,768]{1,0:T(8,128)(2,1)S(1)} %copy-done.25, f32[864,1]{1,0:T(8,128)S(1)} %copy-done.30, f32[1,768]{1,0:T(1,128)S(1)} %slice.619.g_ref, ...), custom_call_target="tpu_custom_call" | custom-call | flops 7134511104 | bytes 21233664 | tf_op jit(solution)/shard_map/attend_back/pallas_call | solution.py:221
  538.3 6.2 collective-permute-done.51
  551.2 9.8 %attend_weights.5 = (bf16[16,5,8,768]{3,2,1,0:T(8,128)(2,1)S(1)}, bf16[16,5,8,768]{3,2,1,0:T(8,128)(2,1)S(1)}, bf16[16,4,8,768]{3,2,1,0:T(8,128)(2,1)S(1)}, bf16...) custom-call(s32[32]{0:T(128)S(1)} %broadcast_xor_fusion.1.refs_0_.refs_2_, ...), custom_call_target="tpu_custom_call" | custom-call | flops 4076863488 | bytes 10616832 | tf_op jit(solution)/shard_map/attend_weights/pallas_call | solution.py:299
  568.1 8.4 %collective-permute-done.57 = bf16[8,4,8,768]{3,2,1,0:T(8,128)(2,1)S(1)} collective-permute-done((bf16[8,4,8,768]{3,2,1,0:T(8,128)(2,1)S(1)}, bf16[8,4,8,768]{3,2,1,0:T(8,128)(2,1)S(1)}, u32[]{:S(2)}, u32[]{:S(2)}) %collective-permute-start.57) | collective-permute-done | bytes 393248 | tf_op jit(solution)/shard_map/ppermute | solution.py:512
  577.7 23.3 %collective-permute-done.61 = bf16[8,4,8,768]{3,2,1,0:T(8,128)(2,1)S(1)} collective-permute-done((bf16[8,4,8,768]{3,2,1,0:T(8,128)(2,1)S(1)}, bf16[8,4,8,768]{3,2,1,0:T(8,128)(2,1)S(1)}, u32[]{:S(2)}, u32[]{:S(2)}) %collective-permute-start.61) | collective-permute-done | bytes 393248 | tf_op jit(solution)/shard_map/ppermute | solution.py:514
  604.1 10.8 %collective-permute-done.58 = bf16[4,4,8,768]{3,2,1,0:T(8,128)(2,1)S(1)} collective-permute-done((bf16[4,4,8,768]{3,2,1,0:T(8,128)(2,1)S(1)}, bf16[4,4,8,768]{3,2,1,0:T(8,128)(2,1)S(1)}, u32[]{:S(2)}, u32[]{:S(2)}) %collective-permute-start.58) | collective-permute-done | bytes 196640 | tf_op jit(solution)/shard_map/ppermute | solution.py:514
  618.5 8.8 %collective-permute-done.63 = bf16[2,4,8,768]{3,2,1,0:T(8,128)(2,1)S(1)} collective-permute-done((bf16[2,4,8,768]{3,2,1,0:T(8,128)(2,1)S(1)}, bf16[2,4,8,768]{3,2,1,0:T(8,128)(2,1)S(1)}, u32[]{:S(2)}, u32[]{:S(2)}) %collective-permute-start.63) | collective-permute-done | bytes 98336 | tf_op jit(solution)/shard_map/ppermute | solution.py:514
  628.5 6.6 collective-permute-done.54
  (429 shorter events, 231.9 us)
Async XLA Ops:
  29.3 38.8 %collective-permute-start.8 = (bf16[4,104,768]{2,1,0:T(8,128)(2,1)S(1)}, bf16[4,104,768]{2,1,0:T(8,128)(2,1)S(1)}, u32[]{:S(2)}, u32[]{:S(2)}) collective-permute-start(bf16[4,104,768]{2,1,0:T(8,128)(2,1)S(1)} %pad_maximum_fusion.3), channel_id=1, source_target_pairs={{0,8},{2,10},{4,12},{6,14},{8,0},{10,2},{12,4},{14,6},{16,24},{18,... | collective-permute-start | bytes 1916936 | tf_op jit(solution)/shard_map/ppermute | solution.py:514
  34.4 35.4 %collective-permute-start.11 = (bf16[4,96,768]{2,1,0:T(8,128)(2,1)S(1)}, bf16[4,96,768]{2,1,0:T(8,128)(2,1)S(1)}, u32[]{:S(2)}, u32[]{:S(2)}) collective-permute-start(bf16[4,96,768]{2,1,0:T(8,128)(2,1)S(1)} %pad_maximum_fusion.4), channel_id=1, source_target_pairs={{0,4},{2,6},{4,0},{6,2},{8,12},{10,14},{12,8},{14,10},{16,20},{18,... | collective-permute-start | bytes 1769480 | tf_op jit(solution)/shard_map/ppermute | solution.py:514
  41.1 28.9 %collective-permute-start.14 = (bf16[4,96,768]{2,1,0:T(8,128)(2,1)S(1)}, bf16[4,96,768]{2,1,0:T(8,128)(2,1)S(1)}, u32[]{:S(2)}, u32[]{:S(2)}) collective-permute-start(bf16[4,96,768]{2,1,0:T(8,128)(2,1)S(1)} %pad_maximum_fusion.5), channel_id=1, source_target_pairs={{0,1},{1,0},{2,3},{3,2},{4,5},{5,4},{6,7},{7,6},{8,9},{9,8},{10,11... | collective-permute-start | bytes 1769480 | tf_op jit(solution)/shard_map/ppermute | solution.py:512
  68.3 30.1 %collective-permute-start.9 = (bf16[8,104,768]{2,1,0:T(8,128)(2,1)S(1)}, bf16[8,104,768]{2,1,0:T(8,128)(2,1)S(1)}, u32[]{:S(2)}, u32[]{:S(2)}) collective-permute-start(bf16[8,104,768]{2,1,0:T(8,128)(2,1)S(1)} %pad_maximum_fusion), channel_id=1, source_target_pairs={{0,1},{1,0},{2,3},{3,2},{4,5},{5,4},{6,7},{7,6},{8,9},{9,8},{10,11... | collective-permute-start | bytes 3833864 | tf_op jit(solution)/shard_map/ppermute | solution.py:512
  69.9 28.5 %collective-permute-start.12 = (bf16[8,96,768]{2,1,0:T(8,128)(2,1)S(1)}, bf16[8,96,768]{2,1,0:T(8,128)(2,1)S(1)}, u32[]{:S(2)}, u32[]{:S(2)}) collective-permute-start(bf16[8,96,768]{2,1,0:T(8,128)(2,1)S(1)} %pad_maximum_fusion.1), channel_id=1, source_target_pairs={{0,8},{2,10},{4,12},{6,14},{8,0},{10,2},{12,4},{14,6},{16,24},{18,... | collective-permute-start | bytes 3538952 | tf_op jit(solution)/shard_map/ppermute | solution.py:514
  70.1 30.0 %collective-permute-start.15 = (bf16[8,96,768]{2,1,0:T(8,128)(2,1)S(1)}, bf16[8,96,768]{2,1,0:T(8,128)(2,1)S(1)}, u32[]{:S(2)}, u32[]{:S(2)}) collective-permute-start(bf16[8,96,768]{2,1,0:T(8,128)(2,1)S(1)} %pad_maximum_fusion.2), channel_id=1, source_target_pairs={{0,4},{2,6},{4,0},{6,2},{8,12},{10,14},{12,8},{14,10},{16,20},{18,... | collective-permute-start | bytes 3538952 | tf_op jit(solution)/shard_map/ppermute | solution.py:514
  103.0 60.1 %collective-permute-start.6 = (bf16[864,768]{1,0:T(8,128)(2,1)}, bf16[864,768]{1,0:T(8,128)(2,1)S(1)}, u32[]{:S(2)}, u32[]{:S(2)}) collective-permute-start(bf16[864,768]{1,0:T(8,128)(2,1)} %param.25), channel_id=1, source_target_pairs={{0,16},{2,18},{4,20},{6,22},{8,24},{10,26},{12,28},{14,30},{16,0},... | collective-permute-start | bytes 3981320 | tf_op jit(solution)/shard_map/ppermute | solution.py:514
  119.8 53.2 %collective-permute-start.20 = (bf16[4,128,768]{2,1,0:T(8,128)(2,1)}, bf16[4,128,768]{2,1,0:T(8,128)(2,1)}, u32[]{:S(2)}, u32[]{:S(2)}) collective-permute-start(bf16[4,128,768]{2,1,0:T(8,128)(2,1)} %constant_dynamic-update-slice_fusion.11), channel_id=1, source_target_pairs={{0,8},{2,10},{4,12},{6,14},{8,0},{10,2},{12,4},{14,6},{16,24},{18,... | collective-permute-start | bytes 2359304 | tf_op jit(solution)/shard_map/ppermute | solution.py:514
  127.0 46.0 %collective-permute-start.22 = (bf16[4,128,768]{2,1,0:T(8,128)(2,1)}, bf16[4,128,768]{2,1,0:T(8,128)(2,1)}, u32[]{:S(2)}, u32[]{:S(2)}) collective-permute-start(bf16[4,128,768]{2,1,0:T(8,128)(2,1)} %constant_dynamic-update-slice_fusion.17), channel_id=1, source_target_pairs={{0,4},{2,6},{4,0},{6,2},{8,12},{10,14},{12,8},{14,10},{16,20},{18,... | collective-permute-start | bytes 2359304 | tf_op jit(solution)/shard_map/ppermute | solution.py:514
  142.8 32.6 %collective-permute-start.24 = (bf16[4,128,768]{2,1,0:T(8,128)(2,1)}, bf16[4,128,768]{2,1,0:T(8,128)(2,1)}, u32[]{:S(2)}, u32[]{:S(2)}) collective-permute-start(bf16[4,128,768]{2,1,0:T(8,128)(2,1)} %constant_dynamic-update-slice_fusion.23), channel_id=1, source_target_pairs={{0,1},{1,0},{2,3},{3,2},{4,5},{5,4},{6,7},{7,6},{8,9},{9,8},{10,11... | collective-permute-start | bytes 2359304 | tf_op jit(solution)/shard_map/ppermute | solution.py:512
  177.8 45.8 %collective-permute-start.25 = (bf16[8,128,768]{2,1,0:T(8,128)(2,1)S(1)}, bf16[8,128,768]{2,1,0:T(8,128)(2,1)S(1)}, u32[]{:S(2)}, u32[]{:S(2)}) collective-permute-start(bf16[8,128,768]{2,1,0:T(8,128)(2,1)S(1)} %constant_dynamic-update-slice_fusion.13), channel_id=1, source_target_pairs={{0,1},{1,0},{2,3},{3,2},{4,5},{5,4},{6,7},{7,6},{8,9},{9,8},{10,11... | collective-permute-start | bytes 4718600 | tf_op jit(solution)/shard_map/ppermute | solution.py:512
  179.6 45.2 %collective-permute-start.26 = (bf16[8,128,768]{2,1,0:T(8,128)(2,1)S(1)}, bf16[8,128,768]{2,1,0:T(8,128)(2,1)}, u32[]{:S(2)}, u32[]{:S(2)}) collective-permute-start(bf16[8,128,768]{2,1,0:T(8,128)(2,1)S(1)} %constant_dynamic-update-slice_fusion.19), channel_id=1, source_target_pairs={{0,8},{2,10},{4,12},{6,14},{8,0},{10,2},{12,4},{14,6},{16,24},{18,... | collective-permute-start | bytes 4718600 | tf_op jit(solution)/shard_map/ppermute | solution.py:514
  180.8 45.3 %collective-permute-start.27 = (bf16[8,128,768]{2,1,0:T(8,128)(2,1)S(1)}, bf16[8,128,768]{2,1,0:T(8,128)(2,1)}, u32[]{:S(2)}, u32[]{:S(2)}) collective-permute-start(bf16[8,128,768]{2,1,0:T(8,128)(2,1)S(1)} %constant_dynamic-update-slice_fusion.25), channel_id=1, source_target_pairs={{0,4},{2,6},{4,0},{6,2},{8,12},{10,14},{12,8},{14,10},{16,20},{18,... | collective-permute-start | bytes 4718600 | tf_op jit(solution)/shard_map/ppermute | solution.py:514
  345.6 33.8 %collective-permute-start.33 = (bf16[8,2,48,768]{3,2,1,0:T(8,128)(2,1)}, bf16[8,2,48,768]{3,2,1,0:T(8,128)(2,1)}, u32[]{:S(2)}, u32[]{:S(2)}) collective-permute-start(bf16[8,2,48,768]{3,2,1,0:T(8,128)(2,1)} %get-tuple-element.396), channel_id=1, source_target_pairs={{0,8},{2,10},{4,12},{6,14},{8,0},{10,2},{12,4},{14,6},{16,24},{18,... | collective-permute-start | bytes 3538952 | tf_op jit(solution)/shard_map/ppermute | solution.py:514
  378.7 46.8 %collective-permute-start.34 = (bf16[16,12,8,768]{3,2,1,0:T(8,128)(2,1)}, bf16[16,12,8,768]{3,2,1,0:T(8,128)(2,1)S(1)}, u32[]{:S(2)}, u32[]{:S(2)}) collective-permute-start(bf16[16,12,8,768]{3,2,1,0:T(8,128)(2,1)} %get-tuple-element.276), channel_id=1, source_target_pairs={{0,2},{2,0},{4,6},{6,4},{8,10},{10,8},{12,14},{14,12},{16,18},{18,... | collective-permute-start | bytes 7077896 | tf_op jit(solution)/shard_map/ppermute | solution.py:514
  378.9 29.1 %collective-permute-start.35 = (bf16[8,2,48,768]{3,2,1,0:T(8,128)(2,1)}, bf16[8,2,48,768]{3,2,1,0:T(8,128)(2,1)}, u32[]{:S(2)}, u32[]{:S(2)}) collective-permute-start(bf16[8,2,48,768]{3,2,1,0:T(8,128)(2,1)} %get-tuple-element.394), channel_id=1, source_target_pairs={{0,4},{2,6},{4,0},{6,2},{8,12},{10,14},{12,8},{14,10},{16,20},{18,... | collective-permute-start | bytes 3538952 | tf_op jit(solution)/shard_map/ppermute | solution.py:514
  381.5 38.5 %collective-permute-start.36 = (bf16[4,2,48,768]{3,2,1,0:T(8,128)(2,1)S(1)}, bf16[4,2,48,768]{3,2,1,0:T(8,128)(2,1)S(1)}, u32[]{:S(2)}, u32[]{:S(2)}) collective-permute-start(bf16[4,2,48,768]{3,2,1,0:T(8,128)(2,1)S(1)} %get-tuple-element.410), channel_id=1, source_target_pairs={{0,4},{2,6},{4,0},{6,2},{8,12},{10,14},{12,8},{14,10},{16,20},{18,... | collective-permute-start | bytes 1769480 | tf_op jit(solution)/shard_map/ppermute | solution.py:514
  438.6 39.9 %collective-permute-start.42 = (bf16[16,12,8,768]{3,2,1,0:T(8,128)(2,1)}, bf16[16,12,8,768]{3,2,1,0:T(8,128)(2,1)}, u32[]{:S(2)}, u32[]{:S(2)}) collective-permute-start(bf16[16,12,8,768]{3,2,1,0:T(8,128)(2,1)} %get-tuple-element.297), channel_id=1, source_target_pairs={{0,2},{2,0},{4,6},{6,4},{8,10},{10,8},{12,14},{14,12},{16,18},{18,... | collective-permute-start | bytes 7077896 | tf_op jit(solution)/shard_map/ppermute | solution.py:514
  439.5 35.7 %collective-permute-start.39 = (bf16[8,12,8,768]{3,2,1,0:T(8,128)(2,1)}, bf16[8,12,8,768]{3,2,1,0:T(8,128)(2,1)}, u32[]{:S(2)}, u32[]{:S(2)}) collective-permute-start(bf16[8,12,8,768]{3,2,1,0:T(8,128)(2,1)} %get-tuple-element.392), channel_id=1, source_target_pairs={{0,1},{1,0},{2,3},{3,2},{4,5},{5,4},{6,7},{7,6},{8,9},{9,8},{10,11... | collective-permute-start | bytes 3538952 | tf_op jit(solution)/shard_map/ppermute | solution.py:512
  459.6 39.2 %collective-permute-start.43 = (bf16[16,2,48,768]{3,2,1,0:T(8,128)(2,1)}, bf16[16,2,48,768]{3,2,1,0:T(8,128)(2,1)}, u32[]{:S(2)}, u32[]{:S(2)}) collective-permute-start(bf16[16,2,48,768]{3,2,1,0:T(8,128)(2,1)} %get-tuple-element.308), channel_id=1, source_target_pairs={{0,2},{2,0},{4,6},{6,4},{8,10},{10,8},{12,14},{14,12},{16,18},{18,... | collective-permute-start | bytes 7077896 | tf_op jit(solution)/shard_map/ppermute | solution.py:514
  474.1 24.8 %collective-permute-start.45 = (bf16[1,2,48,768]{3,2,1,0:T(8,128)(2,1)S(1)}, bf16[1,2,48,768]{3,2,1,0:T(8,128)(2,1)S(1)}, u32[]{:S(2)}, u32[]{:S(2)}) collective-permute-start(bf16[1,2,48,768]{3,2,1,0:T(8,128)(2,1)S(1)} %get-tuple-element.450), channel_id=1, source_target_pairs={{0,16},{2,18},{4,20},{6,22},{8,24},{10,26},{12,28},{14,30},{16,0},... | collective-permute-start | bytes 442376 | tf_op jit(solution)/shard_map/ppermute | solution.py:514
  480.9 26.9 %collective-permute-start.46 = (bf16[8,12,8,768]{3,2,1,0:T(8,128)(2,1)S(1)}, bf16[8,12,8,768]{3,2,1,0:T(8,128)(2,1)S(1)}, u32[]{:S(2)}, u32[]{:S(2)}) collective-permute-start(bf16[8,12,8,768]{3,2,1,0:T(8,128)(2,1)S(1)} %get-tuple-element.390), channel_id=1, source_target_pairs={{0,1},{1,0},{2,3},{3,2},{4,5},{5,4},{6,7},{7,6},{8,9},{9,8},{10,11... | collective-permute-start | bytes 3538952 | tf_op jit(solution)/shard_map/ppermute | solution.py:512
  502.1 29.0 %collective-permute-start.48 = (bf16[8,2,48,768]{3,2,1,0:T(8,128)(2,1)S(1)}, bf16[8,2,48,768]{3,2,1,0:T(8,128)(2,1)S(1)}, u32[]{:S(2)}, u32[]{:S(2)}) collective-permute-start(bf16[8,2,48,768]{3,2,1,0:T(8,128)(2,1)S(1)} %get-tuple-element.388), channel_id=1, source_target_pairs={{0,8},{2,10},{4,12},{6,14},{8,0},{10,2},{12,4},{14,6},{16,24},{18,... | collective-permute-start | bytes 3538952 | tf_op jit(solution)/shard_map/ppermute | solution.py:514
  503.0 46.5 %collective-permute-start.49 = (bf16[16,2,48,768]{3,2,1,0:T(8,128)(2,1)}, bf16[16,2,48,768]{3,2,1,0:T(8,128)(2,1)S(1)}, u32[]{:S(2)}, u32[]{:S(2)}) collective-permute-start(bf16[16,2,48,768]{3,2,1,0:T(8,128)(2,1)} %get-tuple-element.320), channel_id=1, source_target_pairs={{0,2},{2,0},{4,6},{6,4},{8,10},{10,8},{12,14},{14,12},{16,18},{18,... | collective-permute-start | bytes 7077896 | tf_op jit(solution)/shard_map/ppermute | solution.py:514
  503.8 29.6 %collective-permute-start.50 = (bf16[2,12,8,768]{3,2,1,0:T(8,128)(2,1)}, bf16[2,12,8,768]{3,2,1,0:T(8,128)(2,1)}, u32[]{:S(2)}, u32[]{:S(2)}) collective-permute-start(bf16[2,12,8,768]{3,2,1,0:T(8,128)(2,1)} %get-tuple-element.424), channel_id=1, source_target_pairs={{0,4},{2,6},{4,0},{6,2},{8,12},{10,14},{12,8},{14,10},{16,20},{18,... | collective-permute-start | bytes 884744 | tf_op jit(solution)/shard_map/ppermute | solution.py:514
  508.9 35.6 %collective-permute-start.51 = (bf16[4,12,8,768]{3,2,1,0:T(8,128)(2,1)}, bf16[4,12,8,768]{3,2,1,0:T(8,128)(2,1)}, u32[]{:S(2)}, u32[]{:S(2)}) collective-permute-start(bf16[4,12,8,768]{3,2,1,0:T(8,128)(2,1)} %get-tuple-element.404), channel_id=1, source_target_pairs={{0,8},{2,10},{4,12},{6,14},{8,0},{10,2},{12,4},{14,6},{16,24},{18,... | collective-permute-start | bytes 1769480 | tf_op jit(solution)/shard_map/ppermute | solution.py:514
  537.1 110.1 %collective-permute-start.76 = (bf16[1,12,8,768]{3,2,1,0:T(8,128)(2,1)}, bf16[1,12,8,768]{3,2,1,0:T(8,128)(2,1)}, u32[]{:S(2)}, u32[]{:S(2)}) collective-permute-start(bf16[1,12,8,768]{3,2,1,0:T(8,128)(2,1)} %get-tuple-element.440), channel_id=1, source_target_pairs={{0,16},{2,18},{4,20},{6,22},{8,24},{10,26},{12,28},{14,30},{16,0},... | collective-permute-start | bytes 442376 | tf_op jit(solution)/shard_map/ppermute | solution.py:514
  562.2 75.8 %collective-permute-start.47 = (bf16[864,768]{1,0:T(8,128)(2,1)S(1)}, bf16[864,768]{1,0:T(8,128)(2,1)S(1)}, u32[]{:S(2)}, u32[]{:S(2)}) collective-permute-start(bf16[864,768]{1,0:T(8,128)(2,1)S(1)} %select_convert_fusion), channel_id=1, source_target_pairs={{0,16},{2,18},{4,20},{6,22},{8,24},{10,26},{12,28},{14,30},{16,0},... | collective-permute-start | bytes 3981320 | tf_op jit(solution)/shard_map/ppermute | solution.py:514
  563.7 39.0 %collective-permute-start.70 = (bf16[8,2,48,768]{3,2,1,0:T(8,128)(2,1)S(1)}, bf16[8,2,48,768]{3,2,1,0:T(8,128)(2,1)S(1)}, u32[]{:S(2)}, u32[]{:S(2)}) collective-permute-start(bf16[8,2,48,768]{3,2,1,0:T(8,128)(2,1)S(1)} %copy-done.45), channel_id=1, source_target_pairs={{0,4},{2,6},{4,0},{6,2},{8,12},{10,14},{12,8},{14,10},{16,20},{18,... | collective-permute-start | bytes 3538952 | tf_op jit(solution)/shard_map/ppermute | solution.py:514
  566.9 34.1 %collective-permute-start.61 = (bf16[8,4,8,768]{3,2,1,0:T(8,128)(2,1)S(1)}, bf16[8,4,8,768]{3,2,1,0:T(8,128)(2,1)S(1)}, u32[]{:S(2)}, u32[]{:S(2)}) collective-permute-start(bf16[8,4,8,768]{3,2,1,0:T(8,128)(2,1)S(1)} %get-tuple-element.414), channel_id=1, source_target_pairs={{0,4},{2,6},{4,0},{6,2},{8,12},{10,14},{12,8},{14,10},{16,20},{18,... | collective-permute-start | bytes 1179656 | tf_op jit(solution)/shard_map/ppermute | solution.py:514
  576.5 41.2 %collective-permute-start.53 = (bf16[8,5,8,768]{3,2,1,0:T(8,128)(2,1)S(1)}, bf16[8,5,8,768]{3,2,1,0:T(8,128)(2,1)S(1)}, u32[]{:S(2)}, u32[]{:S(2)}) collective-permute-start(bf16[8,5,8,768]{3,2,1,0:T(8,128)(2,1)S(1)} %get-tuple-element.412), channel_id=1, source_target_pairs={{0,4},{2,6},{4,0},{6,2},{8,12},{10,14},{12,8},{14,10},{16,20},{18,... | collective-permute-start | bytes 1474568 | tf_op jit(solution)/shard_map/ppermute | solution.py:514
  628.3 28.5 %collective-permute-start.69 = (bf16[1,2,48,768]{3,2,1,0:T(8,128)(2,1)S(1)}, bf16[1,2,48,768]{3,2,1,0:T(8,128)(2,1)S(1)}, u32[]{:S(2)}, u32[]{:S(2)}) collective-permute-start(bf16[1,2,48,768]{3,2,1,0:T(8,128)(2,1)S(1)} %get-tuple-element.447), channel_id=1, source_target_pairs={{0,16},{2,18},{4,20},{6,22},{8,24},{10,26},{12,28},{14,30},{16,0},... | collective-permute-start | bytes 442376 | tf_op jit(solution)/shard_map/ppermute | solution.py:514
  (110 other events, 1160.0 us)

commit v3 on v2

--- a/solution.py
+++ b/solution.py
@@ -690,12 +690,13 @@
     language = jnp.where(is_words, states, others)
     vision = jnp.where(is_words, others, states)
 
-    ready = beside(vision, *second)
+    ready = vision
     one, one_saved = attention_block(
         ready, ready, object_in, object_out, gains[0:1], no_bias, apart, False
     )
-    two, two_saved = feed_block(one, object_feed, feed_unit, gains[1:2])
-    x = beside(jnp.where(is_words, language, two), *second)
+    two, two_saved = feed_block(beside(one, *second), object_feed, feed_unit, gains[1:2])
+    x = jnp.where(is_words, language, two)
+    step(second, two)
     pairs = [chain.pair() for chain in second]
     cross_in, cross_out = place_weights(tables, pairs, [pairs[0][0].shape[1] - third] * 3)
     y = jnp.where(is_words, two, language)

time: 671 us -> 664 us (0.990)
  waiting for transfers between devices: 212 us -> 201 us
  starting transfers between devices: 86.1 us -> 77.4 us
  other arithmetic: 53 us -> 60.4 us
    ppermute x62, starting transfers between devices: 66.5 us -> 58.5 us  [swap(): lax.ppermute(value, 'stream', [(i, i ^ step) for i in range(self.streams)])]
    ppermute x62, waiting for transfers between devices: 162 us -> 155 us  [swap(): lax.ppermute(value, 'stream', [(i, i ^ step) for i in range(self.streams)])]
    unnamed x148 -> x168, local copies, waits for them, and re-layouts: 18.2 us -> 19.7 us
  transfers between devices with their start and end apart: 77 -> 77, of which waited for: 29 -> 27; matrix products, arithmetic and copies ran while one was open for 13% -> 16% of each run, Pallas kernels for 27% -> 28%
where the time goes in v3:
time: 664 us; the launch traced here: 659 us
  Pallas kernels  264 us (40%)
  waiting for transfers between devices  201 us (30%)
  starting transfers between devices  77.4 us (12%)
  other arithmetic  60.4 us (9%)
  local copies, waits for them, and re-layouts  54.1 us (8%)
    ppermute x62, waiting for transfers between devices, swap(): lax.ppermute(value, 'stream', [(i, i ^ step) for i in range(self.streams)])  155 us
    pallas_call x4, Pallas kernels, feed_back(): pl.pallas_call(functools.partial(feed_back_kernel, first), grid=(steps,),...  70.2 us
    ppermute x62, starting transfers between devices, swap(): lax.ppermute(value, 'stream', [(i, i ^ step) for i in range(self.streams)])  58.5 us
    pallas_call x3, Pallas kernels, attention_block_backward(): pl.pallas_call(functools.partial(attend_back_kernel, cross), grid=(steps,...  57.6 us
    pallas_call x3, Pallas kernels, attention_block(): pl.pallas_call(functools.partial(attend_kernel, cross), grid=(steps,), in...  46.7 us
    ppermute x15, waiting for transfers between devices, swap(): lax.ppermute(value, 'dp', [(i, i ^ step) for i in range(self.replicas)])  45.8 us
    pallas_call x2, Pallas kernels, feed_block(): pl.pallas_call(feed_kernel, grid=(rows // block,), in_specs=[row(width)]...  43.2 us
    convert_element_type x36, other arithmetic, add(): return (left.astype(F32) + right.astype(F32)).astype(left.dtype)  32.8 us
  transfers between devices with their start and end apart: 77, of which 27 were waited for; matrix products, arithmetic and copies ran while one was open for 16% of the time, Pallas kernels for 28%

profile of v3, /device:TPU:0, one launch (start us, length us, event | category | flops | bytes accessed | tf_op | source)
XLA Modules:
  0.0 658.8 jit_solution(3227045988346502966)
XLA Ops:
  11.7 9.5 %collective-permute-done = bf16[1,104,768]{2,1,0:T(8,128)(2,1)S(1)} collective-permute-done((bf16[1,104,768]{2,1,0:T(8,128)(2,1)S(1)}, bf16[1,104,768]{2,1,0:T(8,128)(2,1)S(1)}, u32[]{:S(2)}, u32[]{:S(2)}) %collective-permute-start) | collective-permute-done | bytes 159776 | tf_op jit(solution)/shard_map/ppermute | solution.py:514
  37.4 21.8 %collective-permute-done.14 = bf16[2,96,768]{2,1,0:T(8,128)(2,1)S(1)} collective-permute-done((bf16[2,96,768]{2,1,0:T(8,128)(2,1)S(1)}, bf16[2,96,768]{2,1,0:T(8,128)(2,1)S(1)}, u32[]{:S(2)}, u32[]{:S(2)}) %collective-permute-start.14) | collective-permute-done | bytes 294944 | tf_op jit(solution)/shard_map/ppermute | solution.py:514
  63.5 7.0 %collective-permute-done.1 = bf16[1,128,768]{2,1,0:T(8,128)(2,1)S(1)} collective-permute-done((bf16[1,128,768]{2,1,0:T(8,128)(2,1)S(1)}, bf16[1,128,768]{2,1,0:T(8,128)(2,1)S(1)}, u32[]{:S(2)}, u32[]{:S(2)}) %collective-permute-start.1) | collective-permute-done | bytes 196640 | tf_op jit(solution)/shard_map/ppermute | solution.py:514
  84.2 18.4 %collective-permute-done.9 = bf16[8,104,768]{2,1,0:T(8,128)(2,1)} collective-permute-done((bf16[8,104,768]{2,1,0:T(8,128)(2,1)}, bf16[8,104,768]{2,1,0:T(8,128)(2,1)}, u32[]{:S(2)}, u32[]{:S(2)}) %collective-permute-start.9) | collective-permute-done | bytes 1277984 | tf_op jit(solution)/shard_map/ppermute | solution.py:512
  105.0 19.0 %collective-permute-done.13 = bf16[8,96,768]{2,1,0:T(8,128)(2,1)} collective-permute-done((bf16[8,96,768]{2,1,0:T(8,128)(2,1)}, bf16[8,96,768]{2,1,0:T(8,128)(2,1)}, u32[]{:S(2)}, u32[]{:S(2)}) %collective-permute-start.13) | collective-permute-done | bytes 1179680 | tf_op jit(solution)/shard_map/ppermute | solution.py:514
  131.1 6.8 %collective-permute-done.6 = bf16[864,768]{1,0:T(8,128)(2,1)} collective-permute-done((bf16[864,768]{1,0:T(8,128)(2,1)}, bf16[864,768]{1,0:T(8,128)(2,1)}, u32[]{:S(2)}, u32[]{:S(2)}) %collective-permute-start.6) | collective-permute-done | bytes 1327136 | tf_op jit(solution)/shard_map/ppermute | solution.py:514
  144.4 5.1 place.3
  161.4 15.5 %attend.3 = (bf16[864,768]{1,0:T(8,128)(2,1)S(1)}, bf16[864,2304]{1,0:T(8,128)(2,1)}, bf16[6,3,144,576]{3,2,1,0:T(8,128)(2,1)}, bf16[864,768]{1,0:T(8,128)(2,1)S...) custom-call(bf16[864,768]{1,0:T(8,128)(2,1)} %broadcast_select_fusion.2.x_ref.y_ref.refs_4_.refs_5_, ...), custom_call_target="tpu_custom_call" | custom-call | flops 6115295232 | bytes 15925248 | tf_op jit(solution)/shard_map/attend/pallas_call | solution.py:127
  183.4 21.5 %feed.2 = (bf16[864,768]{1,0:T(8,128)(2,1)S(1)}, bf16[864,3072]{1,0:T(8,128)(2,1)}, bf16[864,3072]{1,0:T(8,128)(2,1)}, bf16[864,768]{1,0:T(8,128)(2,1)S(1)}, f32[864,1]{1,0:T(8,128)S(1)}) custom-call(bf16[864,768]{1,0:T(8,128)(2,1)S(1)} %get-tuple-element.231.x_ref.refs_4_.refs_2_, ...), custom_call_target="tpu_custom_call" | custom-call | flops 8153726976 | bytes 20054016 | tf_op jit(solution)/shard_map/feed/pallas_call | solution.py:354
  236.7 5.4 place.4
  242.1 15.8 %attend.4 = (bf16[864,768]{1,0:T(8,128)(2,1)S(1)}, bf16[864,2304]{1,0:T(8,128)(2,1)}, bf16[6,3,144,576]{3,2,1,0:T(8,128)(2,1)}, bf16[864,768]{1,0:T(8,128)(2,1)S...) custom-call(bf16[864,768]{1,0:T(8,128)(2,1)} %get-tuple-element.396.x_ref.refs_2_, ...), custom_call_target="tpu_custom_call" | custom-call | flops 6115295232 | bytes 15925248 | tf_op jit(solution)/shard_map/attend/pallas_call | solution.py:127
  259.0 5.6 place.5
  264.6 15.4 %attend.5 = (bf16[864,768]{1,0:T(8,128)(2,1)S(1)}, bf16[864,2304]{1,0:T(8,128)(2,1)}, bf16[6,3,144,576]{3,2,1,0:T(8,128)(2,1)}, bf16[864,768]{1,0:T(8,128)(2,1)S...) custom-call(bf16[864,768]{1,0:T(8,128)(2,1)} %copy-done.23, bf16[864,768]{1,0:T(8,128)(2,1)} %copy-done.23, ...), custom_call_target="tpu_custom_call" | custom-call | flops 6115295232 | bytes 15925248 | tf_op jit(solution)/shard_map/attend/pallas_call | solution.py:127
  279.9 21.7 %feed.3 = (bf16[864,768]{1,0:T(8,128)(2,1)}, bf16[864,3072]{1,0:T(8,128)(2,1)}, bf16[864,3072]{1,0:T(8,128)(2,1)}, bf16[864,768]{1,0:T(8,128)(2,1)S(1)}, f32[864,1]{1,0:T(8,128)S(1)}) custom-call(bf16[864,768]{1,0:T(8,128)(2,1)S(1)} %get-tuple-element.246.x_ref.refs_4_.refs_2_, ...), custom_call_target="tpu_custom_call" | custom-call | flops 8153726976 | bytes 20054016 | tf_op jit(solution)/shard_map/feed/pallas_call | solution.py:354
  301.6 17.4 %feed_back.4 = (bf16[864,768]{1,0:T(8,128)(2,1)S(1)}, f32[8,768]{1,0:T(8,128)S(1)}, bf16[16,2,48,768]{3,2,1,0:T(8,128)(2,1)}, bf16[16,2,48,768]{3,2,1,0:T(8,128)(2,1)}, f32[864,768]{1,0:T(8,128)}) custom-call(bf16[864,768]{1,0:T(8,128)(2,1)S(1)} %copy-done.4, bf16[864,768]{1,0:T(8,128)(2,1)S(1)} %get-tuple-element.248.refs_1_, ...), custom_call_target="tpu_custom_call" | custom-call | flops 8153726976 | bytes 17694720 | tf_op jit(solution)/shard_map/feed_back/pallas_call | solution.py:428
  319.1 17.2 %feed_back.5 = (bf16[16,2,48,768]{3,2,1,0:T(8,128)(2,1)S(1)}, bf16[16,2,48,768]{3,2,1,0:T(8,128)(2,1)}, f32[864,768]{1,0:T(8,128)}) custom-call(f32[864,768]{1,0:T(8,128)} %get-tuple-element.254.refs_0_, bf16[864,768]{1,0:T(8,128)(2,1)S(1)} %get-tuple-element.255.refs_1_, bf16[864,768]{1,0:T(8,128)(2,1)S(1)} %get-tuple-element.246.x_ref.refs_4_.refs_2_, ...), custom_call_target="tpu_custom_call" | custom-call | flops 8153726976 | bytes 17694720 | tf_op jit(solution)/shard_map/feed_back/pallas_call | solution.py:428
  339.5 18.9 %attend_back.3 = (bf16[864,768]{1,0:T(8,128)(2,1)S(1)}, bf16[864,2304]{1,0:T(8,128)(2,1)}, f32[864,768]{1,0:T(8,128)}, f32[8,768]{1,0:T(8,128)S(1)}) custom-call(f32[864,768]{1,0:T(8,128)} %get-tuple-element.261.grad_ref, bf16[864,768]{1,0:T(8,128)(2,1)S(1)} %copy-done.27, f32[864,1]{1,0:T(8,128)S(1)} %get-tuple-element.263.rate_ref, ...), custom_call_target="tpu_custom_call" | custom-call | flops 7134511104 | bytes 21233664 | tf_op jit(solution)/shard_map/attend_back/pallas_call | solution.py:221
  360.6 9.9 %attend_weights.3 = (bf16[16,12,8,768]{3,2,1,0:T(8,128)(2,1)}, bf16[16,12,8,768]{3,2,1,0:T(8,128)(2,1)}) custom-call(s32[32]{0:T(128)S(1)} %broadcast_xor_fusion.3.refs_0_, bf16[864,2304]{1,0:T(8,128)(2,1)} %get-tuple-element.271.refs_1_, bf16[864,768]{1,0:T(8,128)(2,1)S(1)} %copy-done.24, bf16[864,768]{1,0:T(8,128)(2,1)S(1)} %copy-done.24, ...), custom_call_target="tpu_custom_call" | custom-call | flops 4076863488 | bytes 10616832 | tf_op jit(solution)/shard_map/attend_weights/pallas_call | solution.py:299
  374.7 19.9 %attend_back.4 = (bf16[864,768]{1,0:T(8,128)(2,1)S(1)}, bf16[864,2304]{1,0:T(8,128)(2,1)}, f32[864,768]{1,0:T(8,128)}, f32[864,768]{1,0:T(8,128)}, f32[8,768]{1,0:T(8,128)S(1)}) custom-call(f32[864,768]{1,0:T(8,128)} %get-tuple-element.277.grad_ref, bf16[864,768]{1,0:T(8,128)(2,1)S(1)} %copy-done.25, f32[864,1]{1,0:T(8,128)S(1)} %copy-done.29, ...), custom_call_target="tpu_custom_call" | custom-call | flops 7134511104 | bytes 21233664 | tf_op jit(solution)/shard_map/attend_back/pallas_call | solution.py:221
  403.0 8.7 %collective-permute-done.36 = bf16[4,2,48,768]{3,2,1,0:T(8,128)(2,1)S(1)} collective-permute-done((bf16[4,2,48,768]{3,2,1,0:T(8,128)(2,1)S(1)}, bf16[4,2,48,768]{3,2,1,0:T(8,128)(2,1)S(1)}, u32[]{:S(2)}, u32[]{:S(2)}) %collective-permute-start.36) | collective-permute-done | bytes 589856 | tf_op jit(solution)/shard_map/ppermute | solution.py:514
  420.5 10.2 %attend_weights.4 = (bf16[16,12,8,768]{3,2,1,0:T(8,128)(2,1)}, bf16[16,12,8,768]{3,2,1,0:T(8,128)(2,1)}) custom-call(s32[32]{0:T(128)S(1)} %broadcast_xor_fusion.3.refs_0_, bf16[864,2304]{1,0:T(8,128)(2,1)} %get-tuple-element.292.refs_1_, bf16[864,768]{1,0:T(8,128)(2,1)S(1)} %copy-done.8, bf16[864,768]{1,0:T(8,128)(2,1)S(1)} %copy-done.7, ...), custom_call_target="tpu_custom_call" | custom-call | flops 4076863488 | bytes 10616832 | tf_op jit(solution)/shard_map/attend_weights/pallas_call | solution.py:299
  433.3 18.6 %feed_back.6 = (bf16[864,768]{1,0:T(8,128)(2,1)S(1)}, f32[8,768]{1,0:T(8,128)S(1)}, bf16[16,2,48,768]{3,2,1,0:T(8,128)(2,1)}, bf16[16,2,48,768]{3,2,1,0:T(8,128)(2,1)}, f32[864,768]{1,0:T(8,128)}) custom-call(f32[864,768]{1,0:T(8,128)} %get-tuple-element.300.refs_0_, bf16[864,768]{1,0:T(8,128)(2,1)S(1)} %copy-done.6, f32[864,1]{1,0:T(8,128)S(1)} %copy-done.11, ...), custom_call_target="tpu_custom_call" | custom-call | flops 8153726976 | bytes 17694720 | tf_op jit(solution)/shard_map/feed_back/pallas_call | solution.py:428
  453.7 9.9 %collective-permute-done.40 = bf16[1,2,48,768]{3,2,1,0:T(8,128)(2,1)} collective-permute-done((bf16[1,2,48,768]{3,2,1,0:T(8,128)(2,1)}, bf16[1,2,48,768]{3,2,1,0:T(8,128)(2,1)}, u32[]{:S(2)}, u32[]{:S(2)}) %collective-permute-start.40) | collective-permute-done | bytes 147488 | tf_op jit(solution)/shard_map/ppermute | solution.py:514
  474.3 17.0 %feed_back.7 = (bf16[16,2,48,768]{3,2,1,0:T(8,128)(2,1)S(1)}, bf16[16,2,48,768]{3,2,1,0:T(8,128)(2,1)}, f32[864,768]{1,0:T(8,128)}) custom-call(f32[864,768]{1,0:T(8,128)} %get-tuple-element.315.refs_0_, bf16[864,768]{1,0:T(8,128)(2,1)S(1)} %get-tuple-element.316.refs_1_, bf16[864,768]{1,0:T(8,128)(2,1)S(1)} %copy-done.1, ...), custom_call_target="tpu_custom_call" | custom-call | flops 8153726976 | bytes 17694720 | tf_op jit(solution)/shard_map/feed_back/pallas_call | solution.py:428
  503.1 18.9 %attend_back.5 = (bf16[864,768]{1,0:T(8,128)(2,1)S(1)}, bf16[864,2304]{1,0:T(8,128)(2,1)}, f32[864,768]{1,0:T(8,128)}, f32[8,768]{1,0:T(8,128)S(1)}) custom-call(f32[864,768]{1,0:T(8,128)} %get-tuple-element.327.grad_ref, bf16[864,768]{1,0:T(8,128)(2,1)S(1)} %copy-done.26, f32[864,1]{1,0:T(8,128)S(1)} %copy-done.31, f32[1,768]{1,0:T(1,128)S(1)} %slice.619.g_ref, ...), custom_call_target="tpu_custom_call" | custom-call | flops 7134511104 | bytes 21233664 | tf_op jit(solution)/shard_map/attend_back/pallas_call | solution.py:221
  530.2 6.8 %collective-permute-done.51 = bf16[4,12,8,768]{3,2,1,0:T(8,128)(2,1)} collective-permute-done((bf16[4,12,8,768]{3,2,1,0:T(8,128)(2,1)}, bf16[4,12,8,768]{3,2,1,0:T(8,128)(2,1)}, u32[]{:S(2)}, u32[]{:S(2)}) %collective-permute-start.51) | collective-permute-done | bytes 589856 | tf_op jit(solution)/shard_map/ppermute | solution.py:514
  544.4 9.8 %attend_weights.5 = (bf16[16,5,8,768]{3,2,1,0:T(8,128)(2,1)S(1)}, bf16[16,5,8,768]{3,2,1,0:T(8,128)(2,1)S(1)}, bf16[16,4,8,768]{3,2,1,0:T(8,128)(2,1)S(1)}, bf16...) custom-call(s32[32]{0:T(128)S(1)} %broadcast_xor_fusion.1.refs_0_.refs_2_, ...), custom_call_target="tpu_custom_call" | custom-call | flops 4076863488 | bytes 10616832 | tf_op jit(solution)/shard_map/attend_weights/pallas_call | solution.py:299
  560.6 8.4 %collective-permute-done.57 = bf16[8,4,8,768]{3,2,1,0:T(8,128)(2,1)S(1)} collective-permute-done((bf16[8,4,8,768]{3,2,1,0:T(8,128)(2,1)S(1)}, bf16[8,4,8,768]{3,2,1,0:T(8,128)(2,1)S(1)}, u32[]{:S(2)}, u32[]{:S(2)}) %collective-permute-start.57) | collective-permute-done | bytes 393248 | tf_op jit(solution)/shard_map/ppermute | solution.py:512
  570.2 23.5 %collective-permute-done.61 = bf16[8,4,8,768]{3,2,1,0:T(8,128)(2,1)S(1)} collective-permute-done((bf16[8,4,8,768]{3,2,1,0:T(8,128)(2,1)S(1)}, bf16[8,4,8,768]{3,2,1,0:T(8,128)(2,1)S(1)}, u32[]{:S(2)}, u32[]{:S(2)}) %collective-permute-start.61) | collective-permute-done | bytes 393248 | tf_op jit(solution)/shard_map/ppermute | solution.py:514
  596.6 11.1 %collective-permute-done.58 = bf16[4,4,8,768]{3,2,1,0:T(8,128)(2,1)S(1)} collective-permute-done((bf16[4,4,8,768]{3,2,1,0:T(8,128)(2,1)S(1)}, bf16[4,4,8,768]{3,2,1,0:T(8,128)(2,1)S(1)}, u32[]{:S(2)}, u32[]{:S(2)}) %collective-permute-start.58) | collective-permute-done | bytes 196640 | tf_op jit(solution)/shard_map/ppermute | solution.py:514
  611.1 9.3 %collective-permute-done.63 = bf16[2,4,8,768]{3,2,1,0:T(8,128)(2,1)S(1)} collective-permute-done((bf16[2,4,8,768]{3,2,1,0:T(8,128)(2,1)S(1)}, bf16[2,4,8,768]{3,2,1,0:T(8,128)(2,1)S(1)}, u32[]{:S(2)}, u32[]{:S(2)}) %collective-permute-start.63) | collective-permute-done | bytes 98336 | tf_op jit(solution)/shard_map/ppermute | solution.py:514
  621.6 6.7 %collective-permute-done.54 = bf16[4,5,8,768]{3,2,1,0:T(8,128)(2,1)S(1)} collective-permute-done((bf16[4,5,8,768]{3,2,1,0:T(8,128)(2,1)S(1)}, bf16[4,5,8,768]{3,2,1,0:T(8,128)(2,1)S(1)}, u32[]{:S(2)}, u32[]{:S(2)}) %collective-permute-start.54) | collective-permute-done | bytes 245792 | tf_op jit(solution)/shard_map/ppermute | solution.py:512
  (449 shorter events, 226.0 us)
Async XLA Ops:
  29.3 41.8 %collective-permute-start.8 = (bf16[4,104,768]{2,1,0:T(8,128)(2,1)S(1)}, bf16[4,104,768]{2,1,0:T(8,128)(2,1)S(1)}, u32[]{:S(2)}, u32[]{:S(2)}) collective-permute-start(bf16[4,104,768]{2,1,0:T(8,128)(2,1)S(1)} %pad_maximum_fusion.3), channel_id=1, source_target_pairs={{0,8},{2,10},{4,12},{6,14},{8,0},{10,2},{12,4},{14,6},{16,24},{18,... | collective-permute-start | bytes 1916936 | tf_op jit(solution)/shard_map/ppermute | solution.py:514
  30.9 28.3 %collective-permute-start.14 = (bf16[2,96,768]{2,1,0:T(8,128)(2,1)S(1)}, bf16[2,96,768]{2,1,0:T(8,128)(2,1)S(1)}, u32[]{:S(2)}, u32[]{:S(2)}) collective-permute-start(bf16[2,96,768]{2,1,0:T(8,128)(2,1)S(1)} %pad_maximum_fusion.11), channel_id=1, source_target_pairs={{0,8},{2,10},{4,12},{6,14},{8,0},{10,2},{12,4},{14,6},{16,24},{18,... | collective-permute-start | bytes 884744 | tf_op jit(solution)/shard_map/ppermute | solution.py:514
  32.2 29.7 %collective-permute-start.3 = (bf16[1,128,768]{2,1,0:T(8,128)(2,1)S(1)}, bf16[1,128,768]{2,1,0:T(8,128)(2,1)S(1)}, u32[]{:S(2)}, u32[]{:S(2)}) collective-permute-start(bf16[1,128,768]{2,1,0:T(8,128)(2,1)S(1)} %get-tuple-element.199), channel_id=1, source_target_pairs={{0,16},{2,18},{4,20},{6,22},{8,24},{10,26},{12,28},{14,30},{16,0},... | collective-permute-start | bytes 589832 | tf_op jit(solution)/shard_map/ppermute | solution.py:514
  35.1 38.8 %collective-permute-start.12 = (bf16[4,96,768]{2,1,0:T(8,128)(2,1)S(1)}, bf16[4,96,768]{2,1,0:T(8,128)(2,1)S(1)}, u32[]{:S(2)}, u32[]{:S(2)}) collective-permute-start(bf16[4,96,768]{2,1,0:T(8,128)(2,1)S(1)} %pad_maximum_fusion.4), channel_id=1, source_target_pairs={{0,4},{2,6},{4,0},{6,2},{8,12},{10,14},{12,8},{14,10},{16,20},{18,... | collective-permute-start | bytes 1769480 | tf_op jit(solution)/shard_map/ppermute | solution.py:514
  37.4 26.1 %collective-permute-start.5 = (bf16[1,128,768]{2,1,0:T(8,128)(2,1)S(1)}, bf16[1,128,768]{2,1,0:T(8,128)(2,1)S(1)}, u32[]{:S(2)}, u32[]{:S(2)}) collective-permute-start(bf16[1,128,768]{2,1,0:T(8,128)(2,1)S(1)} %get-tuple-element.200), channel_id=1, source_target_pairs={{0,16},{2,18},{4,20},{6,22},{8,24},{10,26},{12,28},{14,30},{16,0},... | collective-permute-start | bytes 589832 | tf_op jit(solution)/shard_map/ppermute | solution.py:514
  72.4 30.2 %collective-permute-start.9 = (bf16[8,104,768]{2,1,0:T(8,128)(2,1)}, bf16[8,104,768]{2,1,0:T(8,128)(2,1)}, u32[]{:S(2)}, u32[]{:S(2)}) collective-permute-start(bf16[8,104,768]{2,1,0:T(8,128)(2,1)} %pad_maximum_fusion), channel_id=1, source_target_pairs={{0,1},{1,0},{2,3},{3,2},{4,5},{5,4},{6,7},{7,6},{8,9},{9,8},{10,11... | collective-permute-start | bytes 3833864 | tf_op jit(solution)/shard_map/ppermute | solution.py:512
  75.0 48.9 %collective-permute-start.13 = (bf16[8,96,768]{2,1,0:T(8,128)(2,1)}, bf16[8,96,768]{2,1,0:T(8,128)(2,1)}, u32[]{:S(2)}, u32[]{:S(2)}) collective-permute-start(bf16[8,96,768]{2,1,0:T(8,128)(2,1)} %pad_maximum_fusion.1), channel_id=1, source_target_pairs={{0,8},{2,10},{4,12},{6,14},{8,0},{10,2},{12,4},{14,6},{16,24},{18,... | collective-permute-start | bytes 3538952 | tf_op jit(solution)/shard_map/ppermute | solution.py:514
  77.7 48.6 %collective-permute-start.16 = (bf16[8,96,768]{2,1,0:T(8,128)(2,1)}, bf16[8,96,768]{2,1,0:T(8,128)(2,1)}, u32[]{:S(2)}, u32[]{:S(2)}) collective-permute-start(bf16[8,96,768]{2,1,0:T(8,128)(2,1)} %pad_maximum_fusion.2), channel_id=1, source_target_pairs={{0,4},{2,6},{4,0},{6,2},{8,12},{10,14},{12,8},{14,10},{16,20},{18,... | collective-permute-start | bytes 3538952 | tf_op jit(solution)/shard_map/ppermute | solution.py:514
  79.2 58.7 %collective-permute-start.6 = (bf16[864,768]{1,0:T(8,128)(2,1)}, bf16[864,768]{1,0:T(8,128)(2,1)}, u32[]{:S(2)}, u32[]{:S(2)}) collective-permute-start(bf16[864,768]{1,0:T(8,128)(2,1)} %param.25), channel_id=1, source_target_pairs={{0,16},{2,18},{4,20},{6,22},{8,24},{10,26},{12,28},{14,30},{16,0},... | collective-permute-start | bytes 3981320 | tf_op jit(solution)/shard_map/ppermute | solution.py:514
  104.0 40.5 %collective-permute-start.10 = (bf16[16,104,768]{2,1,0:T(8,128)(2,1)S(1)}, bf16[16,104,768]{2,1,0:T(8,128)(2,1)}, u32[]{:S(2)}, u32[]{:S(2)}) collective-permute-start(bf16[16,104,768]{2,1,0:T(8,128)(2,1)S(1)} %constant_dynamic-update-slice_fusion.refs_1_), channel_id=1, source_target_pairs={{0,2},{2,0},{4,6},{6,4},{8,10},{10,8},{12,14},{14,12},{16,18},{18,... | collective-permute-start | bytes 7667720 | tf_op jit(solution)/shard_map/ppermute | solution.py:514
  178.2 31.8 %collective-permute-start.25 = (bf16[8,128,768]{2,1,0:T(8,128)(2,1)S(1)}, bf16[8,128,768]{2,1,0:T(8,128)(2,1)}, u32[]{:S(2)}, u32[]{:S(2)}) collective-permute-start(bf16[8,128,768]{2,1,0:T(8,128)(2,1)S(1)} %constant_dynamic-update-slice_fusion.13), channel_id=1, source_target_pairs={{0,1},{1,0},{2,3},{3,2},{4,5},{5,4},{6,7},{7,6},{8,9},{9,8},{10,11... | collective-permute-start | bytes 4718600 | tf_op jit(solution)/shard_map/ppermute | solution.py:512
  180.6 31.6 %collective-permute-start.27 = (bf16[8,128,768]{2,1,0:T(8,128)(2,1)}, bf16[8,128,768]{2,1,0:T(8,128)(2,1)}, u32[]{:S(2)}, u32[]{:S(2)}) collective-permute-start(bf16[8,128,768]{2,1,0:T(8,128)(2,1)} %constant_dynamic-update-slice_fusion.19), channel_id=1, source_target_pairs={{0,8},{2,10},{4,12},{6,14},{8,0},{10,2},{12,4},{14,6},{16,24},{18,... | collective-permute-start | bytes 4718600 | tf_op jit(solution)/shard_map/ppermute | solution.py:514
  182.8 34.8 %collective-permute-start.29 = (bf16[8,128,768]{2,1,0:T(8,128)(2,1)}, bf16[8,128,768]{2,1,0:T(8,128)(2,1)}, u32[]{:S(2)}, u32[]{:S(2)}) collective-permute-start(bf16[8,128,768]{2,1,0:T(8,128)(2,1)} %constant_dynamic-update-slice_fusion.25), channel_id=1, source_target_pairs={{0,4},{2,6},{4,0},{6,2},{8,12},{10,14},{12,8},{14,10},{16,20},{18,... | collective-permute-start | bytes 4718600 | tf_op jit(solution)/shard_map/ppermute | solution.py:514
  339.0 32.0 %collective-permute-start.33 = (bf16[8,2,48,768]{3,2,1,0:T(8,128)(2,1)}, bf16[8,2,48,768]{3,2,1,0:T(8,128)(2,1)}, u32[]{:S(2)}, u32[]{:S(2)}) collective-permute-start(bf16[8,2,48,768]{3,2,1,0:T(8,128)(2,1)} %get-tuple-element.394), channel_id=1, source_target_pairs={{0,8},{2,10},{4,12},{6,14},{8,0},{10,2},{12,4},{14,6},{16,24},{18,... | collective-permute-start | bytes 3538952 | tf_op jit(solution)/shard_map/ppermute | solution.py:514
  370.5 47.0 %collective-permute-start.34 = (bf16[16,12,8,768]{3,2,1,0:T(8,128)(2,1)}, bf16[16,12,8,768]{3,2,1,0:T(8,128)(2,1)S(1)}, u32[]{:S(2)}, u32[]{:S(2)}) collective-permute-start(bf16[16,12,8,768]{3,2,1,0:T(8,128)(2,1)} %get-tuple-element.274), channel_id=1, source_target_pairs={{0,2},{2,0},{4,6},{6,4},{8,10},{10,8},{12,14},{14,12},{16,18},{18,... | collective-permute-start | bytes 7077896 | tf_op jit(solution)/shard_map/ppermute | solution.py:514
  370.5 29.1 %collective-permute-start.35 = (bf16[8,2,48,768]{3,2,1,0:T(8,128)(2,1)}, bf16[8,2,48,768]{3,2,1,0:T(8,128)(2,1)}, u32[]{:S(2)}, u32[]{:S(2)}) collective-permute-start(bf16[8,2,48,768]{3,2,1,0:T(8,128)(2,1)} %get-tuple-element.392), channel_id=1, source_target_pairs={{0,4},{2,6},{4,0},{6,2},{8,12},{10,14},{12,8},{14,10},{16,20},{18,... | collective-permute-start | bytes 3538952 | tf_op jit(solution)/shard_map/ppermute | solution.py:514
  373.1 38.7 %collective-permute-start.36 = (bf16[4,2,48,768]{3,2,1,0:T(8,128)(2,1)S(1)}, bf16[4,2,48,768]{3,2,1,0:T(8,128)(2,1)S(1)}, u32[]{:S(2)}, u32[]{:S(2)}) collective-permute-start(bf16[4,2,48,768]{3,2,1,0:T(8,128)(2,1)S(1)} %get-tuple-element.408), channel_id=1, source_target_pairs={{0,4},{2,6},{4,0},{6,2},{8,12},{10,14},{12,8},{14,10},{16,20},{18,... | collective-permute-start | bytes 1769480 | tf_op jit(solution)/shard_map/ppermute | solution.py:514
  430.7 40.2 %collective-permute-start.42 = (bf16[16,12,8,768]{3,2,1,0:T(8,128)(2,1)}, bf16[16,12,8,768]{3,2,1,0:T(8,128)(2,1)}, u32[]{:S(2)}, u32[]{:S(2)}) collective-permute-start(bf16[16,12,8,768]{3,2,1,0:T(8,128)(2,1)} %get-tuple-element.295), channel_id=1, source_target_pairs={{0,2},{2,0},{4,6},{6,4},{8,10},{10,8},{12,14},{14,12},{16,18},{18,... | collective-permute-start | bytes 7077896 | tf_op jit(solution)/shard_map/ppermute | solution.py:514
  431.6 37.1 %collective-permute-start.39 = (bf16[8,12,8,768]{3,2,1,0:T(8,128)(2,1)}, bf16[8,12,8,768]{3,2,1,0:T(8,128)(2,1)}, u32[]{:S(2)}, u32[]{:S(2)}) collective-permute-start(bf16[8,12,8,768]{3,2,1,0:T(8,128)(2,1)} %get-tuple-element.390), channel_id=1, source_target_pairs={{0,1},{1,0},{2,3},{3,2},{4,5},{5,4},{6,7},{7,6},{8,9},{9,8},{10,11... | collective-permute-start | bytes 3538952 | tf_op jit(solution)/shard_map/ppermute | solution.py:512
  451.8 39.5 %collective-permute-start.43 = (bf16[16,2,48,768]{3,2,1,0:T(8,128)(2,1)}, bf16[16,2,48,768]{3,2,1,0:T(8,128)(2,1)}, u32[]{:S(2)}, u32[]{:S(2)}) collective-permute-start(bf16[16,2,48,768]{3,2,1,0:T(8,128)(2,1)} %get-tuple-element.306), channel_id=1, source_target_pairs={{0,2},{2,0},{4,6},{6,4},{8,10},{10,8},{12,14},{14,12},{16,18},{18,... | collective-permute-start | bytes 7077896 | tf_op jit(solution)/shard_map/ppermute | solution.py:514
  466.3 25.1 %collective-permute-start.45 = (bf16[1,2,48,768]{3,2,1,0:T(8,128)(2,1)S(1)}, bf16[1,2,48,768]{3,2,1,0:T(8,128)(2,1)S(1)}, u32[]{:S(2)}, u32[]{:S(2)}) collective-permute-start(bf16[1,2,48,768]{3,2,1,0:T(8,128)(2,1)S(1)} %get-tuple-element.448), channel_id=1, source_target_pairs={{0,16},{2,18},{4,20},{6,22},{8,24},{10,26},{12,28},{14,30},{16,0},... | collective-permute-start | bytes 442376 | tf_op jit(solution)/shard_map/ppermute | solution.py:514
  473.4 27.1 %collective-permute-start.46 = (bf16[8,12,8,768]{3,2,1,0:T(8,128)(2,1)S(1)}, bf16[8,12,8,768]{3,2,1,0:T(8,128)(2,1)S(1)}, u32[]{:S(2)}, u32[]{:S(2)}) collective-permute-start(bf16[8,12,8,768]{3,2,1,0:T(8,128)(2,1)S(1)} %get-tuple-element.388), channel_id=1, source_target_pairs={{0,1},{1,0},{2,3},{3,2},{4,5},{5,4},{6,7},{7,6},{8,9},{9,8},{10,11... | collective-permute-start | bytes 3538952 | tf_op jit(solution)/shard_map/ppermute | solution.py:512
  494.6 29.0 %collective-permute-start.48 = (bf16[8,2,48,768]{3,2,1,0:T(8,128)(2,1)S(1)}, bf16[8,2,48,768]{3,2,1,0:T(8,128)(2,1)S(1)}, u32[]{:S(2)}, u32[]{:S(2)}) collective-permute-start(bf16[8,2,48,768]{3,2,1,0:T(8,128)(2,1)S(1)} %get-tuple-element.386), channel_id=1, source_target_pairs={{0,8},{2,10},{4,12},{6,14},{8,0},{10,2},{12,4},{14,6},{16,24},{18,... | collective-permute-start | bytes 3538952 | tf_op jit(solution)/shard_map/ppermute | solution.py:514
  496.4 46.2 %collective-permute-start.49 = (bf16[16,2,48,768]{3,2,1,0:T(8,128)(2,1)}, bf16[16,2,48,768]{3,2,1,0:T(8,128)(2,1)S(1)}, u32[]{:S(2)}, u32[]{:S(2)}) collective-permute-start(bf16[16,2,48,768]{3,2,1,0:T(8,128)(2,1)} %get-tuple-element.318), channel_id=1, source_target_pairs={{0,2},{2,0},{4,6},{6,4},{8,10},{10,8},{12,14},{14,12},{16,18},{18,... | collective-permute-start | bytes 7077896 | tf_op jit(solution)/shard_map/ppermute | solution.py:514
  497.3 28.7 %collective-permute-start.50 = (bf16[2,12,8,768]{3,2,1,0:T(8,128)(2,1)}, bf16[2,12,8,768]{3,2,1,0:T(8,128)(2,1)}, u32[]{:S(2)}, u32[]{:S(2)}) collective-permute-start(bf16[2,12,8,768]{3,2,1,0:T(8,128)(2,1)} %get-tuple-element.422), channel_id=1, source_target_pairs={{0,4},{2,6},{4,0},{6,2},{8,12},{10,14},{12,8},{14,10},{16,20},{18,... | collective-permute-start | bytes 884744 | tf_op jit(solution)/shard_map/ppermute | solution.py:514
  501.6 35.4 %collective-permute-start.51 = (bf16[4,12,8,768]{3,2,1,0:T(8,128)(2,1)}, bf16[4,12,8,768]{3,2,1,0:T(8,128)(2,1)}, u32[]{:S(2)}, u32[]{:S(2)}) collective-permute-start(bf16[4,12,8,768]{3,2,1,0:T(8,128)(2,1)} %get-tuple-element.402), channel_id=1, source_target_pairs={{0,8},{2,10},{4,12},{6,14},{8,0},{10,2},{12,4},{14,6},{16,24},{18,... | collective-permute-start | bytes 1769480 | tf_op jit(solution)/shard_map/ppermute | solution.py:514
  529.7 110.2 %collective-permute-start.76 = (bf16[1,12,8,768]{3,2,1,0:T(8,128)(2,1)}, bf16[1,12,8,768]{3,2,1,0:T(8,128)(2,1)}, u32[]{:S(2)}, u32[]{:S(2)}) collective-permute-start(bf16[1,12,8,768]{3,2,1,0:T(8,128)(2,1)} %get-tuple-element.438), channel_id=1, source_target_pairs={{0,16},{2,18},{4,20},{6,22},{8,24},{10,26},{12,28},{14,30},{16,0},... | collective-permute-start | bytes 442376 | tf_op jit(solution)/shard_map/ppermute | solution.py:514
  555.4 75.3 %collective-permute-start.47 = (bf16[864,768]{1,0:T(8,128)(2,1)S(1)}, bf16[864,768]{1,0:T(8,128)(2,1)S(1)}, u32[]{:S(2)}, u32[]{:S(2)}) collective-permute-start(bf16[864,768]{1,0:T(8,128)(2,1)S(1)} %select_convert_fusion), channel_id=1, source_target_pairs={{0,16},{2,18},{4,20},{6,22},{8,24},{10,26},{12,28},{14,30},{16,0},... | collective-permute-start | bytes 3981320 | tf_op jit(solution)/shard_map/ppermute | solution.py:514
  556.5 38.7 %collective-permute-start.70 = (bf16[8,2,48,768]{3,2,1,0:T(8,128)(2,1)S(1)}, bf16[8,2,48,768]{3,2,1,0:T(8,128)(2,1)S(1)}, u32[]{:S(2)}, u32[]{:S(2)}) collective-permute-start(bf16[8,2,48,768]{3,2,1,0:T(8,128)(2,1)S(1)} %copy-done.48), channel_id=1, source_target_pairs={{0,4},{2,6},{4,0},{6,2},{8,12},{10,14},{12,8},{14,10},{16,20},{18,... | collective-permute-start | bytes 3538952 | tf_op jit(solution)/shard_map/ppermute | solution.py:514
  559.4 34.3 %collective-permute-start.61 = (bf16[8,4,8,768]{3,2,1,0:T(8,128)(2,1)S(1)}, bf16[8,4,8,768]{3,2,1,0:T(8,128)(2,1)S(1)}, u32[]{:S(2)}, u32[]{:S(2)}) collective-permute-start(bf16[8,4,8,768]{3,2,1,0:T(8,128)(2,1)S(1)} %get-tuple-element.412), channel_id=1, source_target_pairs={{0,4},{2,6},{4,0},{6,2},{8,12},{10,14},{12,8},{14,10},{16,20},{18,... | collective-permute-start | bytes 1179656 | tf_op jit(solution)/shard_map/ppermute | solution.py:514
  569.0 40.8 %collective-permute-start.53 = (bf16[8,5,8,768]{3,2,1,0:T(8,128)(2,1)S(1)}, bf16[8,5,8,768]{3,2,1,0:T(8,128)(2,1)S(1)}, u32[]{:S(2)}, u32[]{:S(2)}) collective-permute-start(bf16[8,5,8,768]{3,2,1,0:T(8,128)(2,1)S(1)} %get-tuple-element.410), channel_id=1, source_target_pairs={{0,4},{2,6},{4,0},{6,2},{8,12},{10,14},{12,8},{14,10},{16,20},{18,... | collective-permute-start | bytes 1474568 | tf_op jit(solution)/shard_map/ppermute | solution.py:514
  621.5 27.7 %collective-permute-start.69 = (bf16[1,2,48,768]{3,2,1,0:T(8,128)(2,1)S(1)}, bf16[1,2,48,768]{3,2,1,0:T(8,128)(2,1)S(1)}, u32[]{:S(2)}, u32[]{:S(2)}) collective-permute-start(bf16[1,2,48,768]{3,2,1,0:T(8,128)(2,1)S(1)} %get-tuple-element.445), channel_id=1, source_target_pairs={{0,16},{2,18},{4,20},{6,22},{8,24},{10,26},{12,28},{14,30},{16,0},... | collective-permute-start | bytes 442376 | tf_op jit(solution)/shard_map/ppermute | solution.py:514
  (120 other events, 1188.1 us)
